TPU v7x, 512 devices: a whole 4x4x16 slice. The times are simulated.
512 devices in a mesh: phase: 4 (over x), blk: 32 (over z, core), rep: 4 (over y).
Axes of the slice: x: 4, y: 4, z: 16, core: 2. Of those that a mesh axis runs over, the one named last changes fastest.
Arguments:
- descriptors: float32 [4, 32, 32768], P(None, None, ('blk', 'rep')), may hold values from -6 to 6
- positions: float32 [4, 3, 32768], P(None, None, 'blk'), as said below
- elements: int32 [4, 32768], P(None, 'blk'), may hold values from 0 to 1
- fragments: int32 [4, 32768], P(None, ('blk', 'rep')), may hold values from 0 to 3, as said below
- neg_input: float32 [2, 15, 32], replicated, may hold values from -1 to 1
- neg_bias: float32 [2, 15], replicated, may hold values from -3 to 3
- neg_hidden: float32 [2, 15, 15], replicated, may hold values from -1.5 to 1.5
- neg_output: float32 [2, 15], replicated, may hold values from -2.4 to 2.4
- short_input: float32 [2, 15, 32], replicated, may hold values from -1 to 1
- short_charge: float32 [2, 15], replicated, may hold values from -12 to 12
- short_bias: float32 [2, 15], replicated, may hold values from -3 to 3
- short_hidden: float32 [2, 15, 15], replicated, may hold values from -1.5 to 1.5
- short_output: float32 [2, 15], replicated, may hold values from -2.4 to 2.4
- widths: float32 [2], replicated, may hold values from 0.8 to 1.6
- hardness: float32 [2], replicated, may hold values from 0.5 to 2
Outputs:
- charges: float32 [4, 32768], P('phase', ('blk', 'rep'))
- energies: float32 [4, 32768], P('phase', ('blk', 'rep'))
Inputs may be any that keep to these rules, and one draw needn't show every extreme that they name: `positions`: each atom lies within 0.7 in each coordinate of its own site of a box lattice of spacing 2, one atom a site, so any two atoms are at least 0.6 apart. `fragments`: each molecule holds exactly 8192 atoms of a frame.
All inputs are finite; a program needn't handle non-finite values.
Results may differ from a plain program's by a relative error of at most 0.00035.
Values sent between devices are 32-bit elements; how exact they have to be, the bound alone decides.
No kernel may reach another device: no remote copies, remote signals or barrier semaphores. Data moves between devices by JAX's collectives and lax.ppermute only.
A program may use at most 64 MiB of HBM per device.

v0:
```python
import jax
import jax.numpy as jnp
from jax import lax
from jax.sharding import PartitionSpec as P

ITERS = 4
FRAGS = 4


highest = lax.Precision.HIGHEST
inv_sqrt_pi = 0.5641895835477563


def network(layer_in, layer_bias, layer_mid, layer_out, features, addition):
    hidden_one = (
        jnp.einsum("ehg,gn->ehn", layer_in, features, precision=highest)
        + layer_bias[:, :, None]
        + addition
    )
    hidden_one = jnp.tanh(hidden_one)
    hidden_two = jnp.tanh(jnp.einsum("ehk,ekn->ehn", layer_mid, hidden_one, precision=highest))
    return jnp.einsum("eh,ehn->en", layer_out, hidden_two, precision=highest)


def select_kind(values, element_ids):
    classes = jnp.arange(values.shape[0], dtype=jnp.int32)[:, None]
    return jnp.sum(jnp.where(element_ids[None, :] == classes, values, jnp.float32(0.0)), axis=0)


def pair_field(targets, sources, source_values, target_ids, source_ids):
    delta_x = targets[0][:, None] - sources[0][None, :]
    delta_y = targets[1][:, None] - sources[1][None, :]
    delta_z = targets[2][:, None] - sources[2][None, :]
    squared = delta_x * delta_x + delta_y * delta_y + delta_z * delta_z
    itself = target_ids[:, None] == source_ids[None, :]
    distance = jnp.sqrt(jnp.where(itself, 1.0, squared))
    inverse_width = lax.rsqrt(targets[3][:, None] + sources[3][None, :])
    kernel = jnp.where(itself, 0.0, lax.erf(distance * inverse_width) / distance)
    return jnp.sum(kernel * source_values[None, :], axis=1)


def on_device(
    descriptors,
    positions,
    elements,
    fragments,
    neg_input,
    neg_bias,
    neg_hidden,
    neg_output,
    short_input,
    short_charge,
    short_bias,
    short_hidden,
    short_output,
    widths,
    hardness,
):
    atoms_own = fragments.shape[1]
    block_atoms = positions.shape[2]
    frame_total = descriptors.shape[0]
    phases = lax.axis_size("phase")
    frames_own = frame_total // phases
    block_index = lax.axis_index("blk")
    rep_index = lax.axis_index("rep")
    phase_index = lax.axis_index("phase")
    members = jnp.float32(atoms_own * lax.axis_size("blk") * lax.axis_size("rep") // FRAGS)
    classes = jnp.arange(FRAGS, dtype=jnp.int32)[:, None]
    target_ids = block_index * block_atoms + jnp.arange(block_atoms, dtype=jnp.int32)
    own_start = rep_index * atoms_own
    kind_count = widths.shape[0]

    def frame_setup(frame_index):
        features = lax.dynamic_index_in_dim(descriptors, frame_index, 0, keepdims=False)
        coords_frame = lax.dynamic_index_in_dim(positions, frame_index, 0, keepdims=False)
        element_ids = lax.dynamic_index_in_dim(elements, frame_index, 0, keepdims=False)
        groups = lax.dynamic_index_in_dim(fragments, frame_index, 0, keepdims=False)
        width_atom = select_kind(
            jnp.broadcast_to(widths[:, None], (kind_count, block_atoms)), element_ids
        )
        targets = jnp.concatenate([coords_frame, (width_atom * width_atom)[None, :]], axis=0)
        own_geometry = lax.dynamic_slice_in_dim(targets, own_start, atoms_own, 1)
        own_kinds = lax.dynamic_slice_in_dim(element_ids, own_start, atoms_own, 0)
        own_width = lax.dynamic_slice_in_dim(width_atom, own_start, atoms_own, 0)
        diagonal = (
            select_kind(jnp.broadcast_to(hardness[:, None], (kind_count, atoms_own)), own_kinds)
            + inv_sqrt_pi / own_width
        )
        onehot = (groups[None, :] == classes).astype(jnp.float32)
        return (features, own_kinds, targets, own_geometry, own_geometry, diagonal, onehot)

    def source_ids(first_row, piece_rows):
        gathered = first_row + jnp.arange(piece_rows, dtype=jnp.int32)
        return gathered // atoms_own * block_atoms + own_start + gathered % atoms_own

    def fold_piece(running, targets, geometry, values):
        piece_rows = values.shape[0]
        sub_rows = min(atoms_own, piece_rows)

        def one_part(part_index, total):
            offset = part_index * sub_rows
            part_geometry = lax.dynamic_slice_in_dim(geometry, offset, sub_rows, 1)
            part_values = lax.dynamic_slice_in_dim(values, offset, sub_rows, 0)
            return total + pair_field(
                targets, part_geometry, part_values, target_ids, source_ids(offset, sub_rows)
            )

        return lax.fori_loop(0, piece_rows // sub_rows, one_part, running)

    def apply_matrix(vector, frame_data):
        targets = frame_data[2]
        own_geometry = frame_data[3]
        zero_field = jnp.zeros((block_atoms,), jnp.float32)
        stacked = jnp.concatenate([vector[None, :], own_geometry], axis=0)
        shard_piece = lax.all_gather(stacked, "blk", axis=1, tiled=True)
        partial_value = fold_piece(zero_field, targets, shard_piece[1:], shard_piece[0])
        return frame_data[5] * vector + lax.psum_scatter(
            partial_value, "rep", scatter_dimension=0, tiled=True
        )

    def fragment_sums(vector, onehot, extras):
        return lax.psum((jnp.dot(onehot, vector, precision=highest), extras), ("blk", "rep"))

    def begin_solve(frame_data):
        onehot = frame_data[6]
        electroneg = select_kind(
            network(neg_input, neg_bias, neg_hidden, neg_output, frame_data[0], 0.0), frame_data[1]
        )
        segment, totals = fragment_sums(electroneg, onehot, jnp.sum(electroneg * electroneg)[None])
        residual = -(electroneg - jnp.dot(segment / members, onehot, precision=highest))
        norm_now = totals[0] - jnp.sum(segment * segment) / members
        solver_state = jnp.stack([jnp.zeros_like(residual), residual, residual])
        return (solver_state, norm_now)

    def iterate(solver_state, norm_now, frame_data):
        onehot = frame_data[6]
        charges = solver_state[0]
        residual = solver_state[1]
        direction = solver_state[2]
        applied = apply_matrix(direction, frame_data)
        segment, totals = fragment_sums(applied, onehot, jnp.sum(direction * applied)[None])
        step_size = norm_now / totals[0]
        charges = charges + step_size * direction
        residual = residual - step_size * (
            applied - jnp.dot(segment / members, onehot, precision=highest)
        )
        norm_next = lax.psum(jnp.sum(residual * residual), ("blk", "rep"))
        direction = residual + norm_next / norm_now * direction
        return (jnp.stack([charges, residual, direction]), norm_next)

    def energy_of(frame_data, charges):
        addition = short_charge[:, :, None] * charges[None, None, :]
        return select_kind(
            network(short_input, short_bias, short_hidden, short_output, frame_data[0], addition),
            frame_data[1],
        )

    charge_out = jnp.zeros((frames_own, atoms_own), jnp.float32)
    energy_out = jnp.zeros((frames_own, atoms_own), jnp.float32)

    def run_frame(local_frame, outputs):
        frame_data = frame_setup(phase_index * frames_own + local_frame)
        solver_state, norm_now = begin_solve(frame_data)
        for iteration in range(ITERS):
            solver_state, norm_now = iterate(solver_state, norm_now, frame_data)
        energy = energy_of(frame_data, solver_state[0])
        return (
            lax.dynamic_update_index_in_dim(outputs[0], solver_state[0], local_frame, 0),
            lax.dynamic_update_index_in_dim(outputs[1], energy, local_frame, 0),
        )

    charge_out, energy_out = lax.fori_loop(0, frames_own, run_frame, (charge_out, energy_out))
    return (charge_out, energy_out)


def solution(mesh):
    return jax.shard_map(
        on_device,
        mesh=mesh,
        in_specs=(
            P(None, None, ("blk", "rep")),
            P(None, None, "blk"),
            P(None, "blk"),
            P(None, ("blk", "rep")),
            P(),
            P(),
            P(),
            P(),
            P(),
            P(),
            P(),
            P(),
            P(),
            P(),
            P(),
        ),
        out_specs=(P("phase", ("blk", "rep")), P("phase", ("blk", "rep"))),
        check_vma=False,
    )
```

profile of v0, /device:TPU:1, one launch (start us, length us, event | category | flops | bytes accessed | tf_op | source)
XLA Modules:
  0.0 2359.1 jit_solution(14287064049151059605)
XLA Ops:
  5.3 254.7 %psum.103 = f32[4]{0:T(128)S(1)} all-reduce(f32[4]{0:T(128)S(1)} %convolution_bitcast_fusion.3), channel_id=1, replica_groups=mesh['phase'=4,'blk'=32,'rep'=4] {'blk','rep'}, use_global_device_ids=true, to_apply=%region_3.4 | all-reduce | flops 4 | bytes 32 | tf_op jit(solution)/shard_map/while/body/eval_jaxpr/psum | solution.py:122
  263.1 32.3 %all_gather.16 = f32[5,8192]{1,0:T(8,128)S(1)} all-gather(f32[5,256]{1,0:T(8,128)S(1)} %pad_maximum_fusion.3), channel_id=1, replica_groups=mesh['phase'=4,'blk'=32,'rep'=4] {'blk'}, dimensions={1}, use_global_device_ids=true | all-gather | bytes 168960 | tf_op jit(solution)/shard_map/while/body/eval_jaxpr/all_gather | solution.py:115
  295.5 48.0 %while.82 = (s32[]{:T(128)}, f32[1024]{0:T(1024)S(1)}, s32[]{:T(128)}, f32[3,1024]{1,0:T(4,128)S(1)}, f32[4,8192]{1,0:T(4,128)S(1)}, /*index=5*/f32[1024]{0:T(10...) while((s32[]{:T(128)}, f32[1024]{0:T(1024)S(1)}, ...), condition=%wide.region_9.10_spmd.clone, body=%wide.region_7.9_spmd.clone.sunk | while | flops 4202250 | bytes 83209 | solution.py:108
  343.5 6.0 all-reduce
  349.5 1.3 dynamic-slice.1
  352.2 246.7 %all-reduce.6 = (f32[4]{0:T(128)S(1)}, f32[]{:T(128)}, f32[]{:T(128)}) all-reduce(f32[4]{0:T(128)S(1)} %convolution_bitcast_fusion.2, f32[]{:T(128)} %get-tuple-element.1153, f32[]{:T(128)} %get-tuple-element.1122), channel_id=1, replica_groups=mesh['phase'=4,'blk'=32,'rep'=4] {'blk','rep'}, use_global_device_ids=true, to_apply=%region_13.14 | all-reduce | flops 6 | bytes 48 | tf_op jit(solution)/shard_map/while/body/eval_jaxpr/psum | solution.py:122
  602.1 247.5 %psum.106 = f32[]{:T(128)} all-reduce(f32[]{:T(128)} %get-tuple-element.1120), channel_id=1, replica_groups=mesh['phase'=4,'blk'=32,'rep'=4] {'blk','rep'}, use_global_device_ids=true, to_apply=%region_15.16 | all-reduce | flops 1 | bytes 8 | tf_op jit(solution)/shard_map/while/body/eval_jaxpr/psum | solution.py:147
  850.3 32.3 %all_gather.17 = f32[5,8192]{1,0:T(8,128)S(1)} all-gather(f32[5,256]{1,0:T(8,128)S(1)} %pad_maximum_fusion.2), channel_id=1, replica_groups=mesh['phase'=4,'blk'=32,'rep'=4] {'blk'}, dimensions={1}, use_global_device_ids=true | all-gather | bytes 168960 | tf_op jit(solution)/shard_map/while/body/eval_jaxpr/all_gather | solution.py:115
  882.7 48.0 %while.83 = (s32[]{:T(128)}, f32[1024]{0:T(1024)S(1)}, s32[]{:T(128)}, f32[3,1024]{1,0:T(4,128)S(1)}, f32[4,8192]{1,0:T(4,128)S(1)}, /*index=5*/f32[1024]{0:T(10...) while((s32[]{:T(128)}, f32[1024]{0:T(1024)S(1)}, ...), condition=%wide.region_18.19_spmd.clone, body=%wide.region_16.18_spmd.clone.sunk | while | flops 4202250 | bytes 83209 | solution.py:108
  930.7 7.7 all-reduce.1
  939.2 244.6 %all-reduce.5 = (f32[4]{0:T(128)S(1)}, f32[]{:T(128)}) all-reduce(f32[4]{0:T(128)S(1)} %convolution_bitcast_fusion.1, f32[]{:T(128)} %get-tuple-element.1118), channel_id=1, replica_groups=mesh['phase'=4,'blk'=32,'rep'=4] {'blk','rep'}, use_global_device_ids=true, to_apply=%region_22.23 | all-reduce | flops 5 | bytes 40 | tf_op jit(solution)/shard_map/while/body/eval_jaxpr/psum | solution.py:122
  1185.8 249.8 %psum.109 = f32[]{:T(128)} all-reduce(f32[]{:T(128)} %get-tuple-element.1116), channel_id=1, replica_groups=mesh['phase'=4,'blk'=32,'rep'=4] {'blk','rep'}, use_global_device_ids=true, to_apply=%region_24.25 | all-reduce | flops 1 | bytes 8 | tf_op jit(solution)/shard_map/while/body/eval_jaxpr/psum | solution.py:147
  1436.9 32.0 %all_gather.18 = f32[5,8192]{1,0:T(8,128)S(1)} all-gather(f32[5,256]{1,0:T(8,128)S(1)} %pad_maximum_fusion.1), channel_id=1, replica_groups=mesh['phase'=4,'blk'=32,'rep'=4] {'blk'}, dimensions={1}, use_global_device_ids=true | all-gather | bytes 168960 | tf_op jit(solution)/shard_map/while/body/eval_jaxpr/all_gather | solution.py:115
  1469.0 48.0 %while.84 = (s32[]{:T(128)}, f32[1024]{0:T(1024)S(1)}, s32[]{:T(128)}, f32[3,1024]{1,0:T(4,128)S(1)}, f32[4,8192]{1,0:T(4,128)S(1)}, /*index=5*/f32[1024]{0:T(10...) while((s32[]{:T(128)}, f32[1024]{0:T(1024)S(1)}, ...), condition=%wide.region_27.28_spmd.clone, body=%wide.region_25.27_spmd.clone.sunk | while | flops 4202250 | bytes 83209 | solution.py:108
  1517.0 6.0 all-reduce.2
  1523.9 246.4 %all-reduce.4 = (f32[4]{0:T(128)S(1)}, f32[]{:T(128)}) all-reduce(f32[4]{0:T(128)S(1)} %convolution_bitcast_fusion, f32[]{:T(128)} %get-tuple-element.1114), channel_id=1, replica_groups=mesh['phase'=4,'blk'=32,'rep'=4] {'blk','rep'}, use_global_device_ids=true, to_apply=%region_31.32 | all-reduce | flops 5 | bytes 40 | tf_op jit(solution)/shard_map/while/body/eval_jaxpr/psum | solution.py:122
  1772.2 247.8 %psum.112 = f32[]{:T(128)} all-reduce(f32[]{:T(128)} %get-tuple-element.1112), channel_id=1, replica_groups=mesh['phase'=4,'blk'=32,'rep'=4] {'blk','rep'}, use_global_device_ids=true, to_apply=%region_33.34 | all-reduce | flops 1 | bytes 8 | tf_op jit(solution)/shard_map/while/body/eval_jaxpr/psum | solution.py:147
  2021.3 32.3 %all_gather.19 = f32[5,8192]{1,0:T(8,128)S(1)} all-gather(f32[5,256]{1,0:T(8,128)S(1)} %pad_maximum_fusion), channel_id=1, replica_groups=mesh['phase'=4,'blk'=32,'rep'=4] {'blk'}, dimensions={1}, use_global_device_ids=true | all-gather | bytes 168960 | tf_op jit(solution)/shard_map/while/body/eval_jaxpr/all_gather | solution.py:115
  2053.7 48.0 %while.85 = (s32[]{:T(128)}, f32[1024]{0:T(1024)S(1)}, s32[]{:T(128)}, f32[3,1024]{1,0:T(4,128)S(1)}, f32[4,8192]{1,0:T(4,128)S(1)}, /*index=5*/f32[1024]{0:T(10...) while((s32[]{:T(128)}, f32[1024]{0:T(1024)S(1)}, ...), condition=%wide.region_36.37_spmd.clone, body=%wide.region_34.36_spmd.clone.sunk | while | flops 4202250 | bytes 83209 | solution.py:108
  2053.9 1.2 fusion.104
  2055.4 1.2 fusion.104
  2056.9 1.2 fusion.104
  2058.4 1.2 fusion.104
  2059.9 1.2 fusion.104
  2061.4 1.2 fusion.104
  2062.9 1.2 fusion.104
  2064.4 1.2 fusion.104
  2065.9 1.2 fusion.104
  2067.4 1.2 fusion.104
  2068.9 1.2 fusion.104
  2070.4 1.2 fusion.104
  2071.9 1.2 fusion.104
  2073.4 1.2 fusion.104
  2074.9 1.2 fusion.104
  2076.4 1.2 fusion.104
  2077.9 1.2 fusion.104
  2079.4 1.2 fusion.104
  2080.9 1.2 fusion.104
  2082.4 1.2 fusion.104
  2083.9 1.2 fusion.104
  2085.4 1.2 fusion.104
  2086.9 1.2 fusion.104
  2088.4 1.2 fusion.104
  2089.9 1.2 fusion.104
  2091.4 1.2 fusion.104
  2092.9 1.2 fusion.104
  2101.7 7.7 all-reduce.3
  2110.1 244.7 %psum.113 = f32[]{:T(128)} all-reduce(f32[]{:T(128)} %fusion.56), channel_id=1, replica_groups=mesh['phase'=4,'blk'=32,'rep'=4] {'blk','rep'}, use_global_device_ids=true, to_apply=%region_39.40 | all-reduce | flops 1 | bytes 8 | tf_op jit(solution)/shard_map/while/body/eval_jaxpr/psum | solution.py:122
  (948 shorter events, 167.8 us)
Async XLA Ops:
  0.6 0.9 copy-start
  0.6 0.9 copy-start.3
  1.5 0.7 copy-start.7
  2.2 0.7 copy-start.1
  3.1 0.7 copy-start.4
  3.8 0.7 copy-start.9
  261.4 0.7 copy-start.8
  2101.7 254.4 %copy-start.10 = (f32[2,15,32]{2,0,1:T(2,128)S(1)}, f32[2,15,32]{2,0,1:T(2,128)}, u32[]{:S(2)}) copy-start(f32[2,15,32]{2,0,1:T(2,128)} %param.31) | copy-start | bytes 11524
  2356.1 0.7 copy-start.11
  2356.1 0.7 copy-start.12
  2356.8 0.6 copy-start.6
  2356.8 0.7 copy-start.2
  2357.7 0.7 copy-start.5
where the time goes:
time: 2360 us
  blocking collectives  2140 us (91%)
  other arithmetic  170 us (7%)
  local copies, waits for them, and re-layouts  31.1 us (1%)
    psum x5, blocking collectives, fragment_sums(): lax.psum((jnp.dot(onehot, vector, precision=highest), extras), ('blk', 'r...  1240 us
    psum x3, blocking collectives, iterate(): norm_next = lax.psum(jnp.sum(residual * residual), ('blk', 'rep'))  745 us
    reduce_sum x128, other arithmetic, pair_field(): return jnp.sum(kernel * source_values[None, :], axis=1)  160 us
    all_gather x4, blocking collectives, apply_matrix(): shard_piece = lax.all_gather(stacked, 'blk', axis=1, tiled=True)  129 us

commit v1 on v0

v1 whole, which is shorter than its diff:
```python
import functools

import jax
import jax.numpy as jnp
from jax import lax
from jax.experimental import pallas as pl
from jax.experimental.pallas import tpu as pltpu
from jax.sharding import Mesh
from jax.sharding import PartitionSpec as P


FRAGS = 4
ELEMS = 2
LANES = 128
OWN = 256
REPS = 4
BLKS = 32
GROUPS = OWN // 8
PIECE = BLKS * 2
ROWS = REPS * PIECE
WINDOW = 16

highest = lax.Precision.HIGHEST
inv_sqrt_pi = 0.5641895835477563
float32 = jnp.float32
VMEM = pl.BlockSpec(memory_space=pltpu.VMEM)
SMEM = pl.BlockSpec(memory_space=pltpu.SMEM)
PARAMS = pltpu.CompilerParams(vmem_limit_bytes=12 * 2**20)


def shaped(*shape):
    return jax.ShapeDtypeStruct(shape, float32)


def eye(size):
    return lax.broadcasted_iota(jnp.int32, (size, size), 0) == lax.broadcasted_iota(jnp.int32, (size, size), 1)


def as_column(row):
    return jnp.sum(jnp.where(eye(row.shape[1]), row, 0.0), axis=1, keepdims=True)


def as_rows(row):
    return jnp.broadcast_to(row, (LANES, LANES)).T


def total_of(values):
    return jnp.sum(jnp.sum(values, axis=0, keepdims=True), axis=1, keepdims=True)


def network(layer_in, layer_bias, layer_mid, layer_out, features, addition):
    outs = []
    for kind in range(ELEMS):
        hidden_one = jnp.dot(layer_in[kind], features, precision=highest, preferred_element_type=float32)
        hidden_one = hidden_one + as_column(layer_bias[kind : kind + 1, :])
        if addition is not None:
            weights, charges = addition
            hidden_one = hidden_one + as_column(weights[kind : kind + 1, :]) * charges
        hidden_one = jnp.tanh(hidden_one)
        hidden_two = jnp.tanh(jnp.dot(layer_mid[kind], hidden_one, precision=highest, preferred_element_type=float32))
        outs.append(jnp.sum(as_column(layer_out[kind : kind + 1, :]) * hidden_two, axis=0, keepdims=True))
    return outs


def prepare_kernel(place, features, coords, kinds, groups, layer_in, layer_bias, layer_mid, layer_out, message):
    frames = features.shape[0]
    own = pl.ds(pl.multiple_of(place[0] * OWN, OWN), OWN)
    wide = jnp.concatenate([features[frame] for frame in range(frames)], axis=1)
    first, second = network(layer_in, layer_bias, layer_mid, layer_out, wide, None)
    chosen = kinds[:, own]
    for frame in range(frames):
        span = slice(frame * OWN, frame * OWN + OWN)
        kind = chosen[frame : frame + 1, :]
        electroneg = jnp.where(kind == 1, second[:, span], first[:, span])
        spot = coords[frame, :, own]
        values = [spot[0:1], spot[1:2], spot[2:3], kind.astype(float32)]
        values += [electroneg, groups[frame : frame + 1, :].astype(float32)]
        for pair in range(3):
            one, two = values[2 * pair], values[2 * pair + 1]
            block = jnp.concatenate([one[:, :LANES], one[:, LANES:], two[:, :LANES], two[:, LANES:]], axis=0)
            for target in range(BLKS // frames):
                message[frame * (BLKS // frames) + target, pair] = block


def fill_rows(atoms, own_block, widths, rows):
    narrow, broad = widths[0], widths[1]
    for half in range(2):
        span = slice(half * LANES, half * LANES + LANES)
        for axis, (pair, line) in enumerate(((0, 0), (0, 2), (1, 0))):
            rows[axis, span] = as_rows(atoms[own_block, pair, line + half : line + half + 1, :])
        kind = as_rows(atoms[own_block, 1, 2 + half : 3 + half, :])
        width = jnp.where(kind > 0.5, broad, narrow)
        rows[3, span] = lax.rsqrt(width * width + narrow * narrow)
        rows[4, span] = lax.rsqrt(width * width + broad * broad)


def build_piece(atoms, rows, piece):
    def one_block(block, carry):
        for half in range(2):
            x, y, z, kind = (
                jnp.broadcast_to(atoms[block, pair, line + half : line + half + 1, :], (8, LANES))
                for pair, line in ((0, 0), (0, 2), (1, 0), (1, 2))
            )
            second = kind > 0.5
            for group in range(GROUPS):
                span = slice(group * 8, group * 8 + 8)
                delta_x = rows[0, span] - x
                delta_y = rows[1, span] - y
                delta_z = rows[2, span] - z
                squared = delta_x * delta_x + delta_y * delta_y + delta_z * delta_z
                inverse = lax.rsqrt(squared)
                scale = jnp.where(second, rows[4, span], rows[3, span])
                piece[2 * block + half, span, :] = lax.erf(squared * inverse * scale) * inverse
        return carry

    lax.fori_loop(0, BLKS, one_block, 0)


def build_own_kernel(place, atoms, widths, hardness, piece, rows):
    own_block = place[1]
    fill_rows(atoms, own_block, widths, rows)
    build_piece(atoms, rows, piece)
    for half in range(2):
        span = slice(half * LANES, half * LANES + LANES)
        second = as_rows(atoms[own_block, 1, 2 + half : 3 + half, :]) > 0.5
        diagonal = jnp.where(second, hardness[1], hardness[0]) + inv_sqrt_pi / jnp.where(second, widths[1], widths[0])
        tile = piece[2 * own_block + half, span, :]
        piece[2 * own_block + half, span, :] = jnp.where(eye(LANES), diagonal, tile)


def apply_rows(pieces, direction, rep):
    sums = tuple(jnp.zeros((8, LANES), float32) for _ in range(GROUPS))
    for turn, piece in enumerate(pieces):
        first = lax.rem(rep + turn, REPS) * PIECE

        def one_line(line, sums):
            values = jnp.broadcast_to(direction[pl.ds(first + line, 1), :], (8, LANES))
            return tuple(
                sums[group] + piece[line, group * 8 : group * 8 + 8, :] * values for group in range(GROUPS)
            )

        sums = lax.fori_loop(0, PIECE, one_line, sums, unroll=8)
    half = GROUPS // 2
    return [
        jnp.sum(jnp.concatenate(sums[part * half : part * half + half], axis=0).T, axis=0, keepdims=True)
        for part in range(2)
    ]


def write_message(image, message):
    block = jnp.concatenate(image * 4, axis=0)
    for line in range(ROWS // 8):
        message[line * 8 : line * 8 + 8, :] = block


def project(vector, groups):
    members = ROWS * LANES // FRAGS
    taken = jnp.zeros_like(vector)
    for group in range(FRAGS):
        inside = groups == float(group)
        mean = total_of(jnp.where(inside, vector, 0.0)) / members
        taken = jnp.where(inside, mean, taken)
    return vector - taken


def first_kernel(place, atoms, widths, own_piece, piece_1, piece_2, piece_3, message, residual, groups, norm, rows):
    rep = place[0]
    fill_rows(atoms.at[rep], place[1], widths, rows)
    for turn, piece in ((1, piece_1), (2, piece_2), (3, piece_3)):
        build_piece(atoms.at[lax.rem(rep + turn, REPS)], rows, piece)
    for part in range(REPS):
        for block in range(BLKS):
            line = part * PIECE + block * 2
            residual[line : line + 2, :] = atoms[part, block, 2, 0:2, :]
            groups[line : line + 2, :] = atoms[part, block, 2, 2:4, :]
    start = -project(residual[...], groups[...])
    residual[...] = start
    norm[...] = jnp.broadcast_to(total_of(start * start), norm.shape)
    write_message(apply_rows((own_piece, piece_1, piece_2, piece_3), residual, rep), message)


def update(image, residual, direction, charges, groups, norm, residual_out, direction_out, charges_out):
    norm_now = norm[0:1, 0:1]
    along, whole = direction[...], image[...]
    step = norm_now / total_of(along * whole)
    charges_out[...] = step * along if charges is None else charges[...] + step * along
    left = residual[...] - step * project(whole, groups[...])
    residual_out[...] = left
    norm_next = total_of(left * left)
    direction_out[...] = left + norm_next / norm_now * along
    return norm_next


def iterate_kernel(*refs, begun):
    place, image, residual, direction = refs[:4]
    charges = refs[4] if begun else None
    groups, norm, *pieces = refs[4 + begun : 10 + begun]
    message, residual_out, direction_out, charges_out, norm_out = refs[10 + begun :]
    norm_next = update(
        image, residual, direction, charges, groups, norm, residual_out, direction_out, charges_out
    )
    norm_out[...] = jnp.broadcast_to(norm_next, norm_out.shape)
    write_message(apply_rows(pieces, direction_out, place[0]), message)


def last_kernel(
    place, image, residual, direction, charges, groups, norm, own, piece_1, piece_2, piece_3, share, message, *scratch
):
    residual_out, direction_out, charges_out = scratch
    rep = place[0]
    norm_next = update(
        image, residual, direction, charges, groups, norm, residual_out, direction_out, charges_out
    )
    applied = apply_rows((own, piece_1, piece_2, piece_3), direction_out, rep)
    line = rep * PIECE + place[1] * 2
    part = applied[0] * direction_out[pl.ds(line, 1), :] + applied[1] * direction_out[pl.ds(line + 1, 1), :]
    share[...] = jnp.broadcast_to(jnp.sum(part, axis=1, keepdims=True) / norm_next, share.shape)
    lines = pl.ds(lax.rem(rep, 2), ROWS // 2, stride=2)
    message[...] = jnp.where(rep < 2, charges_out[lines, :], direction_out[lines, :])


def signal_lane(window):
    return lax.rem(window + 1, LANES // WINDOW) * WINDOW


def join_kernel(place, shares, message, out):
    total = total_of(shares[:, 0:1])
    lane = lax.broadcasted_iota(jnp.int32, message.shape, 1)
    out[...] = jnp.where(lane == signal_lane(place[2]), total, message[...])


def finish_kernel(
    place, parts, features, kinds, layer_in, layer_charge, layer_bias, layer_mid, layer_out, charges_out, energies_out
):
    frame = place[3]
    windows = LANES // WINDOW
    lane = lax.broadcasted_iota(jnp.int32, (windows, LANES), 1)
    window = lax.broadcasted_iota(jnp.int32, (windows, LANES), 0)
    inside = lane // WINDOW == window
    marked = lane == signal_lane(window)
    lines = []
    inverse = jnp.zeros((1, 1), float32)
    for rep in range(REPS):
        block = parts[pl.ds(pl.multiple_of(rep * BLKS + frame * windows, windows), windows), :]
        lines.append(jnp.sum(jnp.where(inside, block, 0.0), axis=0, keepdims=True))
        inverse = inverse + total_of(jnp.where(marked, block, 0.0))
    step = 1.0 / inverse
    charges = jnp.concatenate([lines[0] + step * lines[2], lines[1] + step * lines[3]], axis=1)
    charges_out[...] = charges
    first, second = network(layer_in, layer_bias, layer_mid, layer_out, features[frame], (layer_charge, charges))
    kind = kinds[pl.ds(frame, 1), pl.ds(pl.multiple_of(place[0] * OWN, OWN), OWN)]
    energies_out[...] = jnp.where(kind == 1, second, first)


def call(kernel, outs, name, scratch=(), flops=0):
    def run(place, *args):
        args = [place] + list(args)
        specs = [SMEM if arg.ndim == 1 else VMEM for arg in args]
        many = isinstance(outs, list)
        return pl.pallas_call(
            kernel,
            out_shape=outs,
            in_specs=specs,
            out_specs=[VMEM] * len(outs) if many else VMEM,
            scratch_shapes=list(scratch),
            compiler_params=PARAMS,
            cost_estimate=pl.CostEstimate(flops=flops, bytes_accessed=0, transcendentals=0) if flops else None,
            name=name,
        )(*args)

    return run


def on_device(
    descriptors,
    positions,
    elements,
    fragments,
    neg_input,
    neg_bias,
    neg_hidden,
    neg_output,
    short_input,
    short_charge,
    short_bias,
    short_hidden,
    short_output,
    widths,
    hardness,
):
    rep = lax.axis_index("rep")
    window = lax.axis_index("zr") * 2 + lax.axis_index("core")
    phase = lax.axis_index("phase")
    place = jnp.stack([rep, phase * 8 + window, window, phase]).astype(jnp.int32)
    block_axes = ("zq", "zr", "core")
    cube_axes = ("rep", "phase", "zr", "core")
    column_axes = ("rep", "zq", "zr", "core")
    piece = pltpu.VMEM((PIECE, OWN, LANES), float32)
    whole = shaped(ROWS, LANES)
    small = shaped(8, LANES)
    rows = pltpu.VMEM((5, OWN, LANES), float32)

    def exchange(message):
        sent = message.reshape(ROWS // 2, 2, LANES)
        return lax.all_to_all(sent, cube_axes, 0, 0).reshape(ROWS, LANES)

    def kept(pieces):
        return [pltpu.with_memory_space_constraint(one, pltpu.VMEM) for one in pieces]

    message = call(prepare_kernel, shaped(BLKS, 3, 4, LANES), "prepare")(
        place, descriptors, positions, elements, fragments, neg_input, neg_bias, neg_hidden, neg_output
    )
    atoms_own = lax.all_to_all(message, block_axes, 0, 0)
    atoms = lax.all_to_all(jnp.broadcast_to(atoms_own[None], (REPS,) + atoms_own.shape), "rep", 0, 0)
    piece_0 = call(build_own_kernel, piece, "build_own", [rows], flops=10**9)(place, atoms_own, widths, hardness)
    piece_1, piece_2, piece_3, message, residual, groups, norm = call(
        first_kernel, [piece, piece, piece, whole, whole, whole, small], "build_rest_and_begin", [rows]
    )(place, atoms, widths, *kept([piece_0]))
    pieces = [piece_0, piece_1, piece_2, piece_3]
    message, residual, direction, charges, norm = call(
        functools.partial(iterate_kernel, begun=0), [whole, whole, whole, whole, small], "iterate"
    )(place, exchange(message), residual, residual, groups, norm, *kept(pieces))
    message, residual, direction, charges, norm = call(
        functools.partial(iterate_kernel, begun=1), [whole, whole, whole, whole, small], "iterate"
    )(place, exchange(message), residual, direction, charges, groups, norm, *kept(pieces))
    share, message = call(
        last_kernel, [shaped(4, LANES), shaped(ROWS // 2, LANES)], "last", [pltpu.VMEM((ROWS, LANES), float32)] * 3
    )(place, exchange(message), residual, direction, charges, groups, norm, *kept(pieces))
    shares = lax.all_to_all(share.reshape(4, 1, LANES), "phase", 0, 0).reshape(4, LANES)
    message = call(join_kernel, shaped(ROWS // 2, LANES), "join")(place, shares, message)
    parts = lax.all_to_all(message.reshape(ROWS // 2, 1, LANES), column_axes, 0, 0).reshape(ROWS // 2, LANES)
    return call(finish_kernel, [shaped(1, OWN), shaped(1, OWN)], "finish")(
        place,
        parts,
        descriptors,
        elements,
        short_input,
        short_charge,
        short_bias,
        short_hidden,
        short_output,
    )


def solution(mesh):
    split = Mesh(mesh.devices.reshape(4, 4, 4, 2, 4), ("phase", "zq", "zr", "core", "rep"))
    block_axes = ("zq", "zr", "core")
    return jax.shard_map(
        on_device,
        mesh=split,
        in_specs=(
            P(None, None, block_axes + ("rep",)),
            P(None, None, block_axes),
            P(None, block_axes),
            P(None, block_axes + ("rep",)),
        )
        + (P(),) * 11,
        out_specs=(P("phase", block_axes + ("rep",)), P("phase", block_axes + ("rep",))),
        check_vma=False,
    )
```

time: 2360 us -> 176 us (0.07)
  blocking collectives: 2140 us -> 95.6 us
  other arithmetic: 170 us -> 0.08 us
  Pallas kernels: 0 us -> 36.6 us
    psum x8 -> x0, blocking collectives: 1980 us -> none  [the longest x5 1240 us: fragment_sums(): lax.psum((jnp.dot(onehot, vector, precision=highest), extras), ('blk', 'r...]
    reduce_sum x140 -> x0, other arithmetic: 166 us -> none  [the longest x128 160 us: pair_field(): return jnp.sum(kernel * source_values[None, :], axis=1)]
    all_gather x4 -> x0, blocking collectives: 129 us -> none  [apply_matrix(): shard_piece = lax.all_gather(stacked, 'blk', axis=1, tiled=True)]
    all_to_all x0 -> x5, blocking collectives: none -> 95.6 us  [the longest x3 54 us: exchange(): return lax.all_to_all(sent, cube_axes, 0, 0).reshape(ROWS, LANES)]
    pallas_call x0 -> x8, Pallas kernels: none -> 36.6 us  [run(): pl.pallas_call(kernel, out_shape=outs, in_specs=specs, out_specs=[VMEM] *...]
    unnamed x4 -> x0, blocking collectives: 27.4 us -> none
  transfers between devices with their start and end apart: 0 -> 2, of which waited for: 0 -> 2; matrix products, arithmetic and copies ran while one was open for 0% -> 0% of each run, Pallas kernels for 0% -> 3%
where the time goes in v1:
time: 176 us
  blocking collectives  95.6 us (54%)
  Pallas kernels  36.6 us (21%)
  waiting for transfers between devices  15.3 us (9%)
  local copies, waits for them, and re-layouts  15 us (9%)
  starting transfers between devices  12.3 us (7%)
    all_to_all x3, blocking collectives, exchange(): return lax.all_to_all(sent, cube_axes, 0, 0).reshape(ROWS, LANES)  54 us
    pallas_call x8, Pallas kernels, run(): pl.pallas_call(kernel, out_shape=outs, in_specs=specs, out_specs=[VMEM] *...  36.6 us
    all_to_all x1, blocking collectives, on_device(): atoms_own = lax.all_to_all(message, block_axes, 0, 0)  35.2 us
    all_to_all x1, waiting for transfers between devices, on_device(): lax.all_to_all(message.reshape(ROWS // 2, 1, LANES), column_axes, 0, 0)  15 us
    unnamed x41, local copies, waits for them, and re-layouts  13.9 us
    all_to_all x1, starting transfers between devices, on_device(): lax.all_to_all(message.reshape(ROWS // 2, 1, LANES), column_axes, 0, 0)  8.11 us
    all_to_all x1, blocking collectives, on_device(): lax.all_to_all(share.reshape(4, 1, LANES), 'phase', 0, 0).reshape(4, LANES)  6.44 us
    all_to_all x1, starting transfers between devices, on_device(): lax.all_to_all(jnp.broadcast_to(atoms_own[None], (REPS,) + atoms_own.shap...  4.18 us
  transfers between devices with their start and end apart: 2, of which 2 were waited for; matrix products, arithmetic and copies ran while one was open for 0% of the time, Pallas kernels for 3%

profile of v1, /device:TPU:1, one launch (start us, length us, event | category | flops | bytes accessed | tf_op | source)
XLA Modules:
  0.0 175.7 jit_solution(5754176185799077713)
XLA Ops:
  0.6 0.0 copy-start.9
  0.6 0.8 copy.22.coords
  1.5 0.7 copy.23.layer_in
  2.2 0.7 copy.24.layer_mid
  2.9 0.1 pad_add_fusion.place.refs_0_
  3.0 0.0 copy-start.3
  3.0 0.9 copy-done.3
  3.9 0.0 copy-start.5
  3.9 0.7 copy-done.5
  4.6 0.0 copy-start.7
  4.6 0.7 copy-done.7
  5.3 0.7 copy-done.10
  6.0 0.7 copy-done.11
  6.7 1.2 prepare.1
  7.8 35.2 %all_to_all.35.atoms = f32[32,3,4,128]{3,2,1,0:T(4,128)S(1)} all-to-all(f32[32,3,4,128]{3,2,1,0:T(4,128)S(1)} %prepare.1), channel_id=1, replica_groups=mesh['phase'=4,'zq'=4,'zr'=4,'core'=2,'rep'=4] {'zq','zr','core'}, dimensions={0} | all-to-all | bytes 393216 | tf_op jit(solution)/shard_map/all_to_all | solution.py:313
  43.0 1.1 broadcast_in_dim.2
  44.1 4.2 %all-to-all-start.1 = ((f32[4,32,3,4,128]{4,3,2,1,0:T(4,128)}), f32[4,32,3,4,128]{4,3,2,1,0:T(4,128)S(1)}, u32[]{:S(2)}, u32[]{:S(2)}) async-start(f32[4,32,3,4,128]{4,3,2,1,0:T(4,128)} %broadcast_in_dim.2), calls=%async_computation.1 | async-start | bytes 1572864 | tf_op jit(solution)/shard_map/all_to_all | solution.py:314
  48.3 0.7 copy-done.8
  48.9 0.7 copy-done.15
  49.6 5.2 %build_own.1.own_piece.refs_6_.refs_7_.own = f32[64,256,128]{2,1,0:T(8,128)S(1)} custom-call(s32[4]{0:T(128)S(1)} %pad_add_fusion.place.refs_0_, f32[32,3,4,128]{3,2,1,0:T(4,128)S(1)} %all_to_all.35.atoms, f32[2]{0:T(128)S(1)} %copy-done.8, f32[2]{0:T(128)S(1)} %copy-done.15), custom_call_target="tpu_custom_call" | custom-call | flops 1000000000 | tf_op jit(solution)/shard_map/build_own/pallas_call | solution.py:260
  54.8 0.0 copy-start
  54.8 3.3 %copy-done = f32[64,256,128]{2,1,0:T(8,128)} copy-done((f32[64,256,128]{2,1,0:T(8,128)}, f32[64,256,128]{2,1,0:T(8,128)S(1)}, u32[]{:S(2)}) %copy-start) | copy-done | bytes 8388632
  58.0 0.3 all-to-all-done.1.atoms
  58.4 0.0 copy-done.9
  58.4 3.4 %copy-done.1 = f32[64,256,128]{2,1,0:T(8,128)S(1)} copy-done((f32[64,256,128]{2,1,0:T(8,128)S(1)}, f32[64,256,128]{2,1,0:T(8,128)}, u32[]{:S(2)}) %copy-start.1) | copy-done | bytes 8388632
  61.8 16.7 %build_rest_and_begin.1 = (f32[64,256,128]{2,1,0:T(8,128)S(1)}, f32[64,256,128]{2,1,0:T(8,128)S(1)}, f32[64,256,128]{2,1,0:T(8,128)S(1)}, f32[256,128]{1,0:T(8,1...) custom-call(s32[4]{0:T(128)S(1)} %pad_add_fusion.place.refs_0_, ...), custom_call_target="tpu_custom_call" | custom-call | tf_op jit(solution)/shard_map/build_rest_and_begin/pallas_call | solution.py:260
  78.5 20.7 %all_to_all.36 = f32[128,2,128]{2,1,0:T(2,128)S(1)} all-to-all(f32[128,2,128]{2,1,0:T(2,128)S(1)} %bitcast.23), channel_id=1, replica_groups=mesh['phase'=4,'zq'=4,'zr'=4,'core'=2,'rep'=4] {'rep','phase','zr','core'}, dimensions={0} | all-to-all | bytes 262144 | tf_op jit(solution)/shard_map/all_to_all | solution.py:305
  99.2 0.0 copy-done.2
  99.2 3.5 %iterate.2 = (f32[256,128]{1,0:T(8,128)S(1)}, f32[256,128]{1,0:T(8,128)S(1)}, f32[256,128]{1,0:T(8,128)S(1)}, f32[256,128]{1,0:T(8,128)S(1)}, f32[8,128]{1,0:T(8,128)S(1)}) custom-call(s32[4]{0:T(128)S(1)} %pad_add_fusion.place.refs_0_, f32[256,128]{1,0:T(8,128)S(1)} %bitcast.20, f32[256,128]{1,0:T(8,128)S(1)} %get-tuple-element.22.refs_2_.refs_3_, ...), custom_call_target="tpu_custom_call" | custom-call | tf_op jit(solution)/shard_map/iterate/pallas_call | solution.py:260
  102.8 16.6 %all_to_all.37 = f32[128,2,128]{2,1,0:T(2,128)S(1)} all-to-all(f32[128,2,128]{2,1,0:T(2,128)S(1)} %bitcast.24), channel_id=1, replica_groups=mesh['phase'=4,'zq'=4,'zr'=4,'core'=2,'rep'=4] {'rep','phase','zr','core'}, dimensions={0} | all-to-all | bytes 262144 | tf_op jit(solution)/shard_map/all_to_all | solution.py:305
  119.4 3.5 %iterate.3 = (f32[256,128]{1,0:T(8,128)S(1)}, f32[256,128]{1,0:T(8,128)S(1)}, f32[256,128]{1,0:T(8,128)S(1)}, f32[256,128]{1,0:T(8,128)S(1)}, f32[8,128]{1,0:T(8,128)S(1)}) custom-call(s32[4]{0:T(128)S(1)} %pad_add_fusion.place.refs_0_, f32[256,128]{1,0:T(8,128)S(1)} %bitcast.19, f32[256,128]{1,0:T(8,128)S(1)} %get-tuple-element.29.refs_2_, ...), custom_call_target="tpu_custom_call" | custom-call | tf_op jit(solution)/shard_map/iterate/pallas_call | solution.py:260
  122.9 16.6 %all_to_all.38 = f32[128,2,128]{2,1,0:T(2,128)S(1)} all-to-all(f32[128,2,128]{2,1,0:T(2,128)S(1)} %bitcast.22), channel_id=1, replica_groups=mesh['phase'=4,'zq'=4,'zr'=4,'core'=2,'rep'=4] {'rep','phase','zr','core'}, dimensions={0} | all-to-all | bytes 262144 | tf_op jit(solution)/shard_map/all_to_all | solution.py:305
  139.6 0.0 copy-start.12
  139.6 0.0 copy-start.13
  139.6 0.0 copy-start.14
  139.6 3.6 %last.1 = (f32[4,128]{1,0:T(4,128)S(1)}, f32[128,128]{1,0:T(8,128)S(1)}) custom-call(s32[4]{0:T(128)S(1)} %pad_add_fusion.place.refs_0_, f32[256,128]{1,0:T(8,128)S(1)} %bitcast.18, f32[256,128]{1,0:T(8,128)S(1)} %get-tuple-element.34.residual, f32[256,128]{1,0:T(8,128)S(1)} %get-tuple-element.35.direction, f32[256,128]{1,0:T(8,128)S(1)} %get-tuple-element.36.charges, ...), custom_call_target="tpu_custom_call" | custom-call | tf_op jit(solution)/shard_map/last/pallas_call | solution.py:260
  143.2 6.4 %all_to_all.39 = f32[4,1,128]{2,1,0:T(1,128)S(1)} all-to-all(f32[4,1,128]{2,1,0:T(1,128)S(1)} %bitcast.26), channel_id=1, replica_groups=mesh['phase'=4,'zq'=4,'zr'=4,'core'=2,'rep'=4] {'phase'}, dimensions={0} | all-to-all | bytes 4096 | tf_op jit(solution)/shard_map/all_to_all | solution.py:329
  149.6 1.2 join.1
  150.9 8.1 %all-to-all-start.6 = ((f32[128,1,128]{2,1,0:T(1,128)}), f32[128,1,128]{2,1,0:T(1,128)S(1)}, u32[]{:S(2)}, u32[]{:S(2)}) async-start(f32[128,1,128]{2,1,0:T(1,128)} %bitcast.14), calls=%async_computation.6 | async-start | bytes 131072 | tf_op jit(solution)/shard_map/all_to_all | solution.py:331
  159.0 0.0 copy-done.16
  159.0 0.0 copy-done.17
  159.0 15.0 %all-to-all-done.6 = f32[128,1,128]{2,1,0:T(1,128)S(1)} async-done(((f32[128,1,128]{2,1,0:T(1,128)}), f32[128,1,128]{2,1,0:T(1,128)S(1)}, u32[]{:S(2)}, u32[]{:S(2)}) %all-to-all-start.6) | async-done | bytes 65568 | tf_op jit(solution)/shard_map/all_to_all | solution.py:331
  174.0 0.0 copy-done.4
  174.0 0.0 copy-done.6
  174.0 0.0 copy-done.12
  174.0 0.0 copy-done.13
  174.0 0.0 copy-done.14
  174.0 1.7 finish.1
  (12 shorter events, 0.0 us)
Async XLA Ops:
  0.6 57.7 %copy-start.9 = (f32[2]{0:T(128)S(1)}, f32[2]{0:T(128)}, u32[]{:S(2)}) copy-start(f32[2]{0:T(128)} %widths.3) | copy-start | bytes 28
  3.0 0.9 copy-start.3
  3.9 0.7 copy-start.5
  4.6 0.7 copy-start.7
  5.3 0.7 copy-start.10
  6.0 0.7 copy-start.11
  44.1 14.3 %all-to-all-start.1 = ((f32[4,32,3,4,128]{4,3,2,1,0:T(4,128)}), f32[4,32,3,4,128]{4,3,2,1,0:T(4,128)S(1)}, u32[]{:S(2)}, u32[]{:S(2)}) async-start(f32[4,32,3,4,128]{4,3,2,1,0:T(4,128)} %broadcast_in_dim.2), calls=%async_computation.1 | async-start | bytes 1572864 | tf_op jit(solution)/shard_map/all_to_all | solution.py:314
  48.3 0.7 copy-start.8
  48.9 0.7 copy-start.15
  54.8 3.3 %copy-start = (f32[64,256,128]{2,1,0:T(8,128)}, f32[64,256,128]{2,1,0:T(8,128)S(1)}, u32[]{:S(2)}) copy-start(f32[64,256,128]{2,1,0:T(8,128)S(1)} %build_own.1.own_piece.refs_6_.refs_7_.own) | copy-start | bytes 25165828
  58.4 3.4 %copy-start.1 = (f32[64,256,128]{2,1,0:T(8,128)S(1)}, f32[64,256,128]{2,1,0:T(8,128)}, u32[]{:S(2)}) copy-start(f32[64,256,128]{2,1,0:T(8,128)} %copy-done) | copy-start | bytes 25165828
  61.8 37.5 %copy-start.2 = (f32[64,256,128]{2,1,0:T(8,128)S(1)}, f32[64,256,128]{2,1,0:T(8,128)}, u32[]{:S(2)}) copy-start(f32[64,256,128]{2,1,0:T(8,128)} %copy-done) | copy-start | bytes 25165828
  139.6 19.4 %copy-start.16 = (f32[2,15,32]{2,0,1:T(2,128)S(1)}, f32[2,15,32]{2,0,1:T(2,128)}, u32[]{:S(2)}) copy-start(f32[2,15,32]{2,0,1:T(2,128)} %param.23) | copy-start | bytes 11524
  139.6 19.4 %copy-start.17 = (f32[2,15,15]{2,0,1:T(2,128)S(1)}, f32[2,15,15]{2,0,1:T(2,128)}, u32[]{:S(2)}) copy-start(f32[2,15,15]{2,0,1:T(2,128)} %param.26) | copy-start | bytes 5404
  139.6 34.4 %copy-start.4 = (f32[4,32,256]{2,1,0:T(8,128)S(1)}, f32[4,32,256]{2,1,0:T(8,128)}, u32[]{:S(2)}) copy-start(f32[4,32,256]{2,1,0:T(8,128)} %features.3) | copy-start | bytes 393220
  139.6 34.4 %copy-start.6 = (s32[4,1024]{1,0:T(4,128)S(1)}, s32[4,1024]{1,0:T(4,128)}, u32[]{:S(2)}) copy-start(s32[4,1024]{1,0:T(4,128)} %kinds.3) | copy-start | bytes 49156
  139.6 34.4 %copy-start.12 = (f32[2,15]{1,0:T(2,128)S(1)}, f32[2,15]{1,0:T(2,128)}, u32[]{:S(2)}) copy-start(f32[2,15]{1,0:T(2,128)} %layer_charge.1) | copy-start | bytes 364
  139.6 34.4 %copy-start.13 = (f32[2,15]{1,0:T(2,128)S(1)}, f32[2,15]{1,0:T(2,128)}, u32[]{:S(2)}) copy-start(f32[2,15]{1,0:T(2,128)} %layer_bias.3) | copy-start | bytes 364
  139.6 34.4 %copy-start.14 = (f32[2,15]{1,0:T(2,128)S(1)}, f32[2,15]{1,0:T(2,128)}, u32[]{:S(2)}) copy-start(f32[2,15]{1,0:T(2,128)} %layer_out.3) | copy-start | bytes 364
  150.9 23.1 %all-to-all-start.6 = ((f32[128,1,128]{2,1,0:T(1,128)}), f32[128,1,128]{2,1,0:T(1,128)S(1)}, u32[]{:S(2)}, u32[]{:S(2)}) async-start(f32[128,1,128]{2,1,0:T(1,128)} %bitcast.14), calls=%async_computation.6 | async-start | bytes 131072 | tf_op jit(solution)/shard_map/all_to_all | solution.py:331

commit v2 on v1

v2 whole, which is shorter than its diff:
```python
import functools

import jax
import jax.numpy as jnp
from jax import lax
from jax.experimental import pallas as pl
from jax.experimental.pallas import tpu as pltpu
from jax.sharding import Mesh
from jax.sharding import PartitionSpec as P


FRAGS = 4
ELEMS = 2
LANES = 128
OWN = 256
REPS = 4
BLKS = 32
GROUPS = OWN // 8
PIECE = BLKS * 2
ROWS = REPS * PIECE
WINDOW = 64

highest = lax.Precision.HIGHEST
inv_sqrt_pi = 0.5641895835477563
float32 = jnp.float32
VMEM = pl.BlockSpec(memory_space=pltpu.VMEM)
SMEM = pl.BlockSpec(memory_space=pltpu.SMEM)
PARAMS = pltpu.CompilerParams(vmem_limit_bytes=12 * 2**20)


def shaped(*shape):
    return jax.ShapeDtypeStruct(shape, float32)


def eye(size):
    return lax.broadcasted_iota(jnp.int32, (size, size), 0) == lax.broadcasted_iota(jnp.int32, (size, size), 1)


def as_column(row):
    return jnp.sum(jnp.where(eye(row.shape[1]), row, 0.0), axis=1, keepdims=True)


def as_rows(row):
    return jnp.broadcast_to(row, (LANES, LANES)).T


def total_of(values):
    return jnp.sum(jnp.sum(values, axis=0, keepdims=True), axis=1, keepdims=True)


def last_layers(layer_mid, layer_out, hidden_one, kind):
    hidden_two = jnp.dot(layer_mid[:, kind, :], hidden_one, precision=highest, preferred_element_type=float32)
    return jnp.sum(as_column(layer_out[kind : kind + 1, :]) * jnp.tanh(hidden_two), axis=0, keepdims=True)


def network(layer_in, layer_bias, layer_mid, layer_out, features):
    outs = []
    for kind in range(ELEMS):
        hidden_one = jnp.dot(layer_in[:, kind, :], features, precision=highest, preferred_element_type=float32)
        hidden_one = jnp.tanh(hidden_one + as_column(layer_bias[kind : kind + 1, :]))
        outs.append(last_layers(layer_mid, layer_out, hidden_one, kind))
    return outs


def place_of():
    window = lax.axis_index("zr") * 2 + lax.axis_index("core")
    return lax.axis_index("rep"), lax.axis_index("phase") * 8 + window, window


def prepare_kernel(*refs):
    given, (message, constants), held, arrived = refs[:10], refs[10:12], refs[12:22], refs[22]
    own = pl.ds(pl.multiple_of(lax.axis_index("rep") * OWN, OWN), OWN)
    copies = []
    for index, (source, target) in enumerate(zip(given, held)):
        source = source.at[:, :, own] if index == 1 else source.at[:, own] if index == 2 else source
        copies.append(pltpu.make_async_copy(source, target, arrived.at[index]))
        copies[-1].start()
    for copy in copies:
        copy.wait()
    features, coords, kinds, groups, layer_in, layer_bias, layer_mid, layer_out, widths, hardness = held
    for line, source in enumerate((widths, hardness)):
        for kind in range(ELEMS):
            row = jnp.broadcast_to(source[0:1, kind : kind + 1], (1, LANES))
            constants[2 * line + kind : 2 * line + kind + 1, :] = row
    frames = features.shape[0]
    wide = jnp.concatenate([features[frame] for frame in range(frames)], axis=1)
    first, second = network(layer_in, layer_bias, layer_mid, layer_out, wide)
    for frame in range(frames):
        span = slice(frame * OWN, frame * OWN + OWN)
        kind = kinds[frame : frame + 1, :]
        electroneg = jnp.where(kind == 1, second[:, span], first[:, span])
        values = [coords[axis, frame : frame + 1, :] for axis in range(3)]
        values += [kind.astype(float32), electroneg, groups[frame : frame + 1, :].astype(float32)]
        for pair in range(3):
            one, two = values[2 * pair], values[2 * pair + 1]
            block = jnp.concatenate([one[:, :LANES], one[:, LANES:], two[:, :LANES], two[:, LANES:]], axis=0)
            for target in range(BLKS // frames):
                message[frame * (BLKS // frames) + target, pair] = block


def fill_rows(atoms, own_block, constants, rows):
    narrow, broad = constants[0:1, 0:1], constants[1:2, 0:1]
    for half in range(2):
        span = slice(half * LANES, half * LANES + LANES)
        for axis, (pair, line) in enumerate(((0, 0), (0, 2), (1, 0))):
            rows[axis, span] = as_rows(atoms[own_block, pair, line + half : line + half + 1, :])
        kind = as_rows(atoms[own_block, 1, 2 + half : 3 + half, :])
        width = jnp.where(kind > 0.5, broad, narrow)
        rows[3, span] = lax.rsqrt(width * width + narrow * narrow)
        rows[4, span] = lax.rsqrt(width * width + broad * broad)


def build_piece(atoms, rows, piece):
    def one_block(block, carry):
        for half in range(2):
            x, y, z, kind = (
                jnp.broadcast_to(atoms[block, pair, line + half : line + half + 1, :], (8, LANES))
                for pair, line in ((0, 0), (0, 2), (1, 0), (1, 2))
            )
            second = kind > 0.5
            for group in range(GROUPS):
                span = slice(group * 8, group * 8 + 8)
                delta_x = rows[0, span] - x
                delta_y = rows[1, span] - y
                delta_z = rows[2, span] - z
                squared = delta_x * delta_x + delta_y * delta_y + delta_z * delta_z
                inverse = lax.rsqrt(squared)
                scale = jnp.where(second, rows[4, span], rows[3, span])
                piece[2 * block + half, span, :] = lax.erf(squared * inverse * scale) * inverse
        return carry

    lax.fori_loop(0, BLKS, one_block, 0, unroll=2)


def build_own_kernel(atoms, constants, piece, rows):
    _, own_block, _ = place_of()
    fill_rows(atoms, own_block, constants, rows)
    build_piece(atoms, rows, piece)
    width_0, width_1, hardness_0, hardness_1 = (constants[line : line + 1, 0:1] for line in range(4))
    for half in range(2):
        span = slice(half * LANES, half * LANES + LANES)
        second = as_rows(atoms[own_block, 1, 2 + half : 3 + half, :]) > 0.5
        diagonal = jnp.where(second, hardness_1, hardness_0) + inv_sqrt_pi / jnp.where(second, width_1, width_0)
        tile = piece[2 * own_block + half, span, :]
        piece[2 * own_block + half, span, :] = jnp.where(eye(LANES), diagonal, tile)


def apply_rows(pieces, direction, rep):
    sums = tuple(jnp.zeros((8, LANES), float32) for _ in range(GROUPS))
    for turn, piece in enumerate(pieces):
        first = lax.rem(rep + turn, REPS) * PIECE

        def one_line(line, sums):
            values = jnp.broadcast_to(direction[pl.ds(first + line, 1), :], (8, LANES))
            return tuple(
                sums[group] + piece[line, group * 8 : group * 8 + 8, :] * values for group in range(GROUPS)
            )

        sums = lax.fori_loop(0, PIECE, one_line, sums, unroll=8)
    half = GROUPS // 2
    return [
        jnp.sum(jnp.concatenate(sums[part * half : part * half + half], axis=0).T, axis=0, keepdims=True)
        for part in range(2)
    ]


def write_message(image, message):
    block = jnp.concatenate(image * 4, axis=0)
    for line in range(ROWS // 8):
        message[line * 8 : line * 8 + 8, :] = block


def project(vector, groups):
    members = ROWS * LANES // FRAGS
    taken = jnp.zeros_like(vector)
    for group in range(FRAGS):
        inside = groups == float(group)
        mean = total_of(jnp.where(inside, vector, 0.0)) / members
        taken = jnp.where(inside, mean, taken)
    return vector - taken


def first_kernel(*refs):
    parts, (rows, own_piece), pieces = refs[:4], refs[4:6], refs[6:9]
    message, residual, groups, norm = refs[9:]
    rep, _, _ = place_of()
    for part, piece in zip(parts[1:], pieces):
        build_piece(part, rows, piece)
    for turn, part in enumerate(parts):
        first = lax.rem(rep + turn, REPS) * PIECE
        for block in range(BLKS):
            residual[pl.ds(first + block * 2, 2), :] = part[block, 2, 0:2, :]
            groups[pl.ds(first + block * 2, 2), :] = part[block, 2, 2:4, :]
    start = -project(residual[...], groups[...])
    residual[...] = start
    norm[...] = jnp.broadcast_to(total_of(start * start), norm.shape)
    write_message(apply_rows((own_piece, *pieces), residual, rep), message)


def update(image, residual, direction, charges, groups, norm, residual_out, direction_out, charges_out):
    norm_now = norm[0:1, 0:1]
    along, whole = direction[...], image[...]
    step = norm_now / total_of(along * whole)
    charges_out[...] = step * along if charges is None else charges[...] + step * along
    left = residual[...] - step * project(whole, groups[...])
    residual_out[...] = left
    norm_next = total_of(left * left)
    direction_out[...] = left + norm_next / norm_now * along
    return norm_next


def iterate_kernel(*refs, begun):
    image, residual, direction = refs[:3]
    charges = refs[3] if begun else None
    groups, norm, *pieces = refs[3 + begun : 9 + begun]
    message, residual_out, direction_out, charges_out, norm_out = refs[9 + begun :]
    norm_next = update(image, residual, direction, charges, groups, norm, residual_out, direction_out, charges_out)
    norm_out[...] = jnp.broadcast_to(norm_next, norm_out.shape)
    write_message(apply_rows(pieces, direction_out, place_of()[0]), message)


def last_kernel(
    image, residual, direction, charges, groups, norm, own, piece_1, piece_2, piece_3, share, message, *scratch
):
    residual_out, direction_out, charges_out = scratch
    rep, own_block, window = place_of()
    norm_next = update(image, residual, direction, charges, groups, norm, residual_out, direction_out, charges_out)
    applied = apply_rows((own, piece_1, piece_2, piece_3), direction_out, rep)
    line = rep * PIECE + own_block * 2
    part = applied[0] * direction_out[pl.ds(line, 1), :] + applied[1] * direction_out[pl.ds(line + 1, 1), :]
    share[...] = jnp.broadcast_to(jnp.sum(part, axis=1, keepdims=True) / norm_next, share.shape)
    lines = pl.ds(rep * PIECE + lax.rem(window // 2, 2), BLKS, stride=2)
    message[...] = jnp.where(window < 4, charges_out[lines, :], direction_out[lines, :])


def join_kernel(shares, message, out):
    _, _, window = place_of()
    lane = lax.broadcasted_iota(jnp.int32, message.shape, 1)
    out[...] = jnp.where(lane // WINDOW == lax.rem(window, 2), message[...], total_of(shares[:, 0:1]))


def input_layer_kernel(features, layer_in, layer_bias, out):
    frame = lax.axis_index("phase")
    for kind in range(ELEMS):
        product = jnp.dot(layer_in[:, kind, :], features[frame], precision=highest, preferred_element_type=float32)
        out[kind] = product + as_column(layer_bias[kind : kind + 1, :])


def finish_kernel(parts, inputs, kinds, layer_charge, layer_mid, layer_out, charges_out, energies_out):
    frame = lax.axis_index("phase")
    senders = LANES // WINDOW * 4
    block = parts[pl.ds(pl.multiple_of(frame * senders, senders), senders), :]
    lane = lax.broadcasted_iota(jnp.int32, block.shape, 1) // WINDOW
    sender = lax.broadcasted_iota(jnp.int32, block.shape, 0)
    inside = lane == lax.rem(sender, 2)
    lines = [
        jnp.sum(jnp.where(inside & (sender // 2 == line), block, 0.0), axis=0, keepdims=True) for line in range(4)
    ]
    step = LANES - WINDOW
    step = step / total_of(jnp.where(inside, 0.0, block))
    charges = jnp.concatenate([lines[0] + step * lines[2], lines[1] + step * lines[3]], axis=1)
    charges_out[...] = charges
    outs = []
    for kind in range(ELEMS):
        hidden_one = jnp.tanh(inputs[kind] + as_column(layer_charge[kind : kind + 1, :]) * charges)
        outs.append(last_layers(layer_mid, layer_out, hidden_one, kind))
    own = pl.ds(pl.multiple_of(lax.axis_index("rep") * OWN, OWN), OWN)
    energies_out[...] = jnp.where(kinds[pl.ds(frame, 1), own] == 1, outs[1], outs[0])


def call(kernel, outs, name, scratch=(), flops=0, held=VMEM):
    def run(*args):
        many = isinstance(outs, list)
        return pl.pallas_call(
            kernel,
            out_shape=outs,
            in_specs=[held] * len(args),
            out_specs=[VMEM] * len(outs) if many else VMEM,
            scratch_shapes=list(scratch),
            compiler_params=PARAMS,
            cost_estimate=pl.CostEstimate(flops=flops, bytes_accessed=0, transcendentals=0) if flops else None,
            name=name,
        )(*args)

    return run


def on_device(
    descriptors,
    positions,
    elements,
    fragments,
    neg_input,
    neg_bias,
    neg_hidden,
    neg_output,
    short_input,
    short_charge,
    short_bias,
    short_hidden,
    short_output,
    widths,
    hardness,
):
    block_axes = ("zq", "zr", "core")
    cube_axes = ("rep", "phase", "zr", "core")
    piece = pltpu.VMEM((PIECE, OWN, LANES), float32)
    rows = pltpu.VMEM((5, OWN, LANES), float32)
    whole = shaped(ROWS, LANES)
    small = shaped(8, LANES)

    def exchange(message):
        sent = message.reshape(ROWS // 2, 2, LANES)
        return lax.all_to_all(sent, cube_axes, 0, 0).reshape(ROWS, LANES)

    def kept(pieces):
        return [pltpu.with_memory_space_constraint(one, pltpu.VMEM) for one in pieces]

    def turned(layer):
        return jnp.transpose(layer, (1, 0, 2))

    given = [descriptors, turned(positions), elements, fragments, turned(neg_input), neg_bias, turned(neg_hidden)]
    given += [neg_output, widths[None, :], hardness[None, :]]
    held = [pltpu.VMEM(one.shape, one.dtype) for one in given]
    held[1] = pltpu.VMEM((3, elements.shape[0], OWN), float32)
    held[2] = pltpu.VMEM((elements.shape[0], OWN), jnp.int32)
    message, constants = call(
        prepare_kernel,
        [shaped(BLKS, 3, 4, LANES), small],
        "prepare",
        held + [pltpu.SemaphoreType.DMA((len(given),))],
        held=pl.BlockSpec(memory_space=pl.ANY),
    )(*[pltpu.with_memory_space_constraint(one, pltpu.HBM) for one in given])
    atoms_own = lax.all_to_all(message, block_axes, 0, 0)
    parts = [
        lax.ppermute(atoms_own, "rep", [((rep + turn) % REPS, rep) for rep in range(REPS)]) for turn in range(1, REPS)
    ]
    own_piece, row_values = call(build_own_kernel, [piece, rows], "build_own", flops=10**9)(atoms_own, constants)
    *rest, message, residual, groups, norm = call(
        first_kernel, [piece] * 3 + [whole, whole, whole, small], "build_rest_and_begin"
    )(atoms_own, *parts, *kept([row_values, own_piece]))
    pieces = [own_piece] + rest
    message, residual, direction, charges, norm = call(
        functools.partial(iterate_kernel, begun=0), [whole, whole, whole, whole, small], "iterate"
    )(exchange(message), residual, residual, groups, norm, *kept(pieces))
    message, residual, direction, charges, norm = call(
        functools.partial(iterate_kernel, begun=1), [whole, whole, whole, whole, small], "iterate"
    )(exchange(message), residual, direction, charges, groups, norm, *kept(pieces))
    share, message = call(
        last_kernel, [shaped(16, LANES), shaped(BLKS, LANES)], "last", [pltpu.VMEM((ROWS, LANES), float32)] * 3
    )(exchange(message), residual, direction, charges, groups, norm, *kept(pieces))
    shares = lax.all_to_all(share.reshape(16, 1, LANES), ("phase", "rep"), 0, 0).reshape(16, LANES)
    message = call(join_kernel, shaped(BLKS, LANES), "join")(shares, message)
    parts = lax.all_to_all(message.reshape(BLKS, 1, LANES), block_axes, 0, 0).reshape(BLKS, LANES)
    inputs = call(input_layer_kernel, shaped(ELEMS, short_bias.shape[1], OWN), "input_layer", flops=10**7)(
        descriptors, turned(short_input), short_bias
    )
    return call(finish_kernel, [shaped(1, OWN), shaped(1, OWN)], "finish")(
        parts, inputs, elements, short_charge, turned(short_hidden), short_output
    )


def solution(mesh):
    split = Mesh(mesh.devices.reshape(4, 4, 4, 2, 4), ("phase", "zq", "zr", "core", "rep"))
    block_axes = ("zq", "zr", "core")
    return jax.shard_map(
        on_device,
        mesh=split,
        in_specs=(
            P(None, None, block_axes + ("rep",)),
            P(None, None, block_axes),
            P(None, block_axes),
            P(None, block_axes + ("rep",)),
        )
        + (P(),) * 11,
        out_specs=(P("phase", block_axes + ("rep",)), P("phase", block_axes + ("rep",))),
        check_vma=False,
    )
```

time: 176 us -> 161 us (0.915)
  local copies, waits for them, and re-layouts: 15 us -> 0.03 us
  Pallas kernels: 36.6 us -> 32 us
  starting transfers between devices: 12.3 us -> 16.1 us
    unnamed x41 -> x14, local copies, waits for them, and re-layouts: 13.9 us -> 0.03 us
    ppermute x0 -> x3, starting transfers between devices: none -> 9.48 us  [on_device(): lax.ppermute(atoms_own, 'rep', [((rep + turn) % REPS, rep) for rep in ran...]
    all_to_all x2 -> x1, starting transfers between devices: 12.3 us -> 6.61 us  [on_device(): lax.all_to_all(message.reshape(BLKS, 1, LANES), block_axes, 0, 0)]
    pallas_call x8 -> x9, Pallas kernels: 36.6 us -> 32 us  [run(): pl.pallas_call(kernel, out_shape=outs, in_specs=[held] * len(args), out_s...]
    ppermute x0 -> x3, waiting for transfers between devices: none -> 3.71 us  [on_device(): lax.ppermute(atoms_own, 'rep', [((rep + turn) % REPS, rep) for rep in ran...]
    all_to_all x2 -> x1, waiting for transfers between devices: 15.3 us -> 11.6 us  [on_device(): lax.all_to_all(message.reshape(BLKS, 1, LANES), block_axes, 0, 0)]
    all_to_all x1, blocking collectives: 6.44 us -> 8.95 us  [on_device(): lax.all_to_all(share.reshape(16, 1, LANES), ('phase', 'rep'), 0, 0)]
    all_to_all x3, blocking collectives: 54 us -> 52.2 us  [exchange(): return lax.all_to_all(sent, cube_axes, 0, 0).reshape(ROWS, LANES)]
  transfers between devices with their start and end apart: 2 -> 4, of which waited for: 2 -> 2; matrix products, arithmetic and copies ran while one was open for 0% -> 0% of each run, Pallas kernels for 3% -> 3%
where the time goes in v2:
time: 161 us
  blocking collectives  96.3 us (60%)
  Pallas kernels  32 us (20%)
  starting transfers between devices  16.1 us (10%)
  waiting for transfers between devices  15.3 us (10%)
    all_to_all x3, blocking collectives, exchange(): return lax.all_to_all(sent, cube_axes, 0, 0).reshape(ROWS, LANES)  52.2 us
    all_to_all x1, blocking collectives, on_device(): atoms_own = lax.all_to_all(message, block_axes, 0, 0)  35.2 us
    pallas_call x9, Pallas kernels, run(): pl.pallas_call(kernel, out_shape=outs, in_specs=[held] * len(args), out_s...  32 us
    all_to_all x1, waiting for transfers between devices, on_device(): lax.all_to_all(message.reshape(BLKS, 1, LANES), block_axes, 0, 0)  11.6 us
    ppermute x3, starting transfers between devices, on_device(): lax.ppermute(atoms_own, 'rep', [((rep + turn) % REPS, rep) for rep in ran...  9.48 us
    all_to_all x1, blocking collectives, on_device(): lax.all_to_all(share.reshape(16, 1, LANES), ('phase', 'rep'), 0, 0)  8.95 us
    all_to_all x1, starting transfers between devices, on_device(): lax.all_to_all(message.reshape(BLKS, 1, LANES), block_axes, 0, 0)  6.61 us
    ppermute x3, waiting for transfers between devices, on_device(): lax.ppermute(atoms_own, 'rep', [((rep + turn) % REPS, rep) for rep in ran...  3.71 us
  transfers between devices with their start and end apart: 4, of which 2 were waited for; matrix products, arithmetic and copies ran while one was open for 0% of the time, Pallas kernels for 3%

profile of v2, /device:TPU:1, one launch (start us, length us, event | category | flops | bytes accessed | tf_op | source)
XLA Modules:
  0.0 160.5 jit_solution(15194981846608820055)
XLA Ops:
  0.6 1.7 %prepare.1 = (f32[32,3,4,128]{3,2,1,0:T(4,128)S(1)}, f32[8,128]{1,0:T(8,128)S(1)}) custom-call(f32[4,32,256]{2,1,0:T(8,128)} %features.1, f32[3,4,1024]{2,1,0:T(4,128)} %bitcast.32, s32[4,1024]{1,0:T(4,128)} %kinds.1, s32[4,256]{1,0:T(4,128)} %refs_3_.1, f32[15,2,32]{2,1,0:T(2,128)} %bitcast.33, f32[2,15]{1,0:T(2,128)} %refs_5_.1, f32[15,2,15]{2,1,0:T(2,128)} %bitcast.34, ...), custom_call_target="tpu_custom_call" | custom-call | tf_op jit(solution)/shard_map/prepare/pallas_call | solution.py:274
  2.3 35.2 %all_to_all.30.atoms.refs_0_ = f32[32,3,4,128]{3,2,1,0:T(4,128)S(1)} all-to-all(f32[32,3,4,128]{3,2,1,0:T(4,128)S(1)} %get-tuple-element.25), channel_id=1, replica_groups=mesh['phase'=4,'zq'=4,'zr'=4,'core'=2,'rep'=4] {'zq','zr','core'}, dimensions={0} | all-to-all | bytes 393216 | tf_op jit(solution)/shard_map/all_to_all | solution.py:334
  37.5 4.6 %collective-permute-start = (f32[32,3,4,128]{3,2,1,0:T(4,128)S(1)}, f32[32,3,4,128]{3,2,1,0:T(4,128)S(1)}, u32[]{:S(2)}, u32[]{:S(2)}) collective-permute-start(f32[32,3,4,128]{3,2,1,0:T(4,128)S(1)} %all_to_all.30.atoms.refs_0_), channel_id=1, source_target_pairs={{1,0},{2,1},{3,2},{0,3},{5,4},{6,5},{7,6},{4,7},{9,8},{10,9},{11,1... | collective-permute-start | bytes 589832 | tf_op jit(solution)/shard_map/ppermute | solution.py:336
  42.1 2.3 %collective-permute-start.1 = (f32[32,3,4,128]{3,2,1,0:T(4,128)S(1)}, f32[32,3,4,128]{3,2,1,0:T(4,128)S(1)}, u32[]{:S(2)}, u32[]{:S(2)}) collective-permute-start(f32[32,3,4,128]{3,2,1,0:T(4,128)S(1)} %all_to_all.30.atoms.refs_0_), channel_id=1, source_target_pairs={{2,0},{3,1},{0,2},{1,3},{6,4},{7,5},{4,6},{5,7},{10,8},{11,9},{8,1... | collective-permute-start | bytes 589832 | tf_op jit(solution)/shard_map/ppermute | solution.py:336
  44.4 2.6 %collective-permute-start.2 = (f32[32,3,4,128]{3,2,1,0:T(4,128)S(1)}, f32[32,3,4,128]{3,2,1,0:T(4,128)S(1)}, u32[]{:S(2)}, u32[]{:S(2)}) collective-permute-start(f32[32,3,4,128]{3,2,1,0:T(4,128)S(1)} %all_to_all.30.atoms.refs_0_), channel_id=1, source_target_pairs={{3,0},{0,1},{1,2},{2,3},{7,4},{4,5},{5,6},{6,7},{11,8},{8,9},{9,10... | collective-permute-start | bytes 589832 | tf_op jit(solution)/shard_map/ppermute | solution.py:336
  47.0 4.4 %build_own.1 = (f32[64,256,128]{2,1,0:T(8,128)S(1)}, f32[5,256,128]{2,1,0:T(8,128)S(1)}) custom-call(f32[32,3,4,128]{3,2,1,0:T(4,128)S(1)} %all_to_all.30.atoms.refs_0_, f32[8,128]{1,0:T(8,128)S(1)} %get-tuple-element.26.constants), custom_call_target="tpu_custom_call" | custom-call | flops 1000000000 | tf_op jit(solution)/shard_map/build_own/pallas_call | solution.py:274
  51.4 0.0 collective-permute-done.refs_1_
  51.4 0.0 collective-permute-done.1.refs_2_
  51.4 3.7 %collective-permute-done.2.refs_3_ = f32[32,3,4,128]{3,2,1,0:T(4,128)S(1)} collective-permute-done((f32[32,3,4,128]{3,2,1,0:T(4,128)S(1)}, f32[32,3,4,128]{3,2,1,0:T(4,128)S(1)}, u32[]{:S(2)}, u32[]{:S(2)}) %collective-permute-start.2) | collective-permute-done | bytes 196640 | tf_op jit(solution)/shard_map/ppermute | solution.py:336
  55.1 15.2 %build_rest_and_begin.1 = (f32[64,256,128]{2,1,0:T(8,128)S(1)}, f32[64,256,128]{2,1,0:T(8,128)S(1)}, f32[64,256,128]{2,1,0:T(8,128)S(1)}, f32[256,128]{1,0:T(8,1...) custom-call(f32[32,3,4,128]{3,2,1,0:T(4,128)S(1)} %all_to_all.30.atoms.refs_0_, ...), custom_call_target="tpu_custom_call" | custom-call | tf_op jit(solution)/shard_map/build_rest_and_begin/pallas_call | solution.py:274
  70.3 18.9 %all_to_all.31 = f32[128,2,128]{2,1,0:T(2,128)S(1)} all-to-all(f32[128,2,128]{2,1,0:T(2,128)S(1)} %bitcast.24), channel_id=1, replica_groups=mesh['phase'=4,'zq'=4,'zr'=4,'core'=2,'rep'=4] {'rep','phase','zr','core'}, dimensions={0} | all-to-all | bytes 262144 | tf_op jit(solution)/shard_map/all_to_all | solution.py:314
  89.3 3.0 %iterate.2 = (f32[256,128]{1,0:T(8,128)S(1)}, f32[256,128]{1,0:T(8,128)S(1)}, f32[256,128]{1,0:T(8,128)S(1)}, f32[256,128]{1,0:T(8,128)S(1)}, f32[8,128]{1,0:T(8,128)S(1)}) custom-call(f32[256,128]{1,0:T(8,128)S(1)} %bitcast.23, f32[256,128]{1,0:T(8,128)S(1)} %get-tuple-element.30.refs_1_.refs_2_, f32[256,128]{1,0:T(8,128)S(1)} %get-tuple-element.30.refs_1_.refs_2_, ...), custom_call_target="tpu_custom_call" | custom-call | tf_op jit(solution)/shard_map/iterate/pallas_call | solution.py:274
  92.3 16.6 %all_to_all.32 = f32[128,2,128]{2,1,0:T(2,128)S(1)} all-to-all(f32[128,2,128]{2,1,0:T(2,128)S(1)} %bitcast.26), channel_id=1, replica_groups=mesh['phase'=4,'zq'=4,'zr'=4,'core'=2,'rep'=4] {'rep','phase','zr','core'}, dimensions={0} | all-to-all | bytes 262144 | tf_op jit(solution)/shard_map/all_to_all | solution.py:314
  108.9 3.0 %iterate.3 = (f32[256,128]{1,0:T(8,128)S(1)}, f32[256,128]{1,0:T(8,128)S(1)}, f32[256,128]{1,0:T(8,128)S(1)}, f32[256,128]{1,0:T(8,128)S(1)}, f32[8,128]{1,0:T(8,128)S(1)}) custom-call(f32[256,128]{1,0:T(8,128)S(1)} %bitcast.22, f32[256,128]{1,0:T(8,128)S(1)} %get-tuple-element.37.refs_1_, f32[256,128]{1,0:T(8,128)S(1)} %get-tuple-element.38.refs_2_, ...), custom_call_target="tpu_custom_call" | custom-call | tf_op jit(solution)/shard_map/iterate/pallas_call | solution.py:274
  111.9 16.6 %all_to_all.33 = f32[128,2,128]{2,1,0:T(2,128)S(1)} all-to-all(f32[128,2,128]{2,1,0:T(2,128)S(1)} %bitcast.25), channel_id=1, replica_groups=mesh['phase'=4,'zq'=4,'zr'=4,'core'=2,'rep'=4] {'rep','phase','zr','core'}, dimensions={0} | all-to-all | bytes 262144 | tf_op jit(solution)/shard_map/all_to_all | solution.py:314
  128.5 0.0 copy-start
  128.5 0.0 copy-start.3
  128.5 0.0 copy-start.4
  128.5 0.0 copy-start.1
  128.5 0.0 copy-start.2
  128.5 0.0 copy-start.5
  128.5 0.0 copy-start.6
  128.6 3.1 %last.1 = (f32[16,128]{1,0:T(8,128)S(1)}, f32[32,128]{1,0:T(8,128)S(1)}) custom-call(f32[256,128]{1,0:T(8,128)S(1)} %bitcast.21, f32[256,128]{1,0:T(8,128)S(1)} %get-tuple-element.42.residual, f32[256,128]{1,0:T(8,128)S(1)} %get-tuple-element.43.direction, f32[256,128]{1,0:T(8,128)S(1)} %get-tuple-element.44.charges, ...), custom_call_target="tpu_custom_call" | custom-call | tf_op jit(solution)/shard_map/last/pallas_call | solution.py:274
  131.6 9.0 %all_to_all.34 = f32[16,1,128]{2,1,0:T(1,128)S(1)} all-to-all(f32[16,1,128]{2,1,0:T(1,128)S(1)} %bitcast.31), channel_id=1, replica_groups=mesh['phase'=4,'zq'=4,'zr'=4,'core'=2,'rep'=4] {'phase','rep'}, dimensions={0} | all-to-all | bytes 16384 | tf_op jit(solution)/shard_map/all_to_all | solution.py:352
  140.6 0.7 join.1
  141.2 6.6 %all-to-all-start.5 = ((f32[32,1,128]{2,1,0:T(1,128)}), f32[32,1,128]{2,1,0:T(1,128)S(1)}, u32[]{:S(2)}, u32[]{:S(2)}) async-start(f32[32,1,128]{2,1,0:T(1,128)} %bitcast.15), calls=%async_computation.5 | async-start | bytes 32768 | tf_op jit(solution)/shard_map/all_to_all | solution.py:354
  147.9 0.0 copy-done
  147.9 0.0 copy-done.3
  147.9 0.0 copy-done.4
  147.9 0.1 input_layer.1.inputs
  148.0 11.6 %all-to-all-done.5 = f32[32,1,128]{2,1,0:T(1,128)S(1)} async-done(((f32[32,1,128]{2,1,0:T(1,128)}), f32[32,1,128]{2,1,0:T(1,128)S(1)}, u32[]{:S(2)}, u32[]{:S(2)}) %all-to-all-start.5) | async-done | bytes 16416 | tf_op jit(solution)/shard_map/all_to_all | solution.py:354
  159.6 0.0 copy-done.1
  159.6 0.0 copy-done.2
  159.6 0.0 copy-done.5
  159.6 0.0 copy-done.6
  159.7 0.9 finish.1
Async XLA Ops:
  37.5 13.9 %collective-permute-start = (f32[32,3,4,128]{3,2,1,0:T(4,128)S(1)}, f32[32,3,4,128]{3,2,1,0:T(4,128)S(1)}, u32[]{:S(2)}, u32[]{:S(2)}) collective-permute-start(f32[32,3,4,128]{3,2,1,0:T(4,128)S(1)} %all_to_all.30.atoms.refs_0_), channel_id=1, source_target_pairs={{1,0},{2,1},{3,2},{0,3},{5,4},{6,5},{7,6},{4,7},{9,8},{10,9},{11,1... | collective-permute-start | bytes 589832 | tf_op jit(solution)/shard_map/ppermute | solution.py:336
  42.1 9.3 %collective-permute-start.1 = (f32[32,3,4,128]{3,2,1,0:T(4,128)S(1)}, f32[32,3,4,128]{3,2,1,0:T(4,128)S(1)}, u32[]{:S(2)}, u32[]{:S(2)}) collective-permute-start(f32[32,3,4,128]{3,2,1,0:T(4,128)S(1)} %all_to_all.30.atoms.refs_0_), channel_id=1, source_target_pairs={{2,0},{3,1},{0,2},{1,3},{6,4},{7,5},{4,6},{5,7},{10,8},{11,9},{8,1... | collective-permute-start | bytes 589832 | tf_op jit(solution)/shard_map/ppermute | solution.py:336
  44.4 10.7 %collective-permute-start.2 = (f32[32,3,4,128]{3,2,1,0:T(4,128)S(1)}, f32[32,3,4,128]{3,2,1,0:T(4,128)S(1)}, u32[]{:S(2)}, u32[]{:S(2)}) collective-permute-start(f32[32,3,4,128]{3,2,1,0:T(4,128)S(1)} %all_to_all.30.atoms.refs_0_), channel_id=1, source_target_pairs={{3,0},{0,1},{1,2},{2,3},{7,4},{4,5},{5,6},{6,7},{11,8},{8,9},{9,10... | collective-permute-start | bytes 589832 | tf_op jit(solution)/shard_map/ppermute | solution.py:336
  128.5 19.3 %copy-start = (f32[4,32,256]{2,1,0:T(8,128)S(1)}, f32[4,32,256]{2,1,0:T(8,128)}, u32[]{:S(2)}) copy-start(f32[4,32,256]{2,1,0:T(8,128)} %features.1) | copy-start | bytes 393220
  128.5 19.4 %copy-start.3 = (f32[2,15,32]{2,0,1:T(2,128)S(1)}, f32[2,15,32]{2,0,1:T(2,128)}, u32[]{:S(2)}) copy-start(f32[2,15,32]{2,0,1:T(2,128)} %param.23) | copy-start | bytes 11524
  128.5 19.4 %copy-start.4 = (f32[2,15]{1,0:T(2,128)S(1)}, f32[2,15]{1,0:T(2,128)}, u32[]{:S(2)}) copy-start(f32[2,15]{1,0:T(2,128)} %layer_bias.1) | copy-start | bytes 364
  128.5 31.1 %copy-start.1 = (s32[4,1024]{1,0:T(4,128)S(1)}, s32[4,1024]{1,0:T(4,128)}, u32[]{:S(2)}) copy-start(s32[4,1024]{1,0:T(4,128)} %kinds.1) | copy-start | bytes 49156
  128.5 31.1 %copy-start.2 = (f32[2,15,15]{2,0,1:T(2,128)S(1)}, f32[2,15,15]{2,0,1:T(2,128)}, u32[]{:S(2)}) copy-start(f32[2,15,15]{2,0,1:T(2,128)} %param.26) | copy-start | bytes 5404
  128.5 31.1 %copy-start.5 = (f32[2,15]{1,0:T(2,128)S(1)}, f32[2,15]{1,0:T(2,128)}, u32[]{:S(2)}) copy-start(f32[2,15]{1,0:T(2,128)} %layer_charge.1) | copy-start | bytes 364
  128.5 31.1 %copy-start.6 = (f32[2,15]{1,0:T(2,128)S(1)}, f32[2,15]{1,0:T(2,128)}, u32[]{:S(2)}) copy-start(f32[2,15]{1,0:T(2,128)} %layer_out.1) | copy-start | bytes 364
  141.2 18.4 %all-to-all-start.5 = ((f32[32,1,128]{2,1,0:T(1,128)}), f32[32,1,128]{2,1,0:T(1,128)S(1)}, u32[]{:S(2)}, u32[]{:S(2)}) async-start(f32[32,1,128]{2,1,0:T(1,128)} %bitcast.15), calls=%async_computation.5 | async-start | bytes 32768 | tf_op jit(solution)/shard_map/all_to_all | solution.py:354

commit v3 on v2

--- a/solution.py
+++ b/solution.py
@@ -2,6 +2,7 @@
 
 import jax
 import jax.numpy as jnp
+import numpy as np
 from jax import lax
 from jax.experimental import pallas as pl
 from jax.experimental.pallas import tpu as pltpu
@@ -63,8 +64,35 @@
 
 
 def place_of():
-    window = lax.axis_index("zr") * 2 + lax.axis_index("core")
-    return lax.axis_index("rep"), lax.axis_index("phase") * 8 + window, window
+    core, spot = lax.axis_index("core"), lax.axis_index("zr")
+    turned = jnp.where(lax.axis_index("zq") < 2, 3 - spot, spot)
+    return lax.axis_index("rep"), core * 16 + lax.rem(lax.axis_index("phase") + 2, 4) * 4 + turned, core * 4 + spot
+
+
+def row_of(rep, line):
+    return line // 32 * 128 + lax.rem(rep + 2, 4) * 32 + line % 32
+
+
+def all_devices():
+    return np.arange(512).reshape(4, 4, 4, 2, 4)[[2, 3, 0, 1]][..., [2, 3, 0, 1]]
+
+
+def listed(groups):
+    return [[int(device) for device in group] for group in groups]
+
+
+def cube_groups():
+    devices = all_devices()
+    devices[:, :2] = devices[:, :2, ::-1].copy()
+    return listed(devices.transpose(1, 3, 4, 0, 2).reshape(4, 128))
+
+
+def block_groups():
+    return listed(all_devices()[:, [2, 3, 0, 1]].transpose(0, 4, 3, 1, 2).reshape(16, BLKS))
+
+
+def layer_groups():
+    return listed(all_devices().transpose(1, 2, 3, 0, 4).reshape(BLKS, 16))
 
 
 def prepare_kernel(*refs):
@@ -95,7 +123,7 @@
             one, two = values[2 * pair], values[2 * pair + 1]
             block = jnp.concatenate([one[:, :LANES], one[:, LANES:], two[:, :LANES], two[:, LANES:]], axis=0)
             for target in range(BLKS // frames):
-                message[frame * (BLKS // frames) + target, pair] = block
+                message[target // 4 * 16 + (frame + 2) % 4 * 4 + target % 4, pair] = block
 
 
 def fill_rows(atoms, own_block, constants, rows):
@@ -148,15 +176,17 @@
 def apply_rows(pieces, direction, rep):
     sums = tuple(jnp.zeros((8, LANES), float32) for _ in range(GROUPS))
     for turn, piece in enumerate(pieces):
-        first = lax.rem(rep + turn, REPS) * PIECE
-
-        def one_line(line, sums):
-            values = jnp.broadcast_to(direction[pl.ds(first + line, 1), :], (8, LANES))
-            return tuple(
-                sums[group] + piece[line, group * 8 : group * 8 + 8, :] * values for group in range(GROUPS)
-            )
-
-        sums = lax.fori_loop(0, PIECE, one_line, sums, unroll=8)
+        for core in range(2):
+            first = row_of(lax.rem(rep + turn, REPS), core * BLKS)
+
+            def one_line(line, sums, core=core, piece=piece, first=first):
+                values = jnp.broadcast_to(direction[pl.ds(first + line, 1), :], (8, LANES))
+                here = core * BLKS + line
+                return tuple(
+                    sums[group] + piece[here, group * 8 : group * 8 + 8, :] * values for group in range(GROUPS)
+                )
+
+            sums = lax.fori_loop(0, BLKS, one_line, sums, unroll=8)
     half = GROUPS // 2
     return [
         jnp.sum(jnp.concatenate(sums[part * half : part * half + half], axis=0).T, axis=0, keepdims=True)
@@ -180,21 +210,26 @@
     return vector - taken
 
 
+def build_kernel(part_1, part_3, rows, piece_1, piece_3):
+    build_piece(part_1, rows, piece_1)
+    build_piece(part_3, rows, piece_3)
+
+
 def first_kernel(*refs):
-    parts, (rows, own_piece), pieces = refs[:4], refs[4:6], refs[6:9]
+    parts, (rows, own_piece, piece_1, piece_3, piece_2) = refs[:4], refs[4:9]
     message, residual, groups, norm = refs[9:]
     rep, _, _ = place_of()
-    for part, piece in zip(parts[1:], pieces):
-        build_piece(part, rows, piece)
+    build_piece(parts[2], rows, piece_2)
     for turn, part in enumerate(parts):
-        first = lax.rem(rep + turn, REPS) * PIECE
+        source = lax.rem(rep + turn, REPS)
         for block in range(BLKS):
-            residual[pl.ds(first + block * 2, 2), :] = part[block, 2, 0:2, :]
-            groups[pl.ds(first + block * 2, 2), :] = part[block, 2, 2:4, :]
+            lines = pl.ds(row_of(source, block * 2), 2)
+            residual[lines, :] = part[block, 2, 0:2, :]
+            groups[lines, :] = part[block, 2, 2:4, :]
     start = -project(residual[...], groups[...])
     residual[...] = start
     norm[...] = jnp.broadcast_to(total_of(start * start), norm.shape)
-    write_message(apply_rows((own_piece, *pieces), residual, rep), message)
+    write_message(apply_rows((own_piece, piece_1, piece_2, piece_3), residual, rep), message)
 
 
 def update(image, residual, direction, charges, groups, norm, residual_out, direction_out, charges_out):
@@ -226,11 +261,13 @@
     rep, own_block, window = place_of()
     norm_next = update(image, residual, direction, charges, groups, norm, residual_out, direction_out, charges_out)
     applied = apply_rows((own, piece_1, piece_2, piece_3), direction_out, rep)
-    line = rep * PIECE + own_block * 2
+    line = row_of(rep, own_block * 2)
     part = applied[0] * direction_out[pl.ds(line, 1), :] + applied[1] * direction_out[pl.ds(line + 1, 1), :]
     share[...] = jnp.broadcast_to(jnp.sum(part, axis=1, keepdims=True) / norm_next, share.shape)
-    lines = pl.ds(rep * PIECE + lax.rem(window // 2, 2), BLKS, stride=2)
-    message[...] = jnp.where(window < 4, charges_out[lines, :], direction_out[lines, :])
+    for core in range(2):
+        lines = pl.ds(row_of(rep, core * BLKS) + lax.rem(window // 2, 2), BLKS // 2, stride=2)
+        half = slice(core * BLKS // 2, core * BLKS // 2 + BLKS // 2)
+        message[half, :] = jnp.where(window < 4, charges_out[lines, :], direction_out[lines, :])
 
 
 def join_kernel(shares, message, out):
@@ -248,16 +285,18 @@
 
 def finish_kernel(parts, inputs, kinds, layer_charge, layer_mid, layer_out, charges_out, energies_out):
     frame = lax.axis_index("phase")
-    senders = LANES // WINDOW * 4
-    block = parts[pl.ds(pl.multiple_of(frame * senders, senders), senders), :]
+    block = parts[...]
     lane = lax.broadcasted_iota(jnp.int32, block.shape, 1) // WINDOW
-    sender = lax.broadcasted_iota(jnp.int32, block.shape, 0)
-    inside = lane == lax.rem(sender, 2)
+    place = lax.broadcasted_iota(jnp.int32, block.shape, 0)
+    solved = place // 4 % 4 == lax.rem(frame + 2, 4)
+    sender = place // 16 * 4 + place % 4
+    inside = lane == sender % 2
     lines = [
-        jnp.sum(jnp.where(inside & (sender // 2 == line), block, 0.0), axis=0, keepdims=True) for line in range(4)
+        jnp.sum(jnp.where(inside & solved & (sender // 2 == line), block, 0.0), axis=0, keepdims=True)
+        for line in range(4)
     ]
     step = LANES - WINDOW
-    step = step / total_of(jnp.where(inside, 0.0, block))
+    step = step / total_of(jnp.where(solved & ~inside, block, 0.0))
     charges = jnp.concatenate([lines[0] + step * lines[2], lines[1] + step * lines[3]], axis=1)
     charges_out[...] = charges
     outs = []
@@ -302,8 +341,7 @@
     widths,
     hardness,
 ):
-    block_axes = ("zq", "zr", "core")
-    cube_axes = ("rep", "phase", "zr", "core")
+    all_axes = ("phase", "zq", "zr", "core", "rep")
     piece = pltpu.VMEM((PIECE, OWN, LANES), float32)
     rows = pltpu.VMEM((5, OWN, LANES), float32)
     whole = shaped(ROWS, LANES)
@@ -311,7 +349,7 @@
 
     def exchange(message):
         sent = message.reshape(ROWS // 2, 2, LANES)
-        return lax.all_to_all(sent, cube_axes, 0, 0).reshape(ROWS, LANES)
+        return lax.all_to_all(sent, all_axes, 0, 0, axis_index_groups=cube_groups()).reshape(ROWS, LANES)
 
     def kept(pieces):
         return [pltpu.with_memory_space_constraint(one, pltpu.VMEM) for one in pieces]
@@ -331,15 +369,18 @@
         held + [pltpu.SemaphoreType.DMA((len(given),))],
         held=pl.BlockSpec(memory_space=pl.ANY),
     )(*[pltpu.with_memory_space_constraint(one, pltpu.HBM) for one in given])
-    atoms_own = lax.all_to_all(message, block_axes, 0, 0)
+    atoms_own = lax.all_to_all(message, all_axes, 0, 0, axis_index_groups=block_groups())
     parts = [
         lax.ppermute(atoms_own, "rep", [((rep + turn) % REPS, rep) for rep in range(REPS)]) for turn in range(1, REPS)
     ]
     own_piece, row_values = call(build_own_kernel, [piece, rows], "build_own", flops=10**9)(atoms_own, constants)
-    *rest, message, residual, groups, norm = call(
-        first_kernel, [piece] * 3 + [whole, whole, whole, small], "build_rest_and_begin"
-    )(atoms_own, *parts, *kept([row_values, own_piece]))
-    pieces = [own_piece] + rest
+    piece_1, piece_3 = call(build_kernel, [piece] * 2, "build_next", flops=2 * 10**9)(
+        parts[0], parts[2], *kept([row_values])
+    )
+    piece_2, message, residual, groups, norm = call(
+        first_kernel, [piece, whole, whole, whole, small], "build_rest_and_begin"
+    )(atoms_own, *parts, *kept([row_values, own_piece, piece_1, piece_3]))
+    pieces = [own_piece, piece_1, piece_2, piece_3]
     message, residual, direction, charges, norm = call(
         functools.partial(iterate_kernel, begun=0), [whole, whole, whole, whole, small], "iterate"
     )(exchange(message), residual, residual, groups, norm, *kept(pieces))
@@ -349,9 +390,12 @@
     share, message = call(
         last_kernel, [shaped(16, LANES), shaped(BLKS, LANES)], "last", [pltpu.VMEM((ROWS, LANES), float32)] * 3
     )(exchange(message), residual, direction, charges, groups, norm, *kept(pieces))
-    shares = lax.all_to_all(share.reshape(16, 1, LANES), ("phase", "rep"), 0, 0).reshape(16, LANES)
+    shares = lax.all_to_all(share.reshape(16, 1, LANES), all_axes, 0, 0, axis_index_groups=layer_groups())
+    shares = shares.reshape(16, LANES)
     message = call(join_kernel, shaped(BLKS, LANES), "join")(shares, message)
-    parts = lax.all_to_all(message.reshape(BLKS, 1, LANES), block_axes, 0, 0).reshape(BLKS, LANES)
+    parts = lax.all_to_all(
+        message.reshape(BLKS, 1, LANES), all_axes, 0, 0, axis_index_groups=block_groups()
+    ).reshape(BLKS, LANES)
     inputs = call(input_layer_kernel, shaped(ELEMS, short_bias.shape[1], OWN), "input_layer", flops=10**7)(
         descriptors, turned(short_input), short_bias
     )

time: 161 us -> 151 us (0.938)
  waiting for transfers between devices: 15.3 us -> 1.91 us
  starting transfers between devices: 16.1 us -> 25.2 us
  blocking collectives: 96.3 us -> 90.4 us
    all_to_all x1, waiting for transfers between devices: 11.6 us -> 1.9 us  [on_device(): lax.all_to_all(message.reshape(BLKS, 1, LANES), all_axes, 0, 0, axis_inde...]
    all_to_all x1, starting transfers between devices: 6.61 us -> 15.1 us  [on_device(): lax.all_to_all(message.reshape(BLKS, 1, LANES), all_axes, 0, 0, axis_inde...]
    all_to_all x5, blocking collectives: 96.3 us -> 90.4 us  [the longest x3 52 us: exchange(): lax.all_to_all(sent, all_axes, 0, 0, axis_index_groups=cube_groups())]
    ppermute x3, waiting for transfers between devices: 3.71 us -> 0.01 us  [on_device(): lax.ppermute(atoms_own, 'rep', [((rep + turn) % REPS, rep) for rep in ran...]
    pallas_call x9 -> x10, Pallas kernels: 32 us -> 32 us  [run(): pl.pallas_call(kernel, out_shape=outs, in_specs=[held] * len(args), out_s...]
  transfers between devices with their start and end apart: 4 -> 4, of which waited for: 2 -> 1; matrix products, arithmetic and copies ran while one was open for 0% -> 0% of each run, Pallas kernels for 3% -> 8%
where the time goes in v3:
time: 151 us; the launch traced here: 150 us
  blocking collectives  90.4 us (60%)
  Pallas kernels  32 us (21%)
  starting transfers between devices  25.2 us (17%)
  waiting for transfers between devices  1.91 us (1%)
    all_to_all x3, blocking collectives, exchange(): lax.all_to_all(sent, all_axes, 0, 0, axis_index_groups=cube_groups())  52 us
    pallas_call x10, Pallas kernels, run(): pl.pallas_call(kernel, out_shape=outs, in_specs=[held] * len(args), out_s...  32 us
    all_to_all x1, blocking collectives, on_device(): lax.all_to_all(message, all_axes, 0, 0, axis_index_groups=block_groups())  29.7 us
    all_to_all x1, starting transfers between devices, on_device(): lax.all_to_all(message.reshape(BLKS, 1, LANES), all_axes, 0, 0, axis_inde...  15.1 us
    ppermute x3, starting transfers between devices, on_device(): lax.ppermute(atoms_own, 'rep', [((rep + turn) % REPS, rep) for rep in ran...  10.1 us
    all_to_all x1, blocking collectives, on_device(): lax.all_to_all(share.reshape(16, 1, LANES), all_axes, 0, 0, axis_index_gr...  8.59 us
  transfers between devices with their start and end apart: 4, of which 1 were waited for; matrix products, arithmetic and copies ran while one was open for 0% of the time, Pallas kernels for 8%

profile of v3, /device:TPU:1, one launch (start us, length us, event | category | flops | bytes accessed | tf_op | source)
XLA Modules:
  0.0 150.3 jit_solution(3639813723270505325)
XLA Ops:
  0.6 1.7 %prepare.1 = (f32[32,3,4,128]{3,2,1,0:T(4,128)S(1)}, f32[8,128]{1,0:T(8,128)S(1)}) custom-call(f32[4,32,256]{2,1,0:T(8,128)} %features.1, f32[3,4,1024]{2,1,0:T(4,128)} %bitcast.32, s32[4,1024]{1,0:T(4,128)} %kinds.1, s32[4,256]{1,0:T(4,128)} %refs_3_.1, f32[15,2,32]{2,1,0:T(2,128)} %bitcast.33, f32[2,15]{1,0:T(2,128)} %refs_5_.1, f32[15,2,15]{2,1,0:T(2,128)} %bitcast.34, ...), custom_call_target="tpu_custom_call" | custom-call | tf_op jit(solution)/shard_map/prepare/pallas_call | solution.py:313
  2.3 29.7 %all_to_all.30.atoms.refs_0_ = f32[32,3,4,128]{3,2,1,0:T(4,128)S(1)} all-to-all(f32[32,3,4,128]{3,2,1,0:T(4,128)S(1)} %get-tuple-element.25), channel_id=1, replica_groups={{322,330,338,346,354,362,370,378,258,266,274,282,290,298,306,314,326,33..., dimensions={0} | all-to-all | bytes 393216 | tf_op jit(solution)/shard_map/all_to_all | solution.py:372
  32.0 4.6 %collective-permute-start = (f32[32,3,4,128]{3,2,1,0:T(4,128)S(1)}, f32[32,3,4,128]{3,2,1,0:T(4,128)S(1)}, u32[]{:S(2)}, u32[]{:S(2)}) collective-permute-start(f32[32,3,4,128]{3,2,1,0:T(4,128)S(1)} %all_to_all.30.atoms.refs_0_), channel_id=1, source_target_pairs={{1,0},{2,1},{3,2},{0,3},{5,4},{6,5},{7,6},{4,7},{9,8},{10,9},{11,1... | collective-permute-start | bytes 589832 | tf_op jit(solution)/shard_map/ppermute | solution.py:374
  36.7 1.9 %collective-permute-start.2 = (f32[32,3,4,128]{3,2,1,0:T(4,128)S(1)}, f32[32,3,4,128]{3,2,1,0:T(4,128)S(1)}, u32[]{:S(2)}, u32[]{:S(2)}) collective-permute-start(f32[32,3,4,128]{3,2,1,0:T(4,128)S(1)} %all_to_all.30.atoms.refs_0_), channel_id=1, source_target_pairs={{3,0},{0,1},{1,2},{2,3},{7,4},{4,5},{5,6},{6,7},{11,8},{8,9},{9,10... | collective-permute-start | bytes 589832 | tf_op jit(solution)/shard_map/ppermute | solution.py:374
  38.6 3.5 %collective-permute-start.1 = (f32[32,3,4,128]{3,2,1,0:T(4,128)S(1)}, f32[32,3,4,128]{3,2,1,0:T(4,128)S(1)}, u32[]{:S(2)}, u32[]{:S(2)}) collective-permute-start(f32[32,3,4,128]{3,2,1,0:T(4,128)S(1)} %all_to_all.30.atoms.refs_0_), channel_id=1, source_target_pairs={{2,0},{3,1},{0,2},{1,3},{6,4},{7,5},{4,6},{5,7},{10,8},{11,9},{8,1... | collective-permute-start | bytes 589832 | tf_op jit(solution)/shard_map/ppermute | solution.py:374
  42.2 4.4 %build_own.1 = (f32[64,256,128]{2,1,0:T(8,128)S(1)}, f32[5,256,128]{2,1,0:T(8,128)S(1)}) custom-call(f32[32,3,4,128]{3,2,1,0:T(4,128)S(1)} %all_to_all.30.atoms.refs_0_, f32[8,128]{1,0:T(8,128)S(1)} %get-tuple-element.26.constants), custom_call_target="tpu_custom_call" | custom-call | flops 1000000000 | tf_op jit(solution)/shard_map/build_own/pallas_call | solution.py:313
  46.6 0.0 collective-permute-done.part_1.refs_1_
  46.6 0.0 collective-permute-done.2.part_3.refs_3_
  46.6 8.2 %build_next.1 = (f32[64,256,128]{2,1,0:T(8,128)S(1)}, f32[64,256,128]{2,1,0:T(8,128)S(1)}) custom-call(f32[32,3,4,128]{3,2,1,0:T(4,128)S(1)} %collective-permute-done.part_1.refs_1_, f32[32,3,4,128]{3,2,1,0:T(4,128)S(1)} %collective-permute-done.2.part_3.refs_3_, f32[5,256,128]{2,1,0:T(8,128)S(1)} %get-tuple-element.27.rows.refs_4_), custom_call_target="tpu_custom_call" | custom-call | flops 2000000000 | tf_op jit(solution)/shard_map/build_next/pallas_call | solution.py:313
  54.8 0.0 collective-permute-done.1.refs_2_
  54.8 7.0 %build_rest_and_begin.1 = (f32[64,256,128]{2,1,0:T(8,128)S(1)}, f32[256,128]{1,0:T(8,128)S(1)}, f32[256,128]{1,0:T(8,128)S(1)}, f32[256,128]{1,0:T(8,128)S(1)}, f32[8,128]{1,0:T(8,128)S(1)}) custom-call(f32[32,3,4,128]{3,2,1,0:T(4,128)S(1)} %all_to_all.30.atoms.refs_0_, f32[32,3,4,128]{3,2,1,0:T(4,128)S(1)} %collective-permute-done.part_1.refs_1_, ...), custom_call_target="tpu_custom_call" | custom-call | tf_op jit(solution)/shard_map/build_rest_and_begin/pallas_call | solution.py:313
  61.8 20.2 %all_to_all.31 = f32[128,2,128]{2,1,0:T(2,128)S(1)} all-to-all(f32[128,2,128]{2,1,0:T(2,128)S(1)} %bitcast.24), channel_id=1, replica_groups={{282,274,266,258,410,402,394,386,26,18,10,2,154,146,138,130,283,275,267..., dimensions={0} | all-to-all | bytes 262144 | tf_op jit(solution)/shard_map/all_to_all | solution.py:352
  82.0 3.0 %iterate.2 = (f32[256,128]{1,0:T(8,128)S(1)}, f32[256,128]{1,0:T(8,128)S(1)}, f32[256,128]{1,0:T(8,128)S(1)}, f32[256,128]{1,0:T(8,128)S(1)}, f32[8,128]{1,0:T(8,128)S(1)}) custom-call(f32[256,128]{1,0:T(8,128)S(1)} %bitcast.23, f32[256,128]{1,0:T(8,128)S(1)} %get-tuple-element.32.refs_1_.refs_2_, f32[256,128]{1,0:T(8,128)S(1)} %get-tuple-element.32.refs_1_.refs_2_, ...), custom_call_target="tpu_custom_call" | custom-call | tf_op jit(solution)/shard_map/iterate/pallas_call | solution.py:313
  85.0 15.9 %all_to_all.32 = f32[128,2,128]{2,1,0:T(2,128)S(1)} all-to-all(f32[128,2,128]{2,1,0:T(2,128)S(1)} %bitcast.26), channel_id=1, replica_groups={{282,274,266,258,410,402,394,386,26,18,10,2,154,146,138,130,283,275,267..., dimensions={0} | all-to-all | bytes 262144 | tf_op jit(solution)/shard_map/all_to_all | solution.py:352
  100.9 3.0 %iterate.3 = (f32[256,128]{1,0:T(8,128)S(1)}, f32[256,128]{1,0:T(8,128)S(1)}, f32[256,128]{1,0:T(8,128)S(1)}, f32[256,128]{1,0:T(8,128)S(1)}, f32[8,128]{1,0:T(8,128)S(1)}) custom-call(f32[256,128]{1,0:T(8,128)S(1)} %bitcast.22, f32[256,128]{1,0:T(8,128)S(1)} %get-tuple-element.37.refs_1_, f32[256,128]{1,0:T(8,128)S(1)} %get-tuple-element.38.refs_2_, ...), custom_call_target="tpu_custom_call" | custom-call | tf_op jit(solution)/shard_map/iterate/pallas_call | solution.py:313
  103.9 15.9 %all_to_all.33 = f32[128,2,128]{2,1,0:T(2,128)S(1)} all-to-all(f32[128,2,128]{2,1,0:T(2,128)S(1)} %bitcast.25), channel_id=1, replica_groups={{282,274,266,258,410,402,394,386,26,18,10,2,154,146,138,130,283,275,267..., dimensions={0} | all-to-all | bytes 262144 | tf_op jit(solution)/shard_map/all_to_all | solution.py:352
  119.8 0.0 copy-start
  119.8 0.0 copy-start.3
  119.8 0.0 copy-start.4
  119.9 0.0 copy-start.1
  119.9 0.0 copy-start.2
  119.9 0.0 copy-start.5
  119.9 0.0 copy-start.6
  119.9 3.0 %last.1 = (f32[16,128]{1,0:T(8,128)S(1)}, f32[32,128]{1,0:T(8,128)S(1)}) custom-call(f32[256,128]{1,0:T(8,128)S(1)} %bitcast.21, f32[256,128]{1,0:T(8,128)S(1)} %get-tuple-element.42.residual, f32[256,128]{1,0:T(8,128)S(1)} %get-tuple-element.43.direction, f32[256,128]{1,0:T(8,128)S(1)} %get-tuple-element.44.charges, ...), custom_call_target="tpu_custom_call" | custom-call | tf_op jit(solution)/shard_map/last/pallas_call | solution.py:313
  122.9 8.6 %all_to_all.34 = f32[16,1,128]{2,1,0:T(1,128)S(1)} all-to-all(f32[16,1,128]{2,1,0:T(1,128)S(1)} %bitcast.31), channel_id=1, replica_groups={{258,259,256,257,386,387,384,385,2,3,0,1,130,131,128,129},{262,263,260,..., dimensions={0} | all-to-all | bytes 16384 | tf_op jit(solution)/shard_map/all_to_all | solution.py:393
  131.5 0.7 join.1
  132.2 15.1 %all-to-all-start.5 = ((f32[32,1,128]{2,1,0:T(1,128)}), f32[32,1,128]{2,1,0:T(1,128)S(1)}, u32[]{:S(2)}, u32[]{:S(2)}) async-start(f32[32,1,128]{2,1,0:T(1,128)} %bitcast.15), calls=%async_computation.5 | async-start | bytes 32768 | tf_op jit(solution)/shard_map/all_to_all | solution.py:396
  147.3 0.0 copy-done
  147.3 0.0 copy-done.3
  147.4 0.0 copy-done.4
  147.4 0.1 input_layer.1.inputs
  147.5 1.9 %all-to-all-done.5 = f32[32,1,128]{2,1,0:T(1,128)S(1)} async-done(((f32[32,1,128]{2,1,0:T(1,128)}), f32[32,1,128]{2,1,0:T(1,128)S(1)}, u32[]{:S(2)}, u32[]{:S(2)}) %all-to-all-start.5) | async-done | bytes 16416 | tf_op jit(solution)/shard_map/all_to_all | solution.py:396
  149.4 0.0 copy-done.1
  149.4 0.0 copy-done.2
  149.4 0.0 copy-done.5
  149.4 0.0 copy-done.6
  149.4 0.9 finish.1
Async XLA Ops:
  32.0 14.5 %collective-permute-start = (f32[32,3,4,128]{3,2,1,0:T(4,128)S(1)}, f32[32,3,4,128]{3,2,1,0:T(4,128)S(1)}, u32[]{:S(2)}, u32[]{:S(2)}) collective-permute-start(f32[32,3,4,128]{3,2,1,0:T(4,128)S(1)} %all_to_all.30.atoms.refs_0_), channel_id=1, source_target_pairs={{1,0},{2,1},{3,2},{0,3},{5,4},{6,5},{7,6},{4,7},{9,8},{10,9},{11,1... | collective-permute-start | bytes 589832 | tf_op jit(solution)/shard_map/ppermute | solution.py:374
  36.7 9.9 %collective-permute-start.2 = (f32[32,3,4,128]{3,2,1,0:T(4,128)S(1)}, f32[32,3,4,128]{3,2,1,0:T(4,128)S(1)}, u32[]{:S(2)}, u32[]{:S(2)}) collective-permute-start(f32[32,3,4,128]{3,2,1,0:T(4,128)S(1)} %all_to_all.30.atoms.refs_0_), channel_id=1, source_target_pairs={{3,0},{0,1},{1,2},{2,3},{7,4},{4,5},{5,6},{6,7},{11,8},{8,9},{9,10... | collective-permute-start | bytes 589832 | tf_op jit(solution)/shard_map/ppermute | solution.py:374
  38.6 16.2 %collective-permute-start.1 = (f32[32,3,4,128]{3,2,1,0:T(4,128)S(1)}, f32[32,3,4,128]{3,2,1,0:T(4,128)S(1)}, u32[]{:S(2)}, u32[]{:S(2)}) collective-permute-start(f32[32,3,4,128]{3,2,1,0:T(4,128)S(1)} %all_to_all.30.atoms.refs_0_), channel_id=1, source_target_pairs={{2,0},{3,1},{0,2},{1,3},{6,4},{7,5},{4,6},{5,7},{10,8},{11,9},{8,1... | collective-permute-start | bytes 589832 | tf_op jit(solution)/shard_map/ppermute | solution.py:374
  119.8 27.5 %copy-start = (f32[4,32,256]{2,1,0:T(8,128)S(1)}, f32[4,32,256]{2,1,0:T(8,128)}, u32[]{:S(2)}) copy-start(f32[4,32,256]{2,1,0:T(8,128)} %features.1) | copy-start | bytes 393220
  119.8 27.5 %copy-start.3 = (f32[2,15,32]{2,0,1:T(2,128)S(1)}, f32[2,15,32]{2,0,1:T(2,128)}, u32[]{:S(2)}) copy-start(f32[2,15,32]{2,0,1:T(2,128)} %param.23) | copy-start | bytes 11524
  119.8 27.5 %copy-start.4 = (f32[2,15]{1,0:T(2,128)S(1)}, f32[2,15]{1,0:T(2,128)}, u32[]{:S(2)}) copy-start(f32[2,15]{1,0:T(2,128)} %layer_bias.1) | copy-start | bytes 364
  119.9 29.6 %copy-start.1 = (s32[4,1024]{1,0:T(4,128)S(1)}, s32[4,1024]{1,0:T(4,128)}, u32[]{:S(2)}) copy-start(s32[4,1024]{1,0:T(4,128)} %kinds.1) | copy-start | bytes 49156
  119.9 29.6 %copy-start.2 = (f32[2,15,15]{2,0,1:T(2,128)S(1)}, f32[2,15,15]{2,0,1:T(2,128)}, u32[]{:S(2)}) copy-start(f32[2,15,15]{2,0,1:T(2,128)} %param.26) | copy-start | bytes 5404
  119.9 29.5 %copy-start.5 = (f32[2,15]{1,0:T(2,128)S(1)}, f32[2,15]{1,0:T(2,128)}, u32[]{:S(2)}) copy-start(f32[2,15]{1,0:T(2,128)} %layer_charge.1) | copy-start | bytes 364
  119.9 29.5 %copy-start.6 = (f32[2,15]{1,0:T(2,128)S(1)}, f32[2,15]{1,0:T(2,128)}, u32[]{:S(2)}) copy-start(f32[2,15]{1,0:T(2,128)} %layer_out.1) | copy-start | bytes 364
  132.2 17.2 %all-to-all-start.5 = ((f32[32,1,128]{2,1,0:T(1,128)}), f32[32,1,128]{2,1,0:T(1,128)S(1)}, u32[]{:S(2)}, u32[]{:S(2)}) async-start(f32[32,1,128]{2,1,0:T(1,128)} %bitcast.15), calls=%async_computation.5 | async-start | bytes 32768 | tf_op jit(solution)/shard_map/all_to_all | solution.py:396

commit v4 on v3

--- a/solution.py
+++ b/solution.py
@@ -103,27 +103,30 @@
         source = source.at[:, :, own] if index == 1 else source.at[:, own] if index == 2 else source
         copies.append(pltpu.make_async_copy(source, target, arrived.at[index]))
         copies[-1].start()
-    for copy in copies:
+    features, coords, kinds, groups, layer_in, layer_bias, layer_mid, layer_out, widths, hardness = held
+    frames = features.shape[0]
+
+    def send(frame, pair, one, two):
+        block = jnp.concatenate([one[:, :LANES], one[:, LANES:], two[:, :LANES], two[:, LANES:]], axis=0)
+        for target in range(BLKS // frames):
+            message[target // 4 * 16 + (frame + 2) % 4 * 4 + target % 4, pair] = block
+
+    for copy in copies[1:]:
         copy.wait()
-    features, coords, kinds, groups, layer_in, layer_bias, layer_mid, layer_out, widths, hardness = held
+    for frame in range(frames):
+        send(frame, 0, coords[0, frame : frame + 1, :], coords[1, frame : frame + 1, :])
+        send(frame, 1, coords[2, frame : frame + 1, :], kinds[frame : frame + 1, :].astype(float32))
     for line, source in enumerate((widths, hardness)):
         for kind in range(ELEMS):
             row = jnp.broadcast_to(source[0:1, kind : kind + 1], (1, LANES))
             constants[2 * line + kind : 2 * line + kind + 1, :] = row
-    frames = features.shape[0]
+    copies[0].wait()
     wide = jnp.concatenate([features[frame] for frame in range(frames)], axis=1)
     first, second = network(layer_in, layer_bias, layer_mid, layer_out, wide)
     for frame in range(frames):
         span = slice(frame * OWN, frame * OWN + OWN)
-        kind = kinds[frame : frame + 1, :]
-        electroneg = jnp.where(kind == 1, second[:, span], first[:, span])
-        values = [coords[axis, frame : frame + 1, :] for axis in range(3)]
-        values += [kind.astype(float32), electroneg, groups[frame : frame + 1, :].astype(float32)]
-        for pair in range(3):
-            one, two = values[2 * pair], values[2 * pair + 1]
-            block = jnp.concatenate([one[:, :LANES], one[:, LANES:], two[:, :LANES], two[:, LANES:]], axis=0)
-            for target in range(BLKS // frames):
-                message[target // 4 * 16 + (frame + 2) % 4 * 4 + target % 4, pair] = block
+        electroneg = jnp.where(kinds[frame : frame + 1, :] == 1, second[:, span], first[:, span])
+        send(frame, 2, electroneg, groups[frame : frame + 1, :].astype(float32))
 
 
 def fill_rows(atoms, own_block, constants, rows):
@@ -210,15 +213,15 @@
     return vector - taken
 
 
-def build_kernel(part_1, part_3, rows, piece_1, piece_3):
+def build_kernel(part_1, rows, piece_1):
     build_piece(part_1, rows, piece_1)
-    build_piece(part_3, rows, piece_3)
 
 
 def first_kernel(*refs):
     parts, (rows, own_piece, piece_1, piece_3, piece_2) = refs[:4], refs[4:9]
     message, residual, groups, norm = refs[9:]
     rep, _, _ = place_of()
+    build_piece(parts[3], rows, piece_3)
     build_piece(parts[2], rows, piece_2)
     for turn, part in enumerate(parts):
         source = lax.rem(rep + turn, REPS)
@@ -374,12 +377,10 @@
         lax.ppermute(atoms_own, "rep", [((rep + turn) % REPS, rep) for rep in range(REPS)]) for turn in range(1, REPS)
     ]
     own_piece, row_values = call(build_own_kernel, [piece, rows], "build_own", flops=10**9)(atoms_own, constants)
-    piece_1, piece_3 = call(build_kernel, [piece] * 2, "build_next", flops=2 * 10**9)(
-        parts[0], parts[2], *kept([row_values])
-    )
-    piece_2, message, residual, groups, norm = call(
-        first_kernel, [piece, whole, whole, whole, small], "build_rest_and_begin"
-    )(atoms_own, *parts, *kept([row_values, own_piece, piece_1, piece_3]))
+    piece_1 = call(build_kernel, piece, "build_next", flops=10**9)(parts[0], *kept([row_values]))
+    piece_3, piece_2, message, residual, groups, norm = call(
+        first_kernel, [piece, piece, whole, whole, whole, small], "build_rest_and_begin"
+    )(atoms_own, *parts, *kept([row_values, own_piece, piece_1]))
     pieces = [own_piece, piece_1, piece_2, piece_3]
     message, residual, direction, charges, norm = call(
         functools.partial(iterate_kernel, begun=0), [whole, whole, whole, whole, small], "iterate"

time: 151 us -> 147 us (0.974)
  blocking collectives: 90.4 us -> 86.7 us
    all_to_all x3, blocking collectives: 52 us -> 48.3 us  [exchange(): lax.all_to_all(sent, all_axes, 0, 0, axis_index_groups=cube_groups())]
  transfers between devices with their start and end apart: 4 -> 4, of which waited for: 1 -> 2; matrix products, arithmetic and copies ran while one was open for 0% -> 0% of each run, Pallas kernels for 8% -> 6%
where the time goes in v4:
time: 147 us
  blocking collectives  86.7 us (59%)
  Pallas kernels  32 us (22%)
  starting transfers between devices  24.2 us (16%)
  waiting for transfers between devices  2.82 us (2%)
    all_to_all x3, blocking collectives, exchange(): lax.all_to_all(sent, all_axes, 0, 0, axis_index_groups=cube_groups())  48.3 us
    pallas_call x10, Pallas kernels, run(): pl.pallas_call(kernel, out_shape=outs, in_specs=[held] * len(args), out_s...  32 us
    all_to_all x1, blocking collectives, on_device(): lax.all_to_all(message, all_axes, 0, 0, axis_index_groups=block_groups())  29.7 us
    all_to_all x1, starting transfers between devices, on_device(): lax.all_to_all(message.reshape(BLKS, 1, LANES), all_axes, 0, 0, axis_inde...  14.7 us
    ppermute x3, starting transfers between devices, on_device(): lax.ppermute(atoms_own, 'rep', [((rep + turn) % REPS, rep) for rep in ran...  9.48 us
    all_to_all x1, blocking collectives, on_device(): lax.all_to_all(share.reshape(16, 1, LANES), all_axes, 0, 0, axis_index_gr...  8.59 us
  transfers between devices with their start and end apart: 4, of which 2 were waited for; matrix products, arithmetic and copies ran while one was open for 0% of the time, Pallas kernels for 6%

profile of v4, /device:TPU:1, one launch (start us, length us, event | category | flops | bytes accessed | tf_op | source)
XLA Modules:
  0.0 146.5 jit_solution(14836879106935807379)
XLA Ops:
  0.6 1.7 %prepare.1 = (f32[32,3,4,128]{3,2,1,0:T(4,128)S(1)}, f32[8,128]{1,0:T(8,128)S(1)}) custom-call(f32[4,32,256]{2,1,0:T(8,128)} %features.1, f32[3,4,1024]{2,1,0:T(4,128)} %bitcast.32, s32[4,1024]{1,0:T(4,128)} %kinds.1, s32[4,256]{1,0:T(4,128)} %refs_3_.1, f32[15,2,32]{2,1,0:T(2,128)} %bitcast.33, f32[2,15]{1,0:T(2,128)} %refs_5_.1, f32[15,2,15]{2,1,0:T(2,128)} %bitcast.34, ...), custom_call_target="tpu_custom_call" | custom-call | tf_op jit(solution)/shard_map/prepare/pallas_call | solution.py:316
  2.3 29.7 %all_to_all.30.atoms.refs_0_ = f32[32,3,4,128]{3,2,1,0:T(4,128)S(1)} all-to-all(f32[32,3,4,128]{3,2,1,0:T(4,128)S(1)} %get-tuple-element.24), channel_id=1, replica_groups={{322,330,338,346,354,362,370,378,258,266,274,282,290,298,306,314,326,33..., dimensions={0} | all-to-all | bytes 393216 | tf_op jit(solution)/shard_map/all_to_all | solution.py:375
  32.1 4.6 %collective-permute-start = (f32[32,3,4,128]{3,2,1,0:T(4,128)S(1)}, f32[32,3,4,128]{3,2,1,0:T(4,128)S(1)}, u32[]{:S(2)}, u32[]{:S(2)}) collective-permute-start(f32[32,3,4,128]{3,2,1,0:T(4,128)S(1)} %all_to_all.30.atoms.refs_0_), channel_id=1, source_target_pairs={{1,0},{2,1},{3,2},{0,3},{5,4},{6,5},{7,6},{4,7},{9,8},{10,9},{11,1... | collective-permute-start | bytes 589832 | tf_op jit(solution)/shard_map/ppermute | solution.py:377
  36.7 2.3 %collective-permute-start.1 = (f32[32,3,4,128]{3,2,1,0:T(4,128)S(1)}, f32[32,3,4,128]{3,2,1,0:T(4,128)S(1)}, u32[]{:S(2)}, u32[]{:S(2)}) collective-permute-start(f32[32,3,4,128]{3,2,1,0:T(4,128)S(1)} %all_to_all.30.atoms.refs_0_), channel_id=1, source_target_pairs={{2,0},{3,1},{0,2},{1,3},{6,4},{7,5},{4,6},{5,7},{10,8},{11,9},{8,1... | collective-permute-start | bytes 589832 | tf_op jit(solution)/shard_map/ppermute | solution.py:377
  39.0 2.6 %collective-permute-start.2 = (f32[32,3,4,128]{3,2,1,0:T(4,128)S(1)}, f32[32,3,4,128]{3,2,1,0:T(4,128)S(1)}, u32[]{:S(2)}, u32[]{:S(2)}) collective-permute-start(f32[32,3,4,128]{3,2,1,0:T(4,128)S(1)} %all_to_all.30.atoms.refs_0_), channel_id=1, source_target_pairs={{3,0},{0,1},{1,2},{2,3},{7,4},{4,5},{5,6},{6,7},{11,8},{8,9},{9,10... | collective-permute-start | bytes 589832 | tf_op jit(solution)/shard_map/ppermute | solution.py:377
  41.6 4.4 %build_own.1 = (f32[64,256,128]{2,1,0:T(8,128)S(1)}, f32[5,256,128]{2,1,0:T(8,128)S(1)}) custom-call(f32[32,3,4,128]{3,2,1,0:T(4,128)S(1)} %all_to_all.30.atoms.refs_0_, f32[8,128]{1,0:T(8,128)S(1)} %get-tuple-element.25.constants), custom_call_target="tpu_custom_call" | custom-call | flops 1000000000 | tf_op jit(solution)/shard_map/build_own/pallas_call | solution.py:316
  46.0 0.0 collective-permute-done.part_1.refs_1_
  46.0 4.1 %build_next.1.refs_6_.refs_7_.piece_1 = f32[64,256,128]{2,1,0:T(8,128)S(1)} custom-call(f32[32,3,4,128]{3,2,1,0:T(4,128)S(1)} %collective-permute-done.part_1.refs_1_, f32[5,256,128]{2,1,0:T(8,128)S(1)} %get-tuple-element.26.rows.refs_4_), custom_call_target="tpu_custom_call" | custom-call | flops 1000000000 | tf_op jit(solution)/shard_map/build_next/pallas_call | solution.py:316
  50.1 0.0 collective-permute-done.1.refs_2_
  50.1 0.9 collective-permute-done.2.refs_3_
  51.0 11.1 %build_rest_and_begin.1 = (f32[64,256,128]{2,1,0:T(8,128)S(1)}, f32[64,256,128]{2,1,0:T(8,128)S(1)}, f32[256,128]{1,0:T(8,128)S(1)}, f32[256,128]{1,0:T(8,128)S(...) custom-call(f32[32,3,4,128]{3,2,1,0:T(4,128)S(1)} %all_to_all.30.atoms.refs_0_, ...), custom_call_target="tpu_custom_call" | custom-call | tf_op jit(solution)/shard_map/build_rest_and_begin/pallas_call | solution.py:316
  62.1 16.5 %all_to_all.31 = f32[128,2,128]{2,1,0:T(2,128)S(1)} all-to-all(f32[128,2,128]{2,1,0:T(2,128)S(1)} %bitcast.24), channel_id=1, replica_groups={{282,274,266,258,410,402,394,386,26,18,10,2,154,146,138,130,283,275,267..., dimensions={0} | all-to-all | bytes 262144 | tf_op jit(solution)/shard_map/all_to_all | solution.py:355
  78.7 3.0 %iterate.2 = (f32[256,128]{1,0:T(8,128)S(1)}, f32[256,128]{1,0:T(8,128)S(1)}, f32[256,128]{1,0:T(8,128)S(1)}, f32[256,128]{1,0:T(8,128)S(1)}, f32[8,128]{1,0:T(8,128)S(1)}) custom-call(f32[256,128]{1,0:T(8,128)S(1)} %bitcast.23, f32[256,128]{1,0:T(8,128)S(1)} %get-tuple-element.29.refs_1_.refs_2_, f32[256,128]{1,0:T(8,128)S(1)} %get-tuple-element.29.refs_1_.refs_2_, ...), custom_call_target="tpu_custom_call" | custom-call | tf_op jit(solution)/shard_map/iterate/pallas_call | solution.py:316
  81.7 15.9 %all_to_all.32 = f32[128,2,128]{2,1,0:T(2,128)S(1)} all-to-all(f32[128,2,128]{2,1,0:T(2,128)S(1)} %bitcast.26), channel_id=1, replica_groups={{282,274,266,258,410,402,394,386,26,18,10,2,154,146,138,130,283,275,267..., dimensions={0} | all-to-all | bytes 262144 | tf_op jit(solution)/shard_map/all_to_all | solution.py:355
  97.6 3.0 %iterate.3 = (f32[256,128]{1,0:T(8,128)S(1)}, f32[256,128]{1,0:T(8,128)S(1)}, f32[256,128]{1,0:T(8,128)S(1)}, f32[256,128]{1,0:T(8,128)S(1)}, f32[8,128]{1,0:T(8,128)S(1)}) custom-call(f32[256,128]{1,0:T(8,128)S(1)} %bitcast.22, f32[256,128]{1,0:T(8,128)S(1)} %get-tuple-element.35.refs_1_, f32[256,128]{1,0:T(8,128)S(1)} %get-tuple-element.36.refs_2_, ...), custom_call_target="tpu_custom_call" | custom-call | tf_op jit(solution)/shard_map/iterate/pallas_call | solution.py:316
  100.6 15.9 %all_to_all.33 = f32[128,2,128]{2,1,0:T(2,128)S(1)} all-to-all(f32[128,2,128]{2,1,0:T(2,128)S(1)} %bitcast.25), channel_id=1, replica_groups={{282,274,266,258,410,402,394,386,26,18,10,2,154,146,138,130,283,275,267..., dimensions={0} | all-to-all | bytes 262144 | tf_op jit(solution)/shard_map/all_to_all | solution.py:355
  116.5 0.0 copy-start
  116.5 0.0 copy-start.3
  116.5 0.0 copy-start.4
  116.5 0.0 copy-start.1
  116.5 0.0 copy-start.2
  116.5 0.0 copy-start.5
  116.5 0.0 copy-start.6
  116.5 3.0 %last.1 = (f32[16,128]{1,0:T(8,128)S(1)}, f32[32,128]{1,0:T(8,128)S(1)}) custom-call(f32[256,128]{1,0:T(8,128)S(1)} %bitcast.21, f32[256,128]{1,0:T(8,128)S(1)} %get-tuple-element.40.residual, f32[256,128]{1,0:T(8,128)S(1)} %get-tuple-element.41.direction, f32[256,128]{1,0:T(8,128)S(1)} %get-tuple-element.42.charges, ...), custom_call_target="tpu_custom_call" | custom-call | tf_op jit(solution)/shard_map/last/pallas_call | solution.py:316
  119.5 8.6 %all_to_all.34 = f32[16,1,128]{2,1,0:T(1,128)S(1)} all-to-all(f32[16,1,128]{2,1,0:T(1,128)S(1)} %bitcast.31), channel_id=1, replica_groups={{258,259,256,257,386,387,384,385,2,3,0,1,130,131,128,129},{262,263,260,..., dimensions={0} | all-to-all | bytes 16384 | tf_op jit(solution)/shard_map/all_to_all | solution.py:394
  128.1 0.7 join.1
  128.8 14.7 %all-to-all-start.5 = ((f32[32,1,128]{2,1,0:T(1,128)}), f32[32,1,128]{2,1,0:T(1,128)S(1)}, u32[]{:S(2)}, u32[]{:S(2)}) async-start(f32[32,1,128]{2,1,0:T(1,128)} %bitcast.15), calls=%async_computation.5 | async-start | bytes 32768 | tf_op jit(solution)/shard_map/all_to_all | solution.py:397
  143.6 0.0 copy-done
  143.6 0.0 copy-done.3
  143.6 0.0 copy-done.4
  143.6 0.1 input_layer.1.inputs
  143.7 1.9 %all-to-all-done.5 = f32[32,1,128]{2,1,0:T(1,128)S(1)} async-done(((f32[32,1,128]{2,1,0:T(1,128)}), f32[32,1,128]{2,1,0:T(1,128)S(1)}, u32[]{:S(2)}, u32[]{:S(2)}) %all-to-all-start.5) | async-done | bytes 16416 | tf_op jit(solution)/shard_map/all_to_all | solution.py:397
  145.6 0.0 copy-done.1
  145.6 0.0 copy-done.2
  145.6 0.0 copy-done.5
  145.6 0.0 copy-done.6
  145.6 0.9 finish.1
Async XLA Ops:
  32.1 13.9 %collective-permute-start = (f32[32,3,4,128]{3,2,1,0:T(4,128)S(1)}, f32[32,3,4,128]{3,2,1,0:T(4,128)S(1)}, u32[]{:S(2)}, u32[]{:S(2)}) collective-permute-start(f32[32,3,4,128]{3,2,1,0:T(4,128)S(1)} %all_to_all.30.atoms.refs_0_), channel_id=1, source_target_pairs={{1,0},{2,1},{3,2},{0,3},{5,4},{6,5},{7,6},{4,7},{9,8},{10,9},{11,1... | collective-permute-start | bytes 589832 | tf_op jit(solution)/shard_map/ppermute | solution.py:377
  36.7 13.4 %collective-permute-start.1 = (f32[32,3,4,128]{3,2,1,0:T(4,128)S(1)}, f32[32,3,4,128]{3,2,1,0:T(4,128)S(1)}, u32[]{:S(2)}, u32[]{:S(2)}) collective-permute-start(f32[32,3,4,128]{3,2,1,0:T(4,128)S(1)} %all_to_all.30.atoms.refs_0_), channel_id=1, source_target_pairs={{2,0},{3,1},{0,2},{1,3},{6,4},{7,5},{4,6},{5,7},{10,8},{11,9},{8,1... | collective-permute-start | bytes 589832 | tf_op jit(solution)/shard_map/ppermute | solution.py:377
  39.0 12.0 %collective-permute-start.2 = (f32[32,3,4,128]{3,2,1,0:T(4,128)S(1)}, f32[32,3,4,128]{3,2,1,0:T(4,128)S(1)}, u32[]{:S(2)}, u32[]{:S(2)}) collective-permute-start(f32[32,3,4,128]{3,2,1,0:T(4,128)S(1)} %all_to_all.30.atoms.refs_0_), channel_id=1, source_target_pairs={{3,0},{0,1},{1,2},{2,3},{7,4},{4,5},{5,6},{6,7},{11,8},{8,9},{9,10... | collective-permute-start | bytes 589832 | tf_op jit(solution)/shard_map/ppermute | solution.py:377
  116.5 27.1 %copy-start = (f32[4,32,256]{2,1,0:T(8,128)S(1)}, f32[4,32,256]{2,1,0:T(8,128)}, u32[]{:S(2)}) copy-start(f32[4,32,256]{2,1,0:T(8,128)} %features.1) | copy-start | bytes 393220
  116.5 27.1 %copy-start.3 = (f32[2,15,32]{2,0,1:T(2,128)S(1)}, f32[2,15,32]{2,0,1:T(2,128)}, u32[]{:S(2)}) copy-start(f32[2,15,32]{2,0,1:T(2,128)} %param.23) | copy-start | bytes 11524
  116.5 27.1 %copy-start.4 = (f32[2,15]{1,0:T(2,128)S(1)}, f32[2,15]{1,0:T(2,128)}, u32[]{:S(2)}) copy-start(f32[2,15]{1,0:T(2,128)} %layer_bias.1) | copy-start | bytes 364
  116.5 29.2 %copy-start.1 = (s32[4,1024]{1,0:T(4,128)S(1)}, s32[4,1024]{1,0:T(4,128)}, u32[]{:S(2)}) copy-start(s32[4,1024]{1,0:T(4,128)} %kinds.1) | copy-start | bytes 49156
  116.5 29.2 %copy-start.2 = (f32[2,15,15]{2,0,1:T(2,128)S(1)}, f32[2,15,15]{2,0,1:T(2,128)}, u32[]{:S(2)}) copy-start(f32[2,15,15]{2,0,1:T(2,128)} %param.26) | copy-start | bytes 5404
  116.5 29.1 %copy-start.5 = (f32[2,15]{1,0:T(2,128)S(1)}, f32[2,15]{1,0:T(2,128)}, u32[]{:S(2)}) copy-start(f32[2,15]{1,0:T(2,128)} %layer_charge.1) | copy-start | bytes 364
  116.5 29.1 %copy-start.6 = (f32[2,15]{1,0:T(2,128)S(1)}, f32[2,15]{1,0:T(2,128)}, u32[]{:S(2)}) copy-start(f32[2,15]{1,0:T(2,128)} %layer_out.1) | copy-start | bytes 364
  128.8 16.8 %all-to-all-start.5 = ((f32[32,1,128]{2,1,0:T(1,128)}), f32[32,1,128]{2,1,0:T(1,128)S(1)}, u32[]{:S(2)}, u32[]{:S(2)}) async-start(f32[32,1,128]{2,1,0:T(1,128)} %bitcast.15), calls=%async_computation.5 | async-start | bytes 32768 | tf_op jit(solution)/shard_map/all_to_all | solution.py:397

commit v5 on v4

--- a/solution.py
+++ b/solution.py
@@ -160,7 +160,7 @@
                 piece[2 * block + half, span, :] = lax.erf(squared * inverse * scale) * inverse
         return carry
 
-    lax.fori_loop(0, BLKS, one_block, 0, unroll=2)
+    lax.fori_loop(0, BLKS, one_block, 0, unroll=4)
 
 
 def build_own_kernel(atoms, constants, piece, rows):
@@ -180,7 +180,7 @@
     sums = tuple(jnp.zeros((8, LANES), float32) for _ in range(GROUPS))
     for turn, piece in enumerate(pieces):
         for core in range(2):
-            first = row_of(lax.rem(rep + turn, REPS), core * BLKS)
+            first = row_of(rep ^ turn, core * BLKS)
 
             def one_line(line, sums, core=core, piece=piece, first=first):
                 values = jnp.broadcast_to(direction[pl.ds(first + line, 1), :], (8, LANES))
@@ -224,7 +224,7 @@
     build_piece(parts[3], rows, piece_3)
     build_piece(parts[2], rows, piece_2)
     for turn, part in enumerate(parts):
-        source = lax.rem(rep + turn, REPS)
+        source = rep ^ turn
         for block in range(BLKS):
             lines = pl.ds(row_of(source, block * 2), 2)
             residual[lines, :] = part[block, 2, 0:2, :]
@@ -279,15 +279,15 @@
     out[...] = jnp.where(lane // WINDOW == lax.rem(window, 2), message[...], total_of(shares[:, 0:1]))
 
 
-def input_layer_kernel(features, layer_in, layer_bias, out):
+def finish_kernel(
+    parts, features, kinds, layer_in, layer_charge, layer_bias, layer_mid, layer_out, charges_out, energies_out
+):
     frame = lax.axis_index("phase")
-    for kind in range(ELEMS):
-        product = jnp.dot(layer_in[:, kind, :], features[frame], precision=highest, preferred_element_type=float32)
-        out[kind] = product + as_column(layer_bias[kind : kind + 1, :])
-
-
-def finish_kernel(parts, inputs, kinds, layer_charge, layer_mid, layer_out, charges_out, energies_out):
-    frame = lax.axis_index("phase")
+    inputs = [
+        jnp.dot(layer_in[:, kind, :], features[frame], precision=highest, preferred_element_type=float32)
+        + as_column(layer_bias[kind : kind + 1, :])
+        for kind in range(ELEMS)
+    ]
     block = parts[...]
     lane = lax.broadcasted_iota(jnp.int32, block.shape, 1) // WINDOW
     place = lax.broadcasted_iota(jnp.int32, block.shape, 0)
@@ -374,7 +374,7 @@
     )(*[pltpu.with_memory_space_constraint(one, pltpu.HBM) for one in given])
     atoms_own = lax.all_to_all(message, all_axes, 0, 0, axis_index_groups=block_groups())
     parts = [
-        lax.ppermute(atoms_own, "rep", [((rep + turn) % REPS, rep) for rep in range(REPS)]) for turn in range(1, REPS)
+        lax.ppermute(atoms_own, "rep", [(rep ^ turn, rep) for rep in range(REPS)]) for turn in range(1, REPS)
     ]
     own_piece, row_values = call(build_own_kernel, [piece, rows], "build_own", flops=10**9)(atoms_own, constants)
     piece_1 = call(build_kernel, piece, "build_next", flops=10**9)(parts[0], *kept([row_values]))
@@ -397,11 +397,15 @@
     parts = lax.all_to_all(
         message.reshape(BLKS, 1, LANES), all_axes, 0, 0, axis_index_groups=block_groups()
     ).reshape(BLKS, LANES)
-    inputs = call(input_layer_kernel, shaped(ELEMS, short_bias.shape[1], OWN), "input_layer", flops=10**7)(
-        descriptors, turned(short_input), short_bias
-    )
     return call(finish_kernel, [shaped(1, OWN), shaped(1, OWN)], "finish")(
-        parts, inputs, elements, short_charge, turned(short_hidden), short_output
+        parts,
+        descriptors,
+        elements,
+        turned(short_input),
+        short_charge,
+        short_bias,
+        turned(short_hidden),
+        short_output,
     )
 
 

time: 147 us -> 145 us (0.986)
  blocking collectives: 86.7 us -> 103 us
  starting transfers between devices: 24.2 us -> 9.63 us
  waiting for transfers between devices: 2.82 us -> 0.01 us
    all_to_all x0 -> x1, blocking collectives: none -> 15.7 us  [on_device(): lax.all_to_all(message.reshape(BLKS, 1, LANES), all_axes, 0, 0, axis_inde...]
    all_to_all x1 -> x0, starting transfers between devices: 14.7 us -> none  [on_device(): lax.all_to_all(message.reshape(BLKS, 1, LANES), all_axes, 0, 0, axis_inde...]
    all_to_all x1 -> x0, waiting for transfers between devices: 1.91 us -> none  [on_device(): lax.all_to_all(message.reshape(BLKS, 1, LANES), all_axes, 0, 0, axis_inde...]
    pallas_call x10 -> x9, Pallas kernels: 32 us -> 30.7 us  [run(): pl.pallas_call(kernel, out_shape=outs, in_specs=[held] * len(args), out_s...]
  transfers between devices with their start and end apart: 4 -> 3, of which waited for: 2 -> 0; matrix products, arithmetic and copies ran while one was open for 0% -> 0% of each run, Pallas kernels for 6% -> 6%
where the time goes in v5:
time: 145 us
  blocking collectives  103 us (71%)
  Pallas kernels  30.7 us (21%)
  starting transfers between devices  9.63 us (7%)
    all_to_all x3, blocking collectives, exchange(): lax.all_to_all(sent, all_axes, 0, 0, axis_index_groups=cube_groups())  49.4 us
    pallas_call x9, Pallas kernels, run(): pl.pallas_call(kernel, out_shape=outs, in_specs=[held] * len(args), out_s...  30.7 us
    all_to_all x1, blocking collectives, on_device(): lax.all_to_all(message, all_axes, 0, 0, axis_index_groups=block_groups())  29.7 us
    all_to_all x1, blocking collectives, on_device(): lax.all_to_all(message.reshape(BLKS, 1, LANES), all_axes, 0, 0, axis_inde...  15.7 us
    ppermute x3, starting transfers between devices, on_device(): lax.ppermute(atoms_own, 'rep', [(rep ^ turn, rep) for rep in range(REPS)])  9.63 us
    all_to_all x1, blocking collectives, on_device(): lax.all_to_all(share.reshape(16, 1, LANES), all_axes, 0, 0, axis_index_gr...  8.59 us
  transfers between devices with their start and end apart: 3, of which 0 were waited for; matrix products, arithmetic and copies ran while one was open for 0% of the time, Pallas kernels for 6%

profile of v5, /device:TPU:1, one launch (start us, length us, event | category | flops | bytes accessed | tf_op | source)
XLA Modules:
  0.0 144.6 jit_solution(5520887490054118112)
XLA Ops:
  0.6 1.7 %prepare.1 = (f32[32,3,4,128]{3,2,1,0:T(4,128)S(1)}, f32[8,128]{1,0:T(8,128)S(1)}) custom-call(f32[4,32,256]{2,1,0:T(8,128)} %features.1, f32[3,4,1024]{2,1,0:T(4,128)} %bitcast.33, s32[4,1024]{1,0:T(4,128)} %kinds.1, s32[4,256]{1,0:T(4,128)} %refs_3_.1, f32[15,2,32]{2,1,0:T(2,128)} %bitcast.34, f32[2,15]{1,0:T(2,128)} %refs_5_.1, f32[15,2,15]{2,1,0:T(2,128)} %bitcast.35, ...), custom_call_target="tpu_custom_call" | custom-call | tf_op jit(solution)/shard_map/prepare/pallas_call | solution.py:316
  2.3 29.7 %all_to_all.30.atoms.refs_0_ = f32[32,3,4,128]{3,2,1,0:T(4,128)S(1)} all-to-all(f32[32,3,4,128]{3,2,1,0:T(4,128)S(1)} %get-tuple-element.24), channel_id=1, replica_groups={{322,330,338,346,354,362,370,378,258,266,274,282,290,298,306,314,326,33..., dimensions={0} | all-to-all | bytes 393216 | tf_op jit(solution)/shard_map/all_to_all | solution.py:375
  32.1 3.2 %collective-permute-start = (f32[32,3,4,128]{3,2,1,0:T(4,128)S(1)}, f32[32,3,4,128]{3,2,1,0:T(4,128)S(1)}, u32[]{:S(2)}, u32[]{:S(2)}) collective-permute-start(f32[32,3,4,128]{3,2,1,0:T(4,128)S(1)} %all_to_all.30.atoms.refs_0_), channel_id=1, source_target_pairs={{1,0},{0,1},{3,2},{2,3},{5,4},{4,5},{7,6},{6,7},{9,8},{8,9},{11,10... | collective-permute-start | bytes 589832 | tf_op jit(solution)/shard_map/ppermute | solution.py:377
  35.3 3.8 %collective-permute-start.2 = (f32[32,3,4,128]{3,2,1,0:T(4,128)S(1)}, f32[32,3,4,128]{3,2,1,0:T(4,128)S(1)}, u32[]{:S(2)}, u32[]{:S(2)}) collective-permute-start(f32[32,3,4,128]{3,2,1,0:T(4,128)S(1)} %all_to_all.30.atoms.refs_0_), channel_id=1, source_target_pairs={{3,0},{2,1},{1,2},{0,3},{7,4},{6,5},{5,6},{4,7},{11,8},{10,9},{9,1... | collective-permute-start | bytes 589832 | tf_op jit(solution)/shard_map/ppermute | solution.py:377
  39.1 2.6 %collective-permute-start.1 = (f32[32,3,4,128]{3,2,1,0:T(4,128)S(1)}, f32[32,3,4,128]{3,2,1,0:T(4,128)S(1)}, u32[]{:S(2)}, u32[]{:S(2)}) collective-permute-start(f32[32,3,4,128]{3,2,1,0:T(4,128)S(1)} %all_to_all.30.atoms.refs_0_), channel_id=1, source_target_pairs={{2,0},{3,1},{0,2},{1,3},{6,4},{7,5},{4,6},{5,7},{10,8},{11,9},{8,1... | collective-permute-start | bytes 589832 | tf_op jit(solution)/shard_map/ppermute | solution.py:377
  41.7 4.3 %build_own.1 = (f32[64,256,128]{2,1,0:T(8,128)S(1)}, f32[5,256,128]{2,1,0:T(8,128)S(1)}) custom-call(f32[32,3,4,128]{3,2,1,0:T(4,128)S(1)} %all_to_all.30.atoms.refs_0_, f32[8,128]{1,0:T(8,128)S(1)} %get-tuple-element.25.constants), custom_call_target="tpu_custom_call" | custom-call | flops 1000000000 | tf_op jit(solution)/shard_map/build_own/pallas_call | solution.py:316
  46.0 0.0 collective-permute-done.part_1.refs_1_
  46.0 3.9 %build_next.1.refs_6_.refs_7_.piece_1 = f32[64,256,128]{2,1,0:T(8,128)S(1)} custom-call(f32[32,3,4,128]{3,2,1,0:T(4,128)S(1)} %collective-permute-done.part_1.refs_1_, f32[5,256,128]{2,1,0:T(8,128)S(1)} %get-tuple-element.26.rows.refs_4_), custom_call_target="tpu_custom_call" | custom-call | flops 1000000000 | tf_op jit(solution)/shard_map/build_next/pallas_call | solution.py:316
  50.0 0.0 collective-permute-done.2.refs_3_
  50.0 0.0 collective-permute-done.1.refs_2_
  50.0 10.8 %build_rest_and_begin.1 = (f32[64,256,128]{2,1,0:T(8,128)S(1)}, f32[64,256,128]{2,1,0:T(8,128)S(1)}, f32[256,128]{1,0:T(8,128)S(1)}, f32[256,128]{1,0:T(8,128)S(...) custom-call(f32[32,3,4,128]{3,2,1,0:T(4,128)S(1)} %all_to_all.30.atoms.refs_0_, ...), custom_call_target="tpu_custom_call" | custom-call | tf_op jit(solution)/shard_map/build_rest_and_begin/pallas_call | solution.py:316
  60.8 17.6 %all_to_all.31 = f32[128,2,128]{2,1,0:T(2,128)S(1)} all-to-all(f32[128,2,128]{2,1,0:T(2,128)S(1)} %bitcast.24), channel_id=1, replica_groups={{282,274,266,258,410,402,394,386,26,18,10,2,154,146,138,130,283,275,267..., dimensions={0} | all-to-all | bytes 262144 | tf_op jit(solution)/shard_map/all_to_all | solution.py:355
  78.4 3.0 %iterate.2 = (f32[256,128]{1,0:T(8,128)S(1)}, f32[256,128]{1,0:T(8,128)S(1)}, f32[256,128]{1,0:T(8,128)S(1)}, f32[256,128]{1,0:T(8,128)S(1)}, f32[8,128]{1,0:T(8,128)S(1)}) custom-call(f32[256,128]{1,0:T(8,128)S(1)} %bitcast.23, f32[256,128]{1,0:T(8,128)S(1)} %get-tuple-element.29.refs_1_.refs_2_, f32[256,128]{1,0:T(8,128)S(1)} %get-tuple-element.29.refs_1_.refs_2_, ...), custom_call_target="tpu_custom_call" | custom-call | tf_op jit(solution)/shard_map/iterate/pallas_call | solution.py:316
  81.4 15.9 %all_to_all.32 = f32[128,2,128]{2,1,0:T(2,128)S(1)} all-to-all(f32[128,2,128]{2,1,0:T(2,128)S(1)} %bitcast.26), channel_id=1, replica_groups={{282,274,266,258,410,402,394,386,26,18,10,2,154,146,138,130,283,275,267..., dimensions={0} | all-to-all | bytes 262144 | tf_op jit(solution)/shard_map/all_to_all | solution.py:355
  97.3 3.0 %iterate.3 = (f32[256,128]{1,0:T(8,128)S(1)}, f32[256,128]{1,0:T(8,128)S(1)}, f32[256,128]{1,0:T(8,128)S(1)}, f32[256,128]{1,0:T(8,128)S(1)}, f32[8,128]{1,0:T(8,128)S(1)}) custom-call(f32[256,128]{1,0:T(8,128)S(1)} %bitcast.22, f32[256,128]{1,0:T(8,128)S(1)} %get-tuple-element.35.refs_1_, f32[256,128]{1,0:T(8,128)S(1)} %get-tuple-element.36.refs_2_, ...), custom_call_target="tpu_custom_call" | custom-call | tf_op jit(solution)/shard_map/iterate/pallas_call | solution.py:316
  100.3 15.9 %all_to_all.33 = f32[128,2,128]{2,1,0:T(2,128)S(1)} all-to-all(f32[128,2,128]{2,1,0:T(2,128)S(1)} %bitcast.25), channel_id=1, replica_groups={{282,274,266,258,410,402,394,386,26,18,10,2,154,146,138,130,283,275,267..., dimensions={0} | all-to-all | bytes 262144 | tf_op jit(solution)/shard_map/all_to_all | solution.py:355
  116.2 0.0 copy-start
  116.2 0.0 copy-start.1
  116.2 0.0 copy-start.2
  116.2 0.0 copy-start.3
  116.2 0.0 copy-start.4
  116.2 0.0 copy-start.5
  116.2 0.0 copy-start.6
  116.2 3.0 %last.1 = (f32[16,128]{1,0:T(8,128)S(1)}, f32[32,128]{1,0:T(8,128)S(1)}) custom-call(f32[256,128]{1,0:T(8,128)S(1)} %bitcast.21, f32[256,128]{1,0:T(8,128)S(1)} %get-tuple-element.40.residual, f32[256,128]{1,0:T(8,128)S(1)} %get-tuple-element.41.direction, f32[256,128]{1,0:T(8,128)S(1)} %get-tuple-element.42.charges, ...), custom_call_target="tpu_custom_call" | custom-call | tf_op jit(solution)/shard_map/last/pallas_call | solution.py:316
  119.3 8.6 %all_to_all.34 = f32[16,1,128]{2,1,0:T(1,128)S(1)} all-to-all(f32[16,1,128]{2,1,0:T(1,128)S(1)} %bitcast.32), channel_id=1, replica_groups={{258,259,256,257,386,387,384,385,2,3,0,1,130,131,128,129},{262,263,260,..., dimensions={0} | all-to-all | bytes 16384 | tf_op jit(solution)/shard_map/all_to_all | solution.py:394
  127.9 0.1 join.1
  127.9 15.7 %all_to_all.35 = f32[32,1,128]{2,1,0:T(1,128)S(1)} all-to-all(f32[32,1,128]{2,1,0:T(1,128)S(1)} %bitcast.28), channel_id=1, replica_groups={{322,330,338,346,354,362,370,378,258,266,274,282,290,298,306,314,326,33..., dimensions={0} | all-to-all | bytes 32768 | tf_op jit(solution)/shard_map/all_to_all | solution.py:397
  143.6 0.0 copy-done
  143.6 0.0 copy-done.1
  143.7 0.0 copy-done.2
  143.7 0.0 copy-done.3
  143.7 0.0 copy-done.4
  143.7 0.0 copy-done.5
  143.7 0.0 copy-done.6
  143.7 0.9 finish.1
Async XLA Ops:
  32.1 13.9 %collective-permute-start = (f32[32,3,4,128]{3,2,1,0:T(4,128)S(1)}, f32[32,3,4,128]{3,2,1,0:T(4,128)S(1)}, u32[]{:S(2)}, u32[]{:S(2)}) collective-permute-start(f32[32,3,4,128]{3,2,1,0:T(4,128)S(1)} %all_to_all.30.atoms.refs_0_), channel_id=1, source_target_pairs={{1,0},{0,1},{3,2},{2,3},{5,4},{4,5},{7,6},{6,7},{9,8},{8,9},{11,10... | collective-permute-start | bytes 589832 | tf_op jit(solution)/shard_map/ppermute | solution.py:377
  35.3 14.7 %collective-permute-start.2 = (f32[32,3,4,128]{3,2,1,0:T(4,128)S(1)}, f32[32,3,4,128]{3,2,1,0:T(4,128)S(1)}, u32[]{:S(2)}, u32[]{:S(2)}) collective-permute-start(f32[32,3,4,128]{3,2,1,0:T(4,128)S(1)} %all_to_all.30.atoms.refs_0_), channel_id=1, source_target_pairs={{3,0},{2,1},{1,2},{0,3},{7,4},{6,5},{5,6},{4,7},{11,8},{10,9},{9,1... | collective-permute-start | bytes 589832 | tf_op jit(solution)/shard_map/ppermute | solution.py:377
  39.1 10.9 %collective-permute-start.1 = (f32[32,3,4,128]{3,2,1,0:T(4,128)S(1)}, f32[32,3,4,128]{3,2,1,0:T(4,128)S(1)}, u32[]{:S(2)}, u32[]{:S(2)}) collective-permute-start(f32[32,3,4,128]{3,2,1,0:T(4,128)S(1)} %all_to_all.30.atoms.refs_0_), channel_id=1, source_target_pairs={{2,0},{3,1},{0,2},{1,3},{6,4},{7,5},{4,6},{5,7},{10,8},{11,9},{8,1... | collective-permute-start | bytes 589832 | tf_op jit(solution)/shard_map/ppermute | solution.py:377
  116.2 27.5 %copy-start = (f32[4,32,256]{2,1,0:T(8,128)S(1)}, f32[4,32,256]{2,1,0:T(8,128)}, u32[]{:S(2)}) copy-start(f32[4,32,256]{2,1,0:T(8,128)} %features.1) | copy-start | bytes 393220
  116.2 27.5 %copy-start.1 = (s32[4,1024]{1,0:T(4,128)S(1)}, s32[4,1024]{1,0:T(4,128)}, u32[]{:S(2)}) copy-start(s32[4,1024]{1,0:T(4,128)} %kinds.1) | copy-start | bytes 49156
  116.2 27.5 %copy-start.2 = (f32[2,15,32]{2,0,1:T(2,128)S(1)}, f32[2,15,32]{2,0,1:T(2,128)}, u32[]{:S(2)}) copy-start(f32[2,15,32]{2,0,1:T(2,128)} %param.23) | copy-start | bytes 11524
  116.2 27.5 %copy-start.3 = (f32[2,15,15]{2,0,1:T(2,128)S(1)}, f32[2,15,15]{2,0,1:T(2,128)}, u32[]{:S(2)}) copy-start(f32[2,15,15]{2,0,1:T(2,128)} %param.26) | copy-start | bytes 5404
  116.2 27.5 %copy-start.4 = (f32[2,15]{1,0:T(2,128)S(1)}, f32[2,15]{1,0:T(2,128)}, u32[]{:S(2)}) copy-start(f32[2,15]{1,0:T(2,128)} %layer_charge.1) | copy-start | bytes 364
  116.2 27.5 %copy-start.5 = (f32[2,15]{1,0:T(2,128)S(1)}, f32[2,15]{1,0:T(2,128)}, u32[]{:S(2)}) copy-start(f32[2,15]{1,0:T(2,128)} %layer_bias.1) | copy-start | bytes 364
  116.2 27.5 %copy-start.6 = (f32[2,15]{1,0:T(2,128)S(1)}, f32[2,15]{1,0:T(2,128)}, u32[]{:S(2)}) copy-start(f32[2,15]{1,0:T(2,128)} %layer_out.1) | copy-start | bytes 364

commit v6 on v5

--- a/solution.py
+++ b/solution.py
@@ -160,7 +160,7 @@
                 piece[2 * block + half, span, :] = lax.erf(squared * inverse * scale) * inverse
         return carry
 
-    lax.fori_loop(0, BLKS, one_block, 0, unroll=4)
+    lax.fori_loop(0, BLKS, one_block, 0, unroll=8)
 
 
 def build_own_kernel(atoms, constants, piece, rows):
@@ -189,7 +189,7 @@
                     sums[group] + piece[here, group * 8 : group * 8 + 8, :] * values for group in range(GROUPS)
                 )
 
-            sums = lax.fori_loop(0, BLKS, one_line, sums, unroll=8)
+            sums = lax.fori_loop(0, BLKS, one_line, sums, unroll=16)
     half = GROUPS // 2
     return [
         jnp.sum(jnp.concatenate(sums[part * half : part * half + half], axis=0).T, axis=0, keepdims=True)

time: 145 us -> 144 us (level)
  no operation moved by 1% of the time
where the time goes in v6:
time: 144 us
  blocking collectives  103 us (72%)
  Pallas kernels  29.7 us (21%)
  starting transfers between devices  9.64 us (7%)
    all_to_all x3, blocking collectives, exchange(): lax.all_to_all(sent, all_axes, 0, 0, axis_index_groups=cube_groups())  49.4 us
    all_to_all x1, blocking collectives, on_device(): lax.all_to_all(message, all_axes, 0, 0, axis_index_groups=block_groups())  29.8 us
    pallas_call x9, Pallas kernels, run(): pl.pallas_call(kernel, out_shape=outs, in_specs=[held] * len(args), out_s...  29.7 us
    all_to_all x1, blocking collectives, on_device(): lax.all_to_all(message.reshape(BLKS, 1, LANES), all_axes, 0, 0, axis_inde...  15.7 us
    ppermute x3, starting transfers between devices, on_device(): lax.ppermute(atoms_own, 'rep', [(rep ^ turn, rep) for rep in range(REPS)])  9.64 us
    all_to_all x1, blocking collectives, on_device(): lax.all_to_all(share.reshape(16, 1, LANES), all_axes, 0, 0, axis_index_gr...  8.59 us
  transfers between devices with their start and end apart: 3, of which 0 were waited for; matrix products, arithmetic and copies ran while one was open for 0% of the time, Pallas kernels for 6%

profile of v6, /device:TPU:1, one launch (start us, length us, event | category | flops | bytes accessed | tf_op | source)
XLA Modules:
  0.0 143.6 jit_solution(6219156546739916476)
XLA Ops:
  0.6 1.7 %prepare.1 = (f32[32,3,4,128]{3,2,1,0:T(4,128)S(1)}, f32[8,128]{1,0:T(8,128)S(1)}) custom-call(f32[4,32,256]{2,1,0:T(8,128)} %features.1, f32[3,4,1024]{2,1,0:T(4,128)} %bitcast.33, s32[4,1024]{1,0:T(4,128)} %kinds.1, s32[4,256]{1,0:T(4,128)} %refs_3_.1, f32[15,2,32]{2,1,0:T(2,128)} %bitcast.34, f32[2,15]{1,0:T(2,128)} %refs_5_.1, f32[15,2,15]{2,1,0:T(2,128)} %bitcast.35, ...), custom_call_target="tpu_custom_call" | custom-call | tf_op jit(solution)/shard_map/prepare/pallas_call | solution.py:316
  2.3 29.8 %all_to_all.30.atoms.refs_0_ = f32[32,3,4,128]{3,2,1,0:T(4,128)S(1)} all-to-all(f32[32,3,4,128]{3,2,1,0:T(4,128)S(1)} %get-tuple-element.24), channel_id=1, replica_groups={{322,330,338,346,354,362,370,378,258,266,274,282,290,298,306,314,326,33..., dimensions={0} | all-to-all | bytes 393216 | tf_op jit(solution)/shard_map/all_to_all | solution.py:375
  32.1 3.2 %collective-permute-start = (f32[32,3,4,128]{3,2,1,0:T(4,128)S(1)}, f32[32,3,4,128]{3,2,1,0:T(4,128)S(1)}, u32[]{:S(2)}, u32[]{:S(2)}) collective-permute-start(f32[32,3,4,128]{3,2,1,0:T(4,128)S(1)} %all_to_all.30.atoms.refs_0_), channel_id=1, source_target_pairs={{1,0},{0,1},{3,2},{2,3},{5,4},{4,5},{7,6},{6,7},{9,8},{8,9},{11,10... | collective-permute-start | bytes 589832 | tf_op jit(solution)/shard_map/ppermute | solution.py:377
  35.3 3.8 %collective-permute-start.2 = (f32[32,3,4,128]{3,2,1,0:T(4,128)S(1)}, f32[32,3,4,128]{3,2,1,0:T(4,128)S(1)}, u32[]{:S(2)}, u32[]{:S(2)}) collective-permute-start(f32[32,3,4,128]{3,2,1,0:T(4,128)S(1)} %all_to_all.30.atoms.refs_0_), channel_id=1, source_target_pairs={{3,0},{2,1},{1,2},{0,3},{7,4},{6,5},{5,6},{4,7},{11,8},{10,9},{9,1... | collective-permute-start | bytes 589832 | tf_op jit(solution)/shard_map/ppermute | solution.py:377
  39.1 2.6 %collective-permute-start.1 = (f32[32,3,4,128]{3,2,1,0:T(4,128)S(1)}, f32[32,3,4,128]{3,2,1,0:T(4,128)S(1)}, u32[]{:S(2)}, u32[]{:S(2)}) collective-permute-start(f32[32,3,4,128]{3,2,1,0:T(4,128)S(1)} %all_to_all.30.atoms.refs_0_), channel_id=1, source_target_pairs={{2,0},{3,1},{0,2},{1,3},{6,4},{7,5},{4,6},{5,7},{10,8},{11,9},{8,1... | collective-permute-start | bytes 589832 | tf_op jit(solution)/shard_map/ppermute | solution.py:377
  41.7 4.2 %build_own.1 = (f32[64,256,128]{2,1,0:T(8,128)S(1)}, f32[5,256,128]{2,1,0:T(8,128)S(1)}) custom-call(f32[32,3,4,128]{3,2,1,0:T(4,128)S(1)} %all_to_all.30.atoms.refs_0_, f32[8,128]{1,0:T(8,128)S(1)} %get-tuple-element.25.constants), custom_call_target="tpu_custom_call" | custom-call | flops 1000000000 | tf_op jit(solution)/shard_map/build_own/pallas_call | solution.py:316
  45.9 0.0 collective-permute-done.part_1.refs_1_
  45.9 3.8 %build_next.1.refs_6_.refs_7_.piece_1 = f32[64,256,128]{2,1,0:T(8,128)S(1)} custom-call(f32[32,3,4,128]{3,2,1,0:T(4,128)S(1)} %collective-permute-done.part_1.refs_1_, f32[5,256,128]{2,1,0:T(8,128)S(1)} %get-tuple-element.26.rows.refs_4_), custom_call_target="tpu_custom_call" | custom-call | flops 1000000000 | tf_op jit(solution)/shard_map/build_next/pallas_call | solution.py:316
  49.8 0.0 collective-permute-done.2.refs_3_
  49.8 0.0 collective-permute-done.1.refs_2_
  49.8 10.5 %build_rest_and_begin.1 = (f32[64,256,128]{2,1,0:T(8,128)S(1)}, f32[64,256,128]{2,1,0:T(8,128)S(1)}, f32[256,128]{1,0:T(8,128)S(1)}, f32[256,128]{1,0:T(8,128)S(...) custom-call(f32[32,3,4,128]{3,2,1,0:T(4,128)S(1)} %all_to_all.30.atoms.refs_0_, ...), custom_call_target="tpu_custom_call" | custom-call | tf_op jit(solution)/shard_map/build_rest_and_begin/pallas_call | solution.py:316
  60.3 17.5 %all_to_all.31 = f32[128,2,128]{2,1,0:T(2,128)S(1)} all-to-all(f32[128,2,128]{2,1,0:T(2,128)S(1)} %bitcast.24), channel_id=1, replica_groups={{282,274,266,258,410,402,394,386,26,18,10,2,154,146,138,130,283,275,267..., dimensions={0} | all-to-all | bytes 262144 | tf_op jit(solution)/shard_map/all_to_all | solution.py:355
  77.9 2.8 %iterate.2 = (f32[256,128]{1,0:T(8,128)S(1)}, f32[256,128]{1,0:T(8,128)S(1)}, f32[256,128]{1,0:T(8,128)S(1)}, f32[256,128]{1,0:T(8,128)S(1)}, f32[8,128]{1,0:T(8,128)S(1)}) custom-call(f32[256,128]{1,0:T(8,128)S(1)} %bitcast.23, f32[256,128]{1,0:T(8,128)S(1)} %get-tuple-element.29.refs_1_.refs_2_, f32[256,128]{1,0:T(8,128)S(1)} %get-tuple-element.29.refs_1_.refs_2_, ...), custom_call_target="tpu_custom_call" | custom-call | tf_op jit(solution)/shard_map/iterate/pallas_call | solution.py:316
  80.7 15.9 %all_to_all.32 = f32[128,2,128]{2,1,0:T(2,128)S(1)} all-to-all(f32[128,2,128]{2,1,0:T(2,128)S(1)} %bitcast.26), channel_id=1, replica_groups={{282,274,266,258,410,402,394,386,26,18,10,2,154,146,138,130,283,275,267..., dimensions={0} | all-to-all | bytes 262144 | tf_op jit(solution)/shard_map/all_to_all | solution.py:355
  96.6 2.8 %iterate.3 = (f32[256,128]{1,0:T(8,128)S(1)}, f32[256,128]{1,0:T(8,128)S(1)}, f32[256,128]{1,0:T(8,128)S(1)}, f32[256,128]{1,0:T(8,128)S(1)}, f32[8,128]{1,0:T(8,128)S(1)}) custom-call(f32[256,128]{1,0:T(8,128)S(1)} %bitcast.22, f32[256,128]{1,0:T(8,128)S(1)} %get-tuple-element.35.refs_1_, f32[256,128]{1,0:T(8,128)S(1)} %get-tuple-element.36.refs_2_, ...), custom_call_target="tpu_custom_call" | custom-call | tf_op jit(solution)/shard_map/iterate/pallas_call | solution.py:316
  99.4 15.9 %all_to_all.33 = f32[128,2,128]{2,1,0:T(2,128)S(1)} all-to-all(f32[128,2,128]{2,1,0:T(2,128)S(1)} %bitcast.25), channel_id=1, replica_groups={{282,274,266,258,410,402,394,386,26,18,10,2,154,146,138,130,283,275,267..., dimensions={0} | all-to-all | bytes 262144 | tf_op jit(solution)/shard_map/all_to_all | solution.py:355
  115.3 0.0 copy-start
  115.3 0.0 copy-start.1
  115.4 0.0 copy-start.2
  115.4 0.0 copy-start.3
  115.4 0.0 copy-start.4
  115.4 0.0 copy-start.5
  115.4 0.0 copy-start.6
  115.4 2.9 %last.1 = (f32[16,128]{1,0:T(8,128)S(1)}, f32[32,128]{1,0:T(8,128)S(1)}) custom-call(f32[256,128]{1,0:T(8,128)S(1)} %bitcast.21, f32[256,128]{1,0:T(8,128)S(1)} %get-tuple-element.40.residual, f32[256,128]{1,0:T(8,128)S(1)} %get-tuple-element.41.direction, f32[256,128]{1,0:T(8,128)S(1)} %get-tuple-element.42.charges, ...), custom_call_target="tpu_custom_call" | custom-call | tf_op jit(solution)/shard_map/last/pallas_call | solution.py:316
  118.3 8.6 %all_to_all.34 = f32[16,1,128]{2,1,0:T(1,128)S(1)} all-to-all(f32[16,1,128]{2,1,0:T(1,128)S(1)} %bitcast.32), channel_id=1, replica_groups={{258,259,256,257,386,387,384,385,2,3,0,1,130,131,128,129},{262,263,260,..., dimensions={0} | all-to-all | bytes 16384 | tf_op jit(solution)/shard_map/all_to_all | solution.py:394
  126.9 0.1 join.1
  126.9 15.7 %all_to_all.35 = f32[32,1,128]{2,1,0:T(1,128)S(1)} all-to-all(f32[32,1,128]{2,1,0:T(1,128)S(1)} %bitcast.28), channel_id=1, replica_groups={{322,330,338,346,354,362,370,378,258,266,274,282,290,298,306,314,326,33..., dimensions={0} | all-to-all | bytes 32768 | tf_op jit(solution)/shard_map/all_to_all | solution.py:397
  142.7 0.0 copy-done
  142.7 0.0 copy-done.1
  142.7 0.0 copy-done.2
  142.7 0.0 copy-done.3
  142.7 0.0 copy-done.4
  142.7 0.0 copy-done.5
  142.7 0.0 copy-done.6
  142.7 0.9 finish.1
Async XLA Ops:
  32.1 13.9 %collective-permute-start = (f32[32,3,4,128]{3,2,1,0:T(4,128)S(1)}, f32[32,3,4,128]{3,2,1,0:T(4,128)S(1)}, u32[]{:S(2)}, u32[]{:S(2)}) collective-permute-start(f32[32,3,4,128]{3,2,1,0:T(4,128)S(1)} %all_to_all.30.atoms.refs_0_), channel_id=1, source_target_pairs={{1,0},{0,1},{3,2},{2,3},{5,4},{4,5},{7,6},{6,7},{9,8},{8,9},{11,10... | collective-permute-start | bytes 589832 | tf_op jit(solution)/shard_map/ppermute | solution.py:377
  35.3 14.5 %collective-permute-start.2 = (f32[32,3,4,128]{3,2,1,0:T(4,128)S(1)}, f32[32,3,4,128]{3,2,1,0:T(4,128)S(1)}, u32[]{:S(2)}, u32[]{:S(2)}) collective-permute-start(f32[32,3,4,128]{3,2,1,0:T(4,128)S(1)} %all_to_all.30.atoms.refs_0_), channel_id=1, source_target_pairs={{3,0},{2,1},{1,2},{0,3},{7,4},{6,5},{5,6},{4,7},{11,8},{10,9},{9,1... | collective-permute-start | bytes 589832 | tf_op jit(solution)/shard_map/ppermute | solution.py:377
  39.1 10.7 %collective-permute-start.1 = (f32[32,3,4,128]{3,2,1,0:T(4,128)S(1)}, f32[32,3,4,128]{3,2,1,0:T(4,128)S(1)}, u32[]{:S(2)}, u32[]{:S(2)}) collective-permute-start(f32[32,3,4,128]{3,2,1,0:T(4,128)S(1)} %all_to_all.30.atoms.refs_0_), channel_id=1, source_target_pairs={{2,0},{3,1},{0,2},{1,3},{6,4},{7,5},{4,6},{5,7},{10,8},{11,9},{8,1... | collective-permute-start | bytes 589832 | tf_op jit(solution)/shard_map/ppermute | solution.py:377
  115.3 27.3 %copy-start = (f32[4,32,256]{2,1,0:T(8,128)S(1)}, f32[4,32,256]{2,1,0:T(8,128)}, u32[]{:S(2)}) copy-start(f32[4,32,256]{2,1,0:T(8,128)} %features.1) | copy-start | bytes 393220
  115.3 27.3 %copy-start.1 = (s32[4,1024]{1,0:T(4,128)S(1)}, s32[4,1024]{1,0:T(4,128)}, u32[]{:S(2)}) copy-start(s32[4,1024]{1,0:T(4,128)} %kinds.1) | copy-start | bytes 49156
  115.4 27.3 %copy-start.2 = (f32[2,15,32]{2,0,1:T(2,128)S(1)}, f32[2,15,32]{2,0,1:T(2,128)}, u32[]{:S(2)}) copy-start(f32[2,15,32]{2,0,1:T(2,128)} %param.23) | copy-start | bytes 11524
  115.4 27.3 %copy-start.3 = (f32[2,15,15]{2,0,1:T(2,128)S(1)}, f32[2,15,15]{2,0,1:T(2,128)}, u32[]{:S(2)}) copy-start(f32[2,15,15]{2,0,1:T(2,128)} %param.26) | copy-start | bytes 5404
  115.4 27.3 %copy-start.4 = (f32[2,15]{1,0:T(2,128)S(1)}, f32[2,15]{1,0:T(2,128)}, u32[]{:S(2)}) copy-start(f32[2,15]{1,0:T(2,128)} %layer_charge.1) | copy-start | bytes 364
  115.4 27.3 %copy-start.5 = (f32[2,15]{1,0:T(2,128)S(1)}, f32[2,15]{1,0:T(2,128)}, u32[]{:S(2)}) copy-start(f32[2,15]{1,0:T(2,128)} %layer_bias.1) | copy-start | bytes 364
  115.4 27.3 %copy-start.6 = (f32[2,15]{1,0:T(2,128)S(1)}, f32[2,15]{1,0:T(2,128)}, u32[]{:S(2)}) copy-start(f32[2,15]{1,0:T(2,128)} %layer_out.1) | copy-start | bytes 364

commit v7 on v6

--- a/solution.py
+++ b/solution.py
@@ -67,6 +67,10 @@
     core, spot = lax.axis_index("core"), lax.axis_index("zr")
     turned = jnp.where(lax.axis_index("zq") < 2, 3 - spot, spot)
     return lax.axis_index("rep"), core * 16 + lax.rem(lax.axis_index("phase") + 2, 4) * 4 + turned, core * 4 + spot
+
+
+def source_of(rep, turn):
+    return rep ^ turn if turn in (0, 2) else rep ^ jnp.where(lax.axis_index("core") == 0, turn, 4 - turn)
 
 
 def row_of(rep, line):
@@ -180,7 +184,7 @@
     sums = tuple(jnp.zeros((8, LANES), float32) for _ in range(GROUPS))
     for turn, piece in enumerate(pieces):
         for core in range(2):
-            first = row_of(rep ^ turn, core * BLKS)
+            first = row_of(source_of(rep, turn), core * BLKS)
 
             def one_line(line, sums, core=core, piece=piece, first=first):
                 values = jnp.broadcast_to(direction[pl.ds(first + line, 1), :], (8, LANES))
@@ -224,7 +228,7 @@
     build_piece(parts[3], rows, piece_3)
     build_piece(parts[2], rows, piece_2)
     for turn, part in enumerate(parts):
-        source = rep ^ turn
+        source = source_of(rep, turn)
         for block in range(BLKS):
             lines = pl.ds(row_of(source, block * 2), 2)
             residual[lines, :] = part[block, 2, 0:2, :]
@@ -373,11 +377,14 @@
         held=pl.BlockSpec(memory_space=pl.ANY),
     )(*[pltpu.with_memory_space_constraint(one, pltpu.HBM) for one in given])
     atoms_own = lax.all_to_all(message, all_axes, 0, 0, axis_index_groups=block_groups())
-    parts = [
-        lax.ppermute(atoms_own, "rep", [(rep ^ turn, rep) for rep in range(REPS)]) for turn in range(1, REPS)
-    ]
+    far = [(core * REPS + (rep ^ turn), core * REPS + rep) for core, turn in ((0, 1), (1, 3)) for rep in range(REPS)]
+    part_1 = lax.ppermute(atoms_own, ("core", "rep"), far)
+    part_2 = lax.ppermute(atoms_own, "rep", [(rep ^ 2, rep) for rep in range(REPS)])
     own_piece, row_values = call(build_own_kernel, [piece, rows], "build_own", flops=10**9)(atoms_own, constants)
-    piece_1 = call(build_kernel, piece, "build_next", flops=10**9)(parts[0], *kept([row_values]))
+    part_1, row_values = lax.optimization_barrier((part_1, row_values))
+    part_3 = lax.ppermute(part_1, "core", [(0, 1), (1, 0)])
+    parts = [part_1, part_2, part_3]
+    piece_1 = call(build_kernel, piece, "build_next", flops=10**9)(part_1, *kept([row_values]))
     piece_3, piece_2, message, residual, groups, norm = call(
         first_kernel, [piece, piece, whole, whole, whole, small], "build_rest_and_begin"
     )(atoms_own, *parts, *kept([row_values, own_piece, piece_1]))

time: 144 us -> 144 us (level)
    all_to_all x3, blocking collectives: 49.4 us -> 47.6 us  [exchange(): lax.all_to_all(sent, all_axes, 0, 0, axis_index_groups=cube_groups())]
where the time goes in v7:
time: 144 us; the launch traced here: 143 us
  blocking collectives  102 us (71%)
  Pallas kernels  29.8 us (21%)
  starting transfers between devices  10.6 us (7%)
    all_to_all x3, blocking collectives, exchange(): lax.all_to_all(sent, all_axes, 0, 0, axis_index_groups=cube_groups())  47.6 us
    pallas_call x9, Pallas kernels, run(): pl.pallas_call(kernel, out_shape=outs, in_specs=[held] * len(args), out_s...  29.8 us
    all_to_all x1, blocking collectives, on_device(): lax.all_to_all(message, all_axes, 0, 0, axis_index_groups=block_groups())  29.8 us
    all_to_all x1, blocking collectives, on_device(): lax.all_to_all(message.reshape(BLKS, 1, LANES), all_axes, 0, 0, axis_inde...  16 us
    all_to_all x1, blocking collectives, on_device(): lax.all_to_all(share.reshape(16, 1, LANES), all_axes, 0, 0, axis_index_gr...  8.59 us
    ppermute x1, starting transfers between devices, on_device(): part_1 = lax.ppermute(atoms_own, ('core', 'rep'), far)  4.63 us
    ppermute x1, starting transfers between devices, on_device(): part_3 = lax.ppermute(part_1, 'core', [(0, 1), (1, 0)])  3.75 us
  transfers between devices with their start and end apart: 3, of which 0 were waited for; matrix products, arithmetic and copies ran while one was open for 0% of the time, Pallas kernels for 6%

profile of v7, /device:TPU:1, one launch (start us, length us, event | category | flops | bytes accessed | tf_op | source)
XLA Modules:
  0.0 143.2 jit_solution(18331282010618819231)
XLA Ops:
  0.6 1.7 %prepare.1 = (f32[32,3,4,128]{3,2,1,0:T(4,128)S(1)}, f32[8,128]{1,0:T(8,128)S(1)}) custom-call(f32[4,32,256]{2,1,0:T(8,128)} %features.1, f32[3,4,1024]{2,1,0:T(4,128)} %bitcast.33, s32[4,1024]{1,0:T(4,128)} %kinds.1, s32[4,256]{1,0:T(4,128)} %refs_3_.1, f32[15,2,32]{2,1,0:T(2,128)} %bitcast.34, f32[2,15]{1,0:T(2,128)} %refs_5_.1, f32[15,2,15]{2,1,0:T(2,128)} %bitcast.35, ...), custom_call_target="tpu_custom_call" | custom-call | tf_op jit(solution)/shard_map/prepare/pallas_call | solution.py:320
  2.3 29.8 %all_to_all.30.atoms.refs_0_ = f32[32,3,4,128]{3,2,1,0:T(4,128)S(1)} all-to-all(f32[32,3,4,128]{3,2,1,0:T(4,128)S(1)} %get-tuple-element.26), channel_id=1, replica_groups={{322,330,338,346,354,362,370,378,258,266,274,282,290,298,306,314,326,33..., dimensions={0} | all-to-all | bytes 393216 | tf_op jit(solution)/shard_map/all_to_all | solution.py:379
  32.1 4.6 %collective-permute-start = (f32[32,3,4,128]{3,2,1,0:T(4,128)S(1)}, f32[32,3,4,128]{3,2,1,0:T(4,128)S(1)}, u32[]{:S(2)}, u32[]{:S(2)}) collective-permute-start(f32[32,3,4,128]{3,2,1,0:T(4,128)S(1)} %all_to_all.30.atoms.refs_0_), channel_id=1, source_target_pairs={{1,0},{0,1},{3,2},{2,3},{7,4},{6,5},{5,6},{4,7},{9,8},{8,9},{11,10... | collective-permute-start | bytes 589832 | tf_op jit(solution)/shard_map/ppermute | solution.py:381
  36.7 2.3 %collective-permute-start.1 = (f32[32,3,4,128]{3,2,1,0:T(4,128)S(1)}, f32[32,3,4,128]{3,2,1,0:T(4,128)S(1)}, u32[]{:S(2)}, u32[]{:S(2)}) collective-permute-start(f32[32,3,4,128]{3,2,1,0:T(4,128)S(1)} %all_to_all.30.atoms.refs_0_), channel_id=1, source_target_pairs={{2,0},{3,1},{0,2},{1,3},{6,4},{7,5},{4,6},{5,7},{10,8},{11,9},{8,1... | collective-permute-start | bytes 589832 | tf_op jit(solution)/shard_map/ppermute | solution.py:382
  39.0 4.2 %build_own.1 = (f32[64,256,128]{2,1,0:T(8,128)S(1)}, f32[5,256,128]{2,1,0:T(8,128)S(1)}) custom-call(f32[32,3,4,128]{3,2,1,0:T(4,128)S(1)} %all_to_all.30.atoms.refs_0_, f32[8,128]{1,0:T(8,128)S(1)} %get-tuple-element.27.constants), custom_call_target="tpu_custom_call" | custom-call | flops 1000000000 | tf_op jit(solution)/shard_map/build_own/pallas_call | solution.py:320
  43.2 0.0 collective-permute-done.part_1.refs_1_
  43.2 3.7 %collective-permute-start.2 = (f32[32,3,4,128]{3,2,1,0:T(4,128)S(1)}, f32[32,3,4,128]{3,2,1,0:T(4,128)S(1)}, u32[]{:S(2)}, u32[]{:S(2)}) collective-permute-start(f32[32,3,4,128]{3,2,1,0:T(4,128)S(1)} %collective-permute-done.part_1.refs_1_), channel_id=1, source_target_pairs={{0,4},{4,0},{1,5},{5,1},{2,6},{6,2},{3,7},{7,3},{8,12},{12,8},{9,1... | collective-permute-start | bytes 589832 | tf_op jit(solution)/shard_map/ppermute | solution.py:385
  46.9 3.8 %build_next.1.refs_6_.refs_7_.piece_1 = f32[64,256,128]{2,1,0:T(8,128)S(1)} custom-call(f32[32,3,4,128]{3,2,1,0:T(4,128)S(1)} %collective-permute-done.part_1.refs_1_, f32[5,256,128]{2,1,0:T(8,128)S(1)} %get-tuple-element.30.rows.refs_4_), custom_call_target="tpu_custom_call" | custom-call | flops 1000000000 | tf_op jit(solution)/shard_map/build_next/pallas_call | solution.py:320
  50.8 0.0 collective-permute-done.1.refs_2_
  50.8 0.0 collective-permute-done.2.refs_3_
  50.8 10.5 %build_rest_and_begin.1 = (f32[64,256,128]{2,1,0:T(8,128)S(1)}, f32[64,256,128]{2,1,0:T(8,128)S(1)}, f32[256,128]{1,0:T(8,128)S(1)}, f32[256,128]{1,0:T(8,128)S(...) custom-call(f32[32,3,4,128]{3,2,1,0:T(4,128)S(1)} %all_to_all.30.atoms.refs_0_, ...), custom_call_target="tpu_custom_call" | custom-call | tf_op jit(solution)/shard_map/build_rest_and_begin/pallas_call | solution.py:320
  61.3 15.8 %all_to_all.31 = f32[128,2,128]{2,1,0:T(2,128)S(1)} all-to-all(f32[128,2,128]{2,1,0:T(2,128)S(1)} %bitcast.24), channel_id=1, replica_groups={{282,274,266,258,410,402,394,386,26,18,10,2,154,146,138,130,283,275,267..., dimensions={0} | all-to-all | bytes 262144 | tf_op jit(solution)/shard_map/all_to_all | solution.py:359
  77.1 2.8 %iterate.2 = (f32[256,128]{1,0:T(8,128)S(1)}, f32[256,128]{1,0:T(8,128)S(1)}, f32[256,128]{1,0:T(8,128)S(1)}, f32[256,128]{1,0:T(8,128)S(1)}, f32[8,128]{1,0:T(8,128)S(1)}) custom-call(f32[256,128]{1,0:T(8,128)S(1)} %bitcast.23, f32[256,128]{1,0:T(8,128)S(1)} %get-tuple-element.33.refs_1_.refs_2_, f32[256,128]{1,0:T(8,128)S(1)} %get-tuple-element.33.refs_1_.refs_2_, ...), custom_call_target="tpu_custom_call" | custom-call | tf_op jit(solution)/shard_map/iterate/pallas_call | solution.py:320
  80.0 15.9 %all_to_all.32 = f32[128,2,128]{2,1,0:T(2,128)S(1)} all-to-all(f32[128,2,128]{2,1,0:T(2,128)S(1)} %bitcast.26), channel_id=1, replica_groups={{282,274,266,258,410,402,394,386,26,18,10,2,154,146,138,130,283,275,267..., dimensions={0} | all-to-all | bytes 262144 | tf_op jit(solution)/shard_map/all_to_all | solution.py:359
  95.9 2.8 %iterate.3 = (f32[256,128]{1,0:T(8,128)S(1)}, f32[256,128]{1,0:T(8,128)S(1)}, f32[256,128]{1,0:T(8,128)S(1)}, f32[256,128]{1,0:T(8,128)S(1)}, f32[8,128]{1,0:T(8,128)S(1)}) custom-call(f32[256,128]{1,0:T(8,128)S(1)} %bitcast.22, f32[256,128]{1,0:T(8,128)S(1)} %get-tuple-element.39.refs_1_, f32[256,128]{1,0:T(8,128)S(1)} %get-tuple-element.40.refs_2_, ...), custom_call_target="tpu_custom_call" | custom-call | tf_op jit(solution)/shard_map/iterate/pallas_call | solution.py:320
  98.7 15.9 %all_to_all.33 = f32[128,2,128]{2,1,0:T(2,128)S(1)} all-to-all(f32[128,2,128]{2,1,0:T(2,128)S(1)} %bitcast.25), channel_id=1, replica_groups={{282,274,266,258,410,402,394,386,26,18,10,2,154,146,138,130,283,275,267..., dimensions={0} | all-to-all | bytes 262144 | tf_op jit(solution)/shard_map/all_to_all | solution.py:359
  114.6 0.0 copy-start
  114.6 0.0 copy-start.1
  114.6 0.0 copy-start.2
  114.6 0.0 copy-start.3
  114.6 0.0 copy-start.4
  114.7 0.0 copy-start.5
  114.7 0.0 copy-start.6
  114.7 2.9 %last.1 = (f32[16,128]{1,0:T(8,128)S(1)}, f32[32,128]{1,0:T(8,128)S(1)}) custom-call(f32[256,128]{1,0:T(8,128)S(1)} %bitcast.21, f32[256,128]{1,0:T(8,128)S(1)} %get-tuple-element.44.residual, f32[256,128]{1,0:T(8,128)S(1)} %get-tuple-element.45.direction, f32[256,128]{1,0:T(8,128)S(1)} %get-tuple-element.46.charges, ...), custom_call_target="tpu_custom_call" | custom-call | tf_op jit(solution)/shard_map/last/pallas_call | solution.py:320
  117.6 8.6 %all_to_all.34 = f32[16,1,128]{2,1,0:T(1,128)S(1)} all-to-all(f32[16,1,128]{2,1,0:T(1,128)S(1)} %bitcast.32), channel_id=1, replica_groups={{258,259,256,257,386,387,384,385,2,3,0,1,130,131,128,129},{262,263,260,..., dimensions={0} | all-to-all | bytes 16384 | tf_op jit(solution)/shard_map/all_to_all | solution.py:401
  126.2 0.1 join.1
  126.2 16.0 %all_to_all.35 = f32[32,1,128]{2,1,0:T(1,128)S(1)} all-to-all(f32[32,1,128]{2,1,0:T(1,128)S(1)} %bitcast.28), channel_id=1, replica_groups={{322,330,338,346,354,362,370,378,258,266,274,282,290,298,306,314,326,33..., dimensions={0} | all-to-all | bytes 32768 | tf_op jit(solution)/shard_map/all_to_all | solution.py:404
  142.2 0.0 copy-done
  142.2 0.0 copy-done.1
  142.2 0.0 copy-done.2
  142.2 0.0 copy-done.3
  142.3 0.0 copy-done.4
  142.3 0.0 copy-done.5
  142.3 0.0 copy-done.6
  142.3 0.9 finish.1
Async XLA Ops:
  32.1 11.1 %collective-permute-start = (f32[32,3,4,128]{3,2,1,0:T(4,128)S(1)}, f32[32,3,4,128]{3,2,1,0:T(4,128)S(1)}, u32[]{:S(2)}, u32[]{:S(2)}) collective-permute-start(f32[32,3,4,128]{3,2,1,0:T(4,128)S(1)} %all_to_all.30.atoms.refs_0_), channel_id=1, source_target_pairs={{1,0},{0,1},{3,2},{2,3},{7,4},{6,5},{5,6},{4,7},{9,8},{8,9},{11,10... | collective-permute-start | bytes 589832 | tf_op jit(solution)/shard_map/ppermute | solution.py:381
  36.7 14.1 %collective-permute-start.1 = (f32[32,3,4,128]{3,2,1,0:T(4,128)S(1)}, f32[32,3,4,128]{3,2,1,0:T(4,128)S(1)}, u32[]{:S(2)}, u32[]{:S(2)}) collective-permute-start(f32[32,3,4,128]{3,2,1,0:T(4,128)S(1)} %all_to_all.30.atoms.refs_0_), channel_id=1, source_target_pairs={{2,0},{3,1},{0,2},{1,3},{6,4},{7,5},{4,6},{5,7},{10,8},{11,9},{8,1... | collective-permute-start | bytes 589832 | tf_op jit(solution)/shard_map/ppermute | solution.py:382
  43.2 7.6 %collective-permute-start.2 = (f32[32,3,4,128]{3,2,1,0:T(4,128)S(1)}, f32[32,3,4,128]{3,2,1,0:T(4,128)S(1)}, u32[]{:S(2)}, u32[]{:S(2)}) collective-permute-start(f32[32,3,4,128]{3,2,1,0:T(4,128)S(1)} %collective-permute-done.part_1.refs_1_), channel_id=1, source_target_pairs={{0,4},{4,0},{1,5},{5,1},{2,6},{6,2},{3,7},{7,3},{8,12},{12,8},{9,1... | collective-permute-start | bytes 589832 | tf_op jit(solution)/shard_map/ppermute | solution.py:385
  114.6 27.6 %copy-start = (f32[4,32,256]{2,1,0:T(8,128)S(1)}, f32[4,32,256]{2,1,0:T(8,128)}, u32[]{:S(2)}) copy-start(f32[4,32,256]{2,1,0:T(8,128)} %features.1) | copy-start | bytes 393220
  114.6 27.6 %copy-start.1 = (s32[4,1024]{1,0:T(4,128)S(1)}, s32[4,1024]{1,0:T(4,128)}, u32[]{:S(2)}) copy-start(s32[4,1024]{1,0:T(4,128)} %kinds.1) | copy-start | bytes 49156
  114.6 27.6 %copy-start.2 = (f32[2,15,32]{2,0,1:T(2,128)S(1)}, f32[2,15,32]{2,0,1:T(2,128)}, u32[]{:S(2)}) copy-start(f32[2,15,32]{2,0,1:T(2,128)} %param.23) | copy-start | bytes 11524
  114.6 27.6 %copy-start.3 = (f32[2,15,15]{2,0,1:T(2,128)S(1)}, f32[2,15,15]{2,0,1:T(2,128)}, u32[]{:S(2)}) copy-start(f32[2,15,15]{2,0,1:T(2,128)} %param.26) | copy-start | bytes 5404
  114.6 27.6 %copy-start.4 = (f32[2,15]{1,0:T(2,128)S(1)}, f32[2,15]{1,0:T(2,128)}, u32[]{:S(2)}) copy-start(f32[2,15]{1,0:T(2,128)} %layer_charge.1) | copy-start | bytes 364
  114.7 27.6 %copy-start.5 = (f32[2,15]{1,0:T(2,128)S(1)}, f32[2,15]{1,0:T(2,128)}, u32[]{:S(2)}) copy-start(f32[2,15]{1,0:T(2,128)} %layer_bias.1) | copy-start | bytes 364
  114.7 27.6 %copy-start.6 = (f32[2,15]{1,0:T(2,128)S(1)}, f32[2,15]{1,0:T(2,128)}, u32[]{:S(2)}) copy-start(f32[2,15]{1,0:T(2,128)} %layer_out.1) | copy-start | bytes 364

commit v8 on v7

--- a/solution.py
+++ b/solution.py
@@ -21,7 +21,7 @@
 ROWS = REPS * PIECE
 WINDOW = 64
 
-highest = lax.Precision.HIGHEST
+precise = lax.Precision.HIGH
 inv_sqrt_pi = 0.5641895835477563
 float32 = jnp.float32
 VMEM = pl.BlockSpec(memory_space=pltpu.VMEM)
@@ -50,14 +50,14 @@
 
 
 def last_layers(layer_mid, layer_out, hidden_one, kind):
-    hidden_two = jnp.dot(layer_mid[:, kind, :], hidden_one, precision=highest, preferred_element_type=float32)
+    hidden_two = jnp.dot(layer_mid[:, kind, :], hidden_one, precision=precise, preferred_element_type=float32)
     return jnp.sum(as_column(layer_out[kind : kind + 1, :]) * jnp.tanh(hidden_two), axis=0, keepdims=True)
 
 
 def network(layer_in, layer_bias, layer_mid, layer_out, features):
     outs = []
     for kind in range(ELEMS):
-        hidden_one = jnp.dot(layer_in[:, kind, :], features, precision=highest, preferred_element_type=float32)
+        hidden_one = jnp.dot(layer_in[:, kind, :], features, precision=precise, preferred_element_type=float32)
         hidden_one = jnp.tanh(hidden_one + as_column(layer_bias[kind : kind + 1, :]))
         outs.append(last_layers(layer_mid, layer_out, hidden_one, kind))
     return outs
@@ -193,7 +193,7 @@
                     sums[group] + piece[here, group * 8 : group * 8 + 8, :] * values for group in range(GROUPS)
                 )
 
-            sums = lax.fori_loop(0, BLKS, one_line, sums, unroll=16)
+            sums = lax.fori_loop(0, BLKS, one_line, sums, unroll=32)
     half = GROUPS // 2
     return [
         jnp.sum(jnp.concatenate(sums[part * half : part * half + half], axis=0).T, axis=0, keepdims=True)
@@ -288,7 +288,7 @@
 ):
     frame = lax.axis_index("phase")
     inputs = [
-        jnp.dot(layer_in[:, kind, :], features[frame], precision=highest, preferred_element_type=float32)
+        jnp.dot(layer_in[:, kind, :], features[frame], precision=precise, preferred_element_type=float32)
         + as_column(layer_bias[kind : kind + 1, :])
         for kind in range(ELEMS)
     ]

time: 144 us -> 150 us (1.042)
  Pallas kernels: 29.8 us -> 35.7 us
    pallas_call x9, Pallas kernels: 29.8 us -> 35.7 us  [run(): pl.pallas_call(kernel, out_shape=outs, in_specs=[held] * len(args), out_s...]
  transfers between devices with their start and end apart: 3 -> 3, of which waited for: 0 -> 0; matrix products, arithmetic and copies ran while one was open for 0% -> 0% of each run, Pallas kernels for 6% -> 5%
where the time goes in v8:
time: 150 us; the launch traced here: 149 us
  blocking collectives  102 us (68%)
  Pallas kernels  35.7 us (24%)
  starting transfers between devices  10.6 us (7%)
    all_to_all x3, blocking collectives, exchange(): lax.all_to_all(sent, all_axes, 0, 0, axis_index_groups=cube_groups())  47.6 us
    pallas_call x9, Pallas kernels, run(): pl.pallas_call(kernel, out_shape=outs, in_specs=[held] * len(args), out_s...  35.7 us
    all_to_all x1, blocking collectives, on_device(): lax.all_to_all(message, all_axes, 0, 0, axis_index_groups=block_groups())  29.7 us
    all_to_all x1, blocking collectives, on_device(): lax.all_to_all(message.reshape(BLKS, 1, LANES), all_axes, 0, 0, axis_inde...  16 us
    all_to_all x1, blocking collectives, on_device(): lax.all_to_all(share.reshape(16, 1, LANES), all_axes, 0, 0, axis_index_gr...  8.59 us
    ppermute x1, starting transfers between devices, on_device(): part_1 = lax.ppermute(atoms_own, ('core', 'rep'), far)  4.63 us
    ppermute x1, starting transfers between devices, on_device(): part_3 = lax.ppermute(part_1, 'core', [(0, 1), (1, 0)])  3.75 us
  transfers between devices with their start and end apart: 3, of which 0 were waited for; matrix products, arithmetic and copies ran while one was open for 0% of the time, Pallas kernels for 5%

profile of v8, /device:TPU:1, one launch (start us, length us, event | category | flops | bytes accessed | tf_op | source)
XLA Modules:
  0.0 149.2 jit_solution(5832930745141711006)
XLA Ops:
  0.6 1.6 %prepare.1 = (f32[32,3,4,128]{3,2,1,0:T(4,128)S(1)}, f32[8,128]{1,0:T(8,128)S(1)}) custom-call(f32[4,32,256]{2,1,0:T(8,128)} %features.1, f32[3,4,1024]{2,1,0:T(4,128)} %bitcast.33, s32[4,1024]{1,0:T(4,128)} %kinds.1, s32[4,256]{1,0:T(4,128)} %refs_3_.1, f32[15,2,32]{2,1,0:T(2,128)} %bitcast.34, f32[2,15]{1,0:T(2,128)} %refs_5_.1, f32[15,2,15]{2,1,0:T(2,128)} %bitcast.35, ...), custom_call_target="tpu_custom_call" | custom-call | tf_op jit(solution)/shard_map/prepare/pallas_call | solution.py:320
  2.2 29.7 %all_to_all.30.atoms.refs_0_ = f32[32,3,4,128]{3,2,1,0:T(4,128)S(1)} all-to-all(f32[32,3,4,128]{3,2,1,0:T(4,128)S(1)} %get-tuple-element.26), channel_id=1, replica_groups={{322,330,338,346,354,362,370,378,258,266,274,282,290,298,306,314,326,33..., dimensions={0} | all-to-all | bytes 393216 | tf_op jit(solution)/shard_map/all_to_all | solution.py:379
  32.0 4.6 %collective-permute-start = (f32[32,3,4,128]{3,2,1,0:T(4,128)S(1)}, f32[32,3,4,128]{3,2,1,0:T(4,128)S(1)}, u32[]{:S(2)}, u32[]{:S(2)}) collective-permute-start(f32[32,3,4,128]{3,2,1,0:T(4,128)S(1)} %all_to_all.30.atoms.refs_0_), channel_id=1, source_target_pairs={{1,0},{0,1},{3,2},{2,3},{7,4},{6,5},{5,6},{4,7},{9,8},{8,9},{11,10... | collective-permute-start | bytes 589832 | tf_op jit(solution)/shard_map/ppermute | solution.py:381
  36.6 2.3 %collective-permute-start.1 = (f32[32,3,4,128]{3,2,1,0:T(4,128)S(1)}, f32[32,3,4,128]{3,2,1,0:T(4,128)S(1)}, u32[]{:S(2)}, u32[]{:S(2)}) collective-permute-start(f32[32,3,4,128]{3,2,1,0:T(4,128)S(1)} %all_to_all.30.atoms.refs_0_), channel_id=1, source_target_pairs={{2,0},{3,1},{0,2},{1,3},{6,4},{7,5},{4,6},{5,7},{10,8},{11,9},{8,1... | collective-permute-start | bytes 589832 | tf_op jit(solution)/shard_map/ppermute | solution.py:382
  38.9 4.2 %build_own.1 = (f32[64,256,128]{2,1,0:T(8,128)S(1)}, f32[5,256,128]{2,1,0:T(8,128)S(1)}) custom-call(f32[32,3,4,128]{3,2,1,0:T(4,128)S(1)} %all_to_all.30.atoms.refs_0_, f32[8,128]{1,0:T(8,128)S(1)} %get-tuple-element.27.constants), custom_call_target="tpu_custom_call" | custom-call | flops 1000000000 | tf_op jit(solution)/shard_map/build_own/pallas_call | solution.py:320
  43.1 0.0 collective-permute-done.part_1.refs_1_
  43.1 3.7 %collective-permute-start.2 = (f32[32,3,4,128]{3,2,1,0:T(4,128)S(1)}, f32[32,3,4,128]{3,2,1,0:T(4,128)S(1)}, u32[]{:S(2)}, u32[]{:S(2)}) collective-permute-start(f32[32,3,4,128]{3,2,1,0:T(4,128)S(1)} %collective-permute-done.part_1.refs_1_), channel_id=1, source_target_pairs={{0,4},{4,0},{1,5},{5,1},{2,6},{6,2},{3,7},{7,3},{8,12},{12,8},{9,1... | collective-permute-start | bytes 589832 | tf_op jit(solution)/shard_map/ppermute | solution.py:385
  46.8 3.8 %build_next.1.refs_6_.refs_7_.piece_1 = f32[64,256,128]{2,1,0:T(8,128)S(1)} custom-call(f32[32,3,4,128]{3,2,1,0:T(4,128)S(1)} %collective-permute-done.part_1.refs_1_, f32[5,256,128]{2,1,0:T(8,128)S(1)} %get-tuple-element.30.rows.refs_4_), custom_call_target="tpu_custom_call" | custom-call | flops 1000000000 | tf_op jit(solution)/shard_map/build_next/pallas_call | solution.py:320
  50.7 0.0 collective-permute-done.1.refs_2_
  50.7 0.0 collective-permute-done.2.refs_3_
  50.7 12.0 %build_rest_and_begin.1 = (f32[64,256,128]{2,1,0:T(8,128)S(1)}, f32[64,256,128]{2,1,0:T(8,128)S(1)}, f32[256,128]{1,0:T(8,128)S(1)}, f32[256,128]{1,0:T(8,128)S(...) custom-call(f32[32,3,4,128]{3,2,1,0:T(4,128)S(1)} %all_to_all.30.atoms.refs_0_, ...), custom_call_target="tpu_custom_call" | custom-call | tf_op jit(solution)/shard_map/build_rest_and_begin/pallas_call | solution.py:320
  62.7 15.8 %all_to_all.31 = f32[128,2,128]{2,1,0:T(2,128)S(1)} all-to-all(f32[128,2,128]{2,1,0:T(2,128)S(1)} %bitcast.24), channel_id=1, replica_groups={{282,274,266,258,410,402,394,386,26,18,10,2,154,146,138,130,283,275,267..., dimensions={0} | all-to-all | bytes 262144 | tf_op jit(solution)/shard_map/all_to_all | solution.py:359
  78.5 4.5 %iterate.2 = (f32[256,128]{1,0:T(8,128)S(1)}, f32[256,128]{1,0:T(8,128)S(1)}, f32[256,128]{1,0:T(8,128)S(1)}, f32[256,128]{1,0:T(8,128)S(1)}, f32[8,128]{1,0:T(8,128)S(1)}) custom-call(f32[256,128]{1,0:T(8,128)S(1)} %bitcast.23, f32[256,128]{1,0:T(8,128)S(1)} %get-tuple-element.33.refs_1_.refs_2_, f32[256,128]{1,0:T(8,128)S(1)} %get-tuple-element.33.refs_1_.refs_2_, ...), custom_call_target="tpu_custom_call" | custom-call | tf_op jit(solution)/shard_map/iterate/pallas_call | solution.py:320
  83.0 15.9 %all_to_all.32 = f32[128,2,128]{2,1,0:T(2,128)S(1)} all-to-all(f32[128,2,128]{2,1,0:T(2,128)S(1)} %bitcast.26), channel_id=1, replica_groups={{282,274,266,258,410,402,394,386,26,18,10,2,154,146,138,130,283,275,267..., dimensions={0} | all-to-all | bytes 262144 | tf_op jit(solution)/shard_map/all_to_all | solution.py:359
  98.9 4.2 %iterate.3 = (f32[256,128]{1,0:T(8,128)S(1)}, f32[256,128]{1,0:T(8,128)S(1)}, f32[256,128]{1,0:T(8,128)S(1)}, f32[256,128]{1,0:T(8,128)S(1)}, f32[8,128]{1,0:T(8,128)S(1)}) custom-call(f32[256,128]{1,0:T(8,128)S(1)} %bitcast.22, f32[256,128]{1,0:T(8,128)S(1)} %get-tuple-element.39.refs_1_, f32[256,128]{1,0:T(8,128)S(1)} %get-tuple-element.40.refs_2_, ...), custom_call_target="tpu_custom_call" | custom-call | tf_op jit(solution)/shard_map/iterate/pallas_call | solution.py:320
  103.1 15.9 %all_to_all.33 = f32[128,2,128]{2,1,0:T(2,128)S(1)} all-to-all(f32[128,2,128]{2,1,0:T(2,128)S(1)} %bitcast.25), channel_id=1, replica_groups={{282,274,266,258,410,402,394,386,26,18,10,2,154,146,138,130,283,275,267..., dimensions={0} | all-to-all | bytes 262144 | tf_op jit(solution)/shard_map/all_to_all | solution.py:359
  119.0 0.0 copy-start
  119.0 0.0 copy-start.1
  119.0 0.0 copy-start.2
  119.0 0.0 copy-start.3
  119.0 0.0 copy-start.4
  119.1 0.0 copy-start.5
  119.1 0.0 copy-start.6
  119.1 4.5 %last.1 = (f32[16,128]{1,0:T(8,128)S(1)}, f32[32,128]{1,0:T(8,128)S(1)}) custom-call(f32[256,128]{1,0:T(8,128)S(1)} %bitcast.21, f32[256,128]{1,0:T(8,128)S(1)} %get-tuple-element.44.residual, f32[256,128]{1,0:T(8,128)S(1)} %get-tuple-element.45.direction, f32[256,128]{1,0:T(8,128)S(1)} %get-tuple-element.46.charges, ...), custom_call_target="tpu_custom_call" | custom-call | tf_op jit(solution)/shard_map/last/pallas_call | solution.py:320
  123.5 8.6 %all_to_all.34 = f32[16,1,128]{2,1,0:T(1,128)S(1)} all-to-all(f32[16,1,128]{2,1,0:T(1,128)S(1)} %bitcast.32), channel_id=1, replica_groups={{258,259,256,257,386,387,384,385,2,3,0,1,130,131,128,129},{262,263,260,..., dimensions={0} | all-to-all | bytes 16384 | tf_op jit(solution)/shard_map/all_to_all | solution.py:401
  132.1 0.1 join.1
  132.2 16.0 %all_to_all.35 = f32[32,1,128]{2,1,0:T(1,128)S(1)} all-to-all(f32[32,1,128]{2,1,0:T(1,128)S(1)} %bitcast.28), channel_id=1, replica_groups={{322,330,338,346,354,362,370,378,258,266,274,282,290,298,306,314,326,33..., dimensions={0} | all-to-all | bytes 32768 | tf_op jit(solution)/shard_map/all_to_all | solution.py:404
  148.2 0.0 copy-done
  148.2 0.0 copy-done.1
  148.2 0.0 copy-done.2
  148.2 0.0 copy-done.3
  148.2 0.0 copy-done.4
  148.2 0.0 copy-done.5
  148.3 0.0 copy-done.6
  148.3 0.9 finish.1
Async XLA Ops:
  32.0 11.1 %collective-permute-start = (f32[32,3,4,128]{3,2,1,0:T(4,128)S(1)}, f32[32,3,4,128]{3,2,1,0:T(4,128)S(1)}, u32[]{:S(2)}, u32[]{:S(2)}) collective-permute-start(f32[32,3,4,128]{3,2,1,0:T(4,128)S(1)} %all_to_all.30.atoms.refs_0_), channel_id=1, source_target_pairs={{1,0},{0,1},{3,2},{2,3},{7,4},{6,5},{5,6},{4,7},{9,8},{8,9},{11,10... | collective-permute-start | bytes 589832 | tf_op jit(solution)/shard_map/ppermute | solution.py:381
  36.6 14.1 %collective-permute-start.1 = (f32[32,3,4,128]{3,2,1,0:T(4,128)S(1)}, f32[32,3,4,128]{3,2,1,0:T(4,128)S(1)}, u32[]{:S(2)}, u32[]{:S(2)}) collective-permute-start(f32[32,3,4,128]{3,2,1,0:T(4,128)S(1)} %all_to_all.30.atoms.refs_0_), channel_id=1, source_target_pairs={{2,0},{3,1},{0,2},{1,3},{6,4},{7,5},{4,6},{5,7},{10,8},{11,9},{8,1... | collective-permute-start | bytes 589832 | tf_op jit(solution)/shard_map/ppermute | solution.py:382
  43.1 7.6 %collective-permute-start.2 = (f32[32,3,4,128]{3,2,1,0:T(4,128)S(1)}, f32[32,3,4,128]{3,2,1,0:T(4,128)S(1)}, u32[]{:S(2)}, u32[]{:S(2)}) collective-permute-start(f32[32,3,4,128]{3,2,1,0:T(4,128)S(1)} %collective-permute-done.part_1.refs_1_), channel_id=1, source_target_pairs={{0,4},{4,0},{1,5},{5,1},{2,6},{6,2},{3,7},{7,3},{8,12},{12,8},{9,1... | collective-permute-start | bytes 589832 | tf_op jit(solution)/shard_map/ppermute | solution.py:385
  119.0 29.2 %copy-start = (f32[4,32,256]{2,1,0:T(8,128)S(1)}, f32[4,32,256]{2,1,0:T(8,128)}, u32[]{:S(2)}) copy-start(f32[4,32,256]{2,1,0:T(8,128)} %features.1) | copy-start | bytes 393220
  119.0 29.2 %copy-start.1 = (s32[4,1024]{1,0:T(4,128)S(1)}, s32[4,1024]{1,0:T(4,128)}, u32[]{:S(2)}) copy-start(s32[4,1024]{1,0:T(4,128)} %kinds.1) | copy-start | bytes 49156
  119.0 29.2 %copy-start.2 = (f32[2,15,32]{2,0,1:T(2,128)S(1)}, f32[2,15,32]{2,0,1:T(2,128)}, u32[]{:S(2)}) copy-start(f32[2,15,32]{2,0,1:T(2,128)} %param.23) | copy-start | bytes 11524
  119.0 29.2 %copy-start.3 = (f32[2,15,15]{2,0,1:T(2,128)S(1)}, f32[2,15,15]{2,0,1:T(2,128)}, u32[]{:S(2)}) copy-start(f32[2,15,15]{2,0,1:T(2,128)} %param.26) | copy-start | bytes 5404
  119.0 29.2 %copy-start.4 = (f32[2,15]{1,0:T(2,128)S(1)}, f32[2,15]{1,0:T(2,128)}, u32[]{:S(2)}) copy-start(f32[2,15]{1,0:T(2,128)} %layer_charge.1) | copy-start | bytes 364
  119.1 29.2 %copy-start.5 = (f32[2,15]{1,0:T(2,128)S(1)}, f32[2,15]{1,0:T(2,128)}, u32[]{:S(2)}) copy-start(f32[2,15]{1,0:T(2,128)} %layer_bias.1) | copy-start | bytes 364
  119.1 29.2 %copy-start.6 = (f32[2,15]{1,0:T(2,128)S(1)}, f32[2,15]{1,0:T(2,128)}, u32[]{:S(2)}) copy-start(f32[2,15]{1,0:T(2,128)} %layer_out.1) | copy-start | bytes 364
